TPU v7x, 32 devices: a whole 2x2x4 slice. The times are simulated.
32 devices in a mesh: tm: 4 (over y, x), chan: 8 (over z, core).
Axes of the slice: x: 2, y: 2, z: 4, core: 2. Of those that a mesh axis runs over, the one named last changes fastest.
Arguments:
- strain_rate: bfloat16 [20480, 10240], P('tm', 'chan'), may hold values from -120 to 120
- filter_taps: float32 [40], replicated, may hold values from -1 to 1
- send_rows: int32 [32, 4, 8, 32], P(('tm', 'chan')), may hold values from 0 to 319
- pair_source: int32 [32, 2048], P(('tm', 'chan')), may hold values from 0 to 1023, as said below
- pair_receiver: int32 [32, 2048], P(('tm', 'chan')), may hold values from 0 to 319
- pair_count: int32 [32], P(('tm', 'chan')), may hold values from 1024 to 2048, as said below
Outputs:
- correlations: float32 [32, 2048, 256], P(('tm', 'chan'))
Inputs may be any that keep to these rules, and one draw needn't show every extreme that they name: `pair_source`: in each owner's list the first 1024 entries name every slot once; the others are any slots. `pair_count`: every owner has at least 1024 live pairs and some owner has exactly 2048.
All inputs are finite; a program needn't handle non-finite values.
Results may differ from a plain program's by a relative error of at most 0.02.
Values may be sent and summed in bfloat16 or wider, within the bound.
No kernel may reach another device: no remote copies, remote signals or barrier semaphores. Data moves between devices by JAX's collectives and lax.ppermute only.
A program may use at most 192 MiB of HBM per device.

v0:
```python
import math

import jax
import jax.numpy as jnp
import numpy as np
from jax import lax
from jax.experimental import pallas as pl
from jax.experimental.pallas import tpu as pltpu
from jax.sharding import PartitionSpec as P

Q = 5
TAPS = 40
RIM = TAPS // 2
SEG = 1024
NF = 256
WF = 32
F0 = 40
TW = 32
WT = 64
LAGS = 256
BINS = NF + 2 * WF
TB = 128
EDGE = 32
BAND = 704
FIRST = 672
BF = jnp.bfloat16
F32 = jnp.float32
VMEM = 56 * 1024 * 1024


def forward_table():
    phases = np.arange(F0 - WF, F0 + NF + WF)[:, None] * np.arange(SEG)[None, :] % SEG
    phases = phases * (2.0 * np.pi / SEG)
    return np.concatenate([np.cos(phases), -np.sin(phases)], axis=0).astype(BF)


def lag_table():
    phases = (F0 + np.arange(NF))[:, None] * (np.arange(LAGS) - LAGS // 2)[None, :] % SEG
    phases = phases * (2.0 * np.pi / SEG)
    return np.concatenate([np.cos(phases), -np.sin(phases)], axis=0).astype(BF)


def taper():
    bins = np.arange(NF)
    edge = np.minimum(bins, NF - 1 - bins)
    return np.where(edge < TW, 0.5 - 0.5 * np.cos(np.pi * (edge + 0.5) / TW), 1.0).astype(np.float32)


def ones_band(rows, columns, width):
    lag = np.arange(columns)[None, :] - np.arange(rows)[:, None]
    return ((lag >= 0) & (lag < width)).astype(BF)


def whole(shape):
    return pl.BlockSpec(shape, lambda *_: (0,) * len(shape))


def params():
    return pltpu.CompilerParams(vmem_limit_bytes=VMEM)


def band_kernel(taps_ref, main_ref, first_ref, last_ref):
    def fill(ref, start):
        width = ref.shape[1]
        tap = (
            lax.broadcasted_iota(jnp.int32, (TB, width), 1)
            + (start + RIM)
            - Q * lax.broadcasted_iota(jnp.int32, (TB, width), 0)
        )
        values = jnp.zeros((TB, width), F32)
        for k in range(TAPS):
            values = jnp.where(tap == k, taps_ref[k], values)
        upper = values.astype(BF)
        ref[:TB] = upper
        ref[TB:] = (values - upper.astype(F32)).astype(BF)

    fill(main_ref, -EDGE)
    fill(first_ref, 0)
    fill(last_ref, Q * TB)


def filter_bands(taps):
    widths = (BAND, FIRST, EDGE)
    return pl.pallas_call(
        band_kernel,
        in_specs=[pl.BlockSpec(memory_space=pltpu.SMEM)],
        out_shape=[jax.ShapeDtypeStruct((2 * TB, width), BF) for width in widths],
        compiler_params=params(),
    )(taps)


def decimate_kernel(x_ref, rim_ref, main_ref, first_ref, last_ref, out_ref):
    blocks = out_ref.shape[0] // TB
    for b in range(blocks):
        start = Q * TB * b
        if b == 0:
            total = jnp.dot(first_ref[...], x_ref[:FIRST], preferred_element_type=F32)
            total += jnp.dot(main_ref[:, :EDGE], rim_ref[:EDGE], preferred_element_type=F32)
        elif b < blocks - 1:
            total = jnp.dot(
                main_ref[...], x_ref[start - EDGE : start - EDGE + BAND], preferred_element_type=F32
            )
        else:
            width = EDGE + Q * TB
            total = jnp.dot(
                main_ref[:, :width], x_ref[start - EDGE :], preferred_element_type=F32
            )
            total += jnp.dot(last_ref[...], rim_ref[EDGE:], preferred_element_type=F32)
        out_ref[TB * b : TB * (b + 1)] = (total[:TB] + total[TB:]).astype(BF)


def lane_chunk(width):
    return 256 if width % 256 == 0 else 128


def decimate(x, rim, bands):
    rows, width = x.shape
    chunk = lane_chunk(width)
    return pl.pallas_call(
        decimate_kernel,
        grid=(width // chunk,),
        in_specs=[
            pl.BlockSpec((rows, chunk), lambda c: (0, c)),
            pl.BlockSpec((2 * EDGE, chunk), lambda c: (0, c)),
        ]
        + [whole(band.shape) for band in bands],
        out_specs=pl.BlockSpec((rows // Q, chunk), lambda c: (0, c)),
        out_shape=jax.ShapeDtypeStruct((rows // Q, width), BF),
        compiler_params=params(),
    )(x, rim, *bands)


def whiten_kernel(
    place_ref, dec_ref, before_ref, after_ref, ones_ref, table_ref, smooth_ref, taper_ref, out_ref, size, flat
):
    length = dec_ref.shape[0]
    blocks = length // TB
    size[:WT] = jnp.abs(before_ref[...])
    size[WT : WT + length] = jnp.abs(dec_ref[...])
    size[WT + length :] = jnp.abs(after_ref[...])
    origin = place_ref[0] * length
    total = place_ref[1] * length
    for b in range(blocks):
        window = jnp.dot(ones_ref[...], size[TB * b : TB * b + TB + 2 * WT], preferred_element_type=F32)
        if b == 0 or b == blocks - 1:
            place = origin + TB * b + lax.broadcasted_iota(jnp.int32, (TB, 1), 0)
            count = jnp.minimum(place + WT, total - 1) - jnp.maximum(place - WT, 0) + 1
            mean = window / count.astype(F32)
        else:
            mean = window * (1.0 / (2 * WT + 1))
        values = dec_ref[TB * b : TB * (b + 1)].astype(F32) / (mean + 1e-05)
        flat[TB * b : TB * (b + 1)] = values.astype(BF)
    spectrum = jnp.dot(table_ref[...], flat[...], preferred_element_type=F32)
    real, imag = spectrum[:BINS], spectrum[BINS:]
    magnitude = jnp.sqrt(real * real + imag * imag)
    upper = magnitude.astype(BF)
    lower = (magnitude - upper.astype(F32)).astype(BF)
    smooth = jnp.dot(smooth_ref[...], upper, preferred_element_type=F32)
    smooth += jnp.dot(smooth_ref[...], lower, preferred_element_type=F32)
    factor = taper_ref[...] / (smooth * (1.0 / (2 * WF + 1)) + 1e-05)
    out_ref[:, :NF] = (real[WF : WF + NF] * factor).T.astype(BF)
    out_ref[:, NF:] = (imag[WF : WF + NF] * factor).T.astype(BF)


def whiten(place, dec, before, after):
    length, width = dec.shape
    chunk = lane_chunk(width)
    tables = (
        ones_band(TB, TB + 2 * WT, 2 * WT + 1),
        forward_table(),
        ones_band(NF, BINS, 2 * WF + 1),
        taper()[:, None],
    )
    column = lambda c: (0, c)
    return pl.pallas_call(
        whiten_kernel,
        grid=(width // chunk,),
        in_specs=[
            pl.BlockSpec(memory_space=pltpu.SMEM),
            pl.BlockSpec((length, chunk), column),
            pl.BlockSpec((WT, chunk), column),
            pl.BlockSpec((WT, chunk), column),
        ]
        + [whole(table.shape) for table in tables],
        out_specs=pl.BlockSpec((chunk, 2 * NF), lambda c: (c, 0)),
        out_shape=jax.ShapeDtypeStruct((width, 2 * NF), BF),
        scratch_shapes=[pltpu.VMEM((length + 2 * WT, chunk), BF), pltpu.VMEM((length, chunk), BF)],
        compiler_params=params(),
    )(place, dec, before, after, *tables)


def one_hot(ids, columns):
    hits = ids == lax.broadcasted_iota(jnp.int32, (ids.shape[0], columns), 1)
    return jnp.where(hits, 1.0, 0.0).astype(BF)


def pick_kernel(ids_ref, rows_ref, out_ref):
    owners, rows, width = out_ref.shape
    picked = jnp.dot(one_hot(ids_ref[...], rows_ref.shape[0]), rows_ref[...], preferred_element_type=F32)
    out_ref[...] = picked.astype(BF).reshape(owners, rows, width)


def pick(ids, spectra, owners, groups, capacity):
    join = 1
    while join * capacity % 16 != 0:
        join *= 2
    steps = groups // join
    held = spectra.shape[0] // steps
    local = ids.reshape(steps, join, owners, capacity).transpose(0, 2, 1, 3)
    local = local + (jnp.arange(join, dtype=jnp.int32) * (held // join))[None, None, :, None]
    rows = owners * join * capacity
    return pl.pallas_call(
        pick_kernel,
        grid=(steps,),
        in_specs=[
            pl.BlockSpec((rows, 1), lambda g: (g, 0)),
            pl.BlockSpec((held, 2 * NF), lambda g: (g, 0)),
        ],
        out_specs=pl.BlockSpec((owners, join * capacity, 2 * NF), lambda g: (0, g, 0)),
        out_shape=jax.ShapeDtypeStruct((owners, groups * capacity, 2 * NF), BF),
        compiler_params=params(),
    )(local.reshape(steps * rows, 1), spectra)


def correlate_kernel(count_ref, ids_ref, source_ref, receiver_ref, table_ref, out_ref):
    pairs = out_ref.shape[0]
    segments = source_ref.shape[0]
    pick_source = one_hot(ids_ref[:, :1], source_ref.shape[1])
    pick_receiver = one_hot(ids_ref[:, 1:], receiver_ref.shape[1])
    real = imag = None
    for s in range(segments):
        a = jnp.dot(pick_source, source_ref[s], preferred_element_type=F32)
        b = jnp.dot(pick_receiver, receiver_ref[s], preferred_element_type=F32)
        a_re, a_im, b_re, b_im = a[:, :NF], a[:, NF:], b[:, :NF], b[:, NF:]
        re = a_re * b_re + a_im * b_im
        im = a_im * b_re - a_re * b_im
        real = re if s == 0 else real + re
        imag = im if s == 0 else imag + im
    values = jnp.dot(real.astype(BF), table_ref[:NF], preferred_element_type=F32)
    values += jnp.dot(imag.astype(BF), table_ref[NF:], preferred_element_type=F32)
    place = pl.program_id(0) * pairs + lax.broadcasted_iota(jnp.int32, values.shape, 0)
    scale = 1.0 / math.sqrt(segments * NF)
    out_ref[...] = jnp.where(place < count_ref[0], values * scale, 0.0)


def correlate(count, ids, source, receiver):
    pairs = ids.shape[0]
    block = 256
    return pl.pallas_call(
        correlate_kernel,
        grid=(pairs // block,),
        in_specs=[
            pl.BlockSpec(memory_space=pltpu.SMEM),
            pl.BlockSpec((block, 2), lambda p: (p, 0)),
            whole(source.shape),
            whole(receiver.shape),
            whole((2 * NF, LAGS)),
        ],
        out_specs=pl.BlockSpec((block, LAGS), lambda p: (p, 0)),
        out_shape=jax.ShapeDtypeStruct((pairs, LAGS), F32),
        compiler_params=params(),
    )(count, ids, source, receiver, lag_table())


def from_neighbours(low, high):
    count = lax.axis_size("tm")
    before = lax.ppermute(high, "tm", [(i, i + 1) for i in range(count - 1)])
    after = lax.ppermute(low, "tm", [(i + 1, i) for i in range(count - 1)])
    return before, after


def on_device(strain, taps, send_rows, pair_source, pair_receiver, pair_count):
    n_tm, n_chan = lax.axis_size("tm"), lax.axis_size("chan")
    owners = n_tm * n_chan
    capacity = send_rows.shape[3]
    before, after = from_neighbours(strain[:EDGE], strain[-EDGE:])
    bands = filter_bands(taps)
    asked = lax.all_gather(send_rows[0], "tm")
    dec = decimate(strain, jnp.concatenate([before, after]), bands)
    before, after = from_neighbours(dec[:WT], dec[-WT:])
    place = jnp.stack([lax.axis_index("tm"), jnp.int32(n_tm)]).astype(jnp.int32)
    spectra = whiten(place, dec, before, after)
    outgoing = pick(asked.reshape(-1), spectra, owners, n_tm, capacity)
    source = lax.all_to_all(outgoing, ("tm", "chan"), 0, 0, tiled=True)
    source = source.reshape(n_tm, -1, 2 * NF)
    receiver = lax.all_to_all(spectra.reshape(n_tm, -1, 2 * NF), "tm", 0, 0, tiled=True)
    sender, column = pair_source[0] // capacity, pair_source[0] % capacity
    slot = (sender % n_chan * n_tm + sender // n_chan) * capacity + column
    ids = jnp.stack([slot, pair_receiver[0]], axis=1)
    return correlate(pair_count, ids, source, receiver)[None]


def solution(mesh):
    return jax.shard_map(
        on_device,
        mesh=mesh,
        in_specs=(
            P("tm", "chan"),
            P(),
            P(("tm", "chan"), None, None, None),
            P(("tm", "chan"), None),
            P(("tm", "chan"), None),
            P(("tm", "chan")),
        ),
        out_specs=P(("tm", "chan"), None, None),
        check_vma=False,
    )
```

profile of v0, /device:TPU:0, one launch (start us, length us, event | category | flops | bytes accessed | tf_op | source)
XLA Modules:
  0.0 201.2 jit_solution(2024193402431581467)
XLA Ops:
  0.0 0.9 fusion.3
  0.9 4.8 %collective-permute-start = (bf16[32,1280]{1,0:T(8,128)(2,1)S(1)}, bf16[32,1280]{1,0:T(8,128)(2,1)S(1)}, u32[]{:S(2)}, u32[]{:S(2)}) collective-permute-start(bf16[32,1280]{1,0:T(8,128)(2,1)S(1)} %get-tuple-element.11), channel_id=1, source_target_pairs={{0,8},{8,16},{16,24},{1,9},{9,17},{17,25},{2,10},{10,18},{18,26},{... | collective-permute-start | bytes 245768 | tf_op jit(solution)/shard_map/ppermute | solution.py:267
  5.8 1.3 collective-permute-start.1
  7.1 3.8 %shard_map.109 = (bf16[256,704]{1,0:T(8,128)(2,1)}, bf16[256,672]{1,0:T(8,128)(2,1)}, bf16[256,32]{1,0:T(8,128)(2,1)}) custom-call(f32[40]{0:T(128)} %taps_ref.1), custom_call_target="tpu_custom_call" | custom-call | tf_op jit(solution)/shard_map/pallas_call | solution.py:84
  10.8 0.0 collective-permute-done
  10.9 1.3 collective-permute-done.1
  12.1 0.7 pad_maximum_fusion.rim_ref
  12.8 9.8 %shard_map.110.dec_ref = bf16[1024,1280]{1,0:T(8,128)(2,1)} custom-call(bf16[5120,1280]{1,0:T(8,128)(2,1)} %x_ref.1, bf16[64,1280]{1,0:T(8,128)(2,1)} %pad_maximum_fusion.rim_ref, bf16[256,704]{1,0:T(8,128)(2,1)} %get-tuple-element.8.main_ref, bf16[256,672]{1,0:T(8,128)(2,1)} %get-tuple-element.9.first_ref, bf16[256,32]{1,0:T(8,128)(2,1)} %get-tuple-element.10.last_ref), custom_call_target="tpu_custom_call" | custom-call | tf_op jit(solution)/shard_map/pallas_call | solution.py:119
  22.6 1.0 fusion.4
  23.7 4.3 %collective-permute-start.2 = (bf16[64,1280]{1,0:T(8,128)(2,1)S(1)}, bf16[64,1280]{1,0:T(8,128)(2,1)S(1)}, u32[]{:S(2)}, u32[]{:S(2)}) collective-permute-start(bf16[64,1280]{1,0:T(8,128)(2,1)S(1)} %get-tuple-element.14), channel_id=1, source_target_pairs={{0,8},{8,16},{16,24},{1,9},{9,17},{17,25},{2,10},{10,18},{18,26},{... | collective-permute-start | bytes 491528 | tf_op jit(solution)/shard_map/ppermute | solution.py:267
  28.0 1.3 collective-permute-start.3
  29.3 0.7 pad_add_fusion.1.place_ref
  29.9 0.8 collective-permute-done.2.before_ref
  30.8 5.4 %collective-permute-done.3.after_ref = bf16[64,1280]{1,0:T(8,128)(2,1)S(1)} collective-permute-done((bf16[64,1280]{1,0:T(8,128)(2,1)S(1)}, bf16[64,1280]{1,0:T(8,128)(2,1)S(1)}, u32[]{:S(2)}, u32[]{:S(2)}) %collective-permute-start.3) | collective-permute-done | bytes 163872 | tf_op jit(solution)/shard_map/ppermute | solution.py:268
  36.2 0.0 copy-done.1
  36.2 0.7 copy-done.2
  36.8 9.8 %shard_map.111.rows_ref = bf16[1280,512]{1,0:T(8,128)(2,1)} custom-call(s32[2]{0:T(128)} %pad_add_fusion.1.place_ref, bf16[1024,1280]{1,0:T(8,128)(2,1)} %shard_map.110.dec_ref, bf16[64,1280]{1,0:T(8,128)(2,1)} %copy-done.1, bf16[64,1280]{1,0:T(8,128)(2,1)} %copy-done.2, bf16[128,256]{1,0:T(8,128)(2,1)} %constant.68.clone.ones_ref, ...), custom_call_target="tpu_custom_call" | custom-call | tf_op jit(solution)/shard_map/pallas_call | solution.py:175
  46.6 3.7 %all-to-all-start.1 = ((bf16[4,320,512]{2,1,0:T(8,128)(2,1)}), bf16[4,320,512]{2,1,0:T(8,128)(2,1)S(1)}, u32[]{:S(2)}, u32[]{:S(2)}) async-start(bf16[4,320,512]{2,1,0:T(8,128)(2,1)} %bitcast.20), calls=%async_computation.1 | async-start | bytes 2621440 | tf_op jit(solution)/shard_map/all_to_all | solution.py:286
  50.3 0.0 copy-done.3
  50.3 18.9 %all_gather.3 = s32[4,4,8,32]{3,2,1,0:T(8,128)S(1)} all-gather(s32[1,4,8,32]{3,2,1,0:T(8,128)S(1)} %copy-done.3), channel_id=1, replica_groups=mesh['tm'=4,'chan'=8] {'tm'}, dimensions={0}, use_global_device_ids=true | all-gather | bytes 20480 | tf_op jit(solution)/shard_map/all_gather | solution.py:278
  69.3 3.5 %reshape_transpose_reshape_reshape.4.ids_ref = s32[4096,1]{1,0:T(8,128)} reshape(s32[4,4,8,32]{3,2,1,0:T(8,128)S(1)} %all_gather.3) | data formatting | bytes 32768 | tf_op jit(solution)/shard_map/reshape;transpose;reshape;reshape | solution.py:222
  72.8 6.1 %shard_map.112 = bf16[32,128,512]{2,1,0:T(8,128)(2,1)} custom-call(s32[4096,1]{1,0:T(8,128)} %reshape_transpose_reshape_reshape.4.ids_ref, bf16[1280,512]{1,0:T(8,128)(2,1)} %shard_map.111.rows_ref), custom_call_target="tpu_custom_call" | custom-call | tf_op jit(solution)/shard_map/pallas_call | solution.py:212
  78.8 0.0 all-to-all-done.1.receiver_ref
  78.8 0.0 copy-start
  78.8 1.1 copy-done
  80.0 5.0 %all-to-all-start = ((bf16[32,128,512]{2,1,0:T(8,128)(2,1)}), bf16[32,128,512]{2,1,0:T(8,128)(2,1)}, u32[]{:S(2)}, u32[]{:S(2)}) async-start(bf16[32,128,512]{2,1,0:T(8,128)(2,1)} %shard_map.112), calls=%async_computation | async-start | bytes 8388608 | tf_op jit(solution)/shard_map/all_to_all | solution.py:284
  84.9 0.0 copy-done.4
  85.0 0.1 fusion
  85.1 0.0 copy-done.5
  85.1 1.4 copy.19.ids_ref
  87.2 92.9 %all-to-all-done = bf16[32,128,512]{2,1,0:T(8,128)(2,1)} async-done(((bf16[32,128,512]{2,1,0:T(8,128)(2,1)}), bf16[32,128,512]{2,1,0:T(8,128)(2,1)}, u32[]{:S(2)}, u32[]{:S(2)}) %all-to-all-start) | async-done | bytes 4194336 | tf_op jit(solution)/shard_map/all_to_all | solution.py:284
  180.0 21.2 %shard_map.113 = f32[2048,256]{1,0:T(8,128)} custom-call(s32[1]{0:T(128)S(6)} %copy.20.count_ref, s32[2048,2]{1,0:T(8,128)} %copy.19.ids_ref, bf16[4,1024,512]{2,1,0:T(8,128)(2,1)} %bitcast.3.source_ref, bf16[4,320,512]{2,1,0:T(8,128)(2,1)} %copy-done, bf16[512,256]{1,0:T(8,128)(2,1)} %constant.72.clone.table_ref), custom_call_target="tpu_custom_call" | custom-call | tf_op jit(solution)/shard_map/pallas_call | solution.py:249
  (6 shorter events, 0.0 us)
Async XLA Ops:
  0.9 9.9 %collective-permute-start = (bf16[32,1280]{1,0:T(8,128)(2,1)S(1)}, bf16[32,1280]{1,0:T(8,128)(2,1)S(1)}, u32[]{:S(2)}, u32[]{:S(2)}) collective-permute-start(bf16[32,1280]{1,0:T(8,128)(2,1)S(1)} %get-tuple-element.11), channel_id=1, source_target_pairs={{0,8},{8,16},{16,24},{1,9},{9,17},{17,25},{2,10},{10,18},{18,26},{... | collective-permute-start | bytes 245768 | tf_op jit(solution)/shard_map/ppermute | solution.py:267
  5.8 6.3 %collective-permute-start.1 = (bf16[32,1280]{1,0:T(8,128)(2,1)S(1)}, bf16[32,1280]{1,0:T(8,128)(2,1)S(1)}, u32[]{:S(2)}, u32[]{:S(2)}) collective-permute-start(bf16[32,1280]{1,0:T(8,128)(2,1)S(1)} %get-tuple-element.12), channel_id=1, source_target_pairs={{8,0},{16,8},{24,16},{9,1},{17,9},{25,17},{10,2},{18,10},{26,18},{... | collective-permute-start | bytes 245768 | tf_op jit(solution)/shard_map/ppermute | solution.py:268
  23.7 7.1 %collective-permute-start.2 = (bf16[64,1280]{1,0:T(8,128)(2,1)S(1)}, bf16[64,1280]{1,0:T(8,128)(2,1)S(1)}, u32[]{:S(2)}, u32[]{:S(2)}) collective-permute-start(bf16[64,1280]{1,0:T(8,128)(2,1)S(1)} %get-tuple-element.14), channel_id=1, source_target_pairs={{0,8},{8,16},{16,24},{1,9},{9,17},{17,25},{2,10},{10,18},{18,26},{... | collective-permute-start | bytes 491528 | tf_op jit(solution)/shard_map/ppermute | solution.py:267
  28.0 8.2 %collective-permute-start.3 = (bf16[64,1280]{1,0:T(8,128)(2,1)S(1)}, bf16[64,1280]{1,0:T(8,128)(2,1)S(1)}, u32[]{:S(2)}, u32[]{:S(2)}) collective-permute-start(bf16[64,1280]{1,0:T(8,128)(2,1)S(1)} %get-tuple-element.13), channel_id=1, source_target_pairs={{8,0},{16,8},{24,16},{9,1},{17,9},{25,17},{10,2},{18,10},{26,18},{... | collective-permute-start | bytes 491528 | tf_op jit(solution)/shard_map/ppermute | solution.py:268
  30.8 5.4 %copy-start.1 = (bf16[64,1280]{1,0:T(8,128)(2,1)}, bf16[64,1280]{1,0:T(8,128)(2,1)S(1)}, u32[]{:S(2)}) copy-start(bf16[64,1280]{1,0:T(8,128)(2,1)S(1)} %collective-permute-done.2.before_ref) | copy-start | bytes 491524
  36.2 0.7 copy-start.2
  46.6 3.7 %copy-start.3 = (s32[1,4,8,32]{3,2,1,0:T(8,128)S(1)}, s32[1,4,8,32]{3,2,1,0:T(8,128)}, u32[]{:S(2)}) copy-start(s32[1,4,8,32]{3,2,1,0:T(8,128)} %param.13) | copy-start | bytes 12292
  46.6 32.2 %all-to-all-start.1 = ((bf16[4,320,512]{2,1,0:T(8,128)(2,1)}), bf16[4,320,512]{2,1,0:T(8,128)(2,1)S(1)}, u32[]{:S(2)}, u32[]{:S(2)}) async-start(bf16[4,320,512]{2,1,0:T(8,128)(2,1)} %bitcast.20), calls=%async_computation.1 | async-start | bytes 2621440 | tf_op jit(solution)/shard_map/all_to_all | solution.py:286
  78.8 6.1 %copy-start.4 = (s32[1,2048]{1,0:T(1,128)S(1)}, s32[1,2048]{1,0:T(1,128)}, u32[]{:S(2)}) copy-start(s32[1,2048]{1,0:T(1,128)} %param.14) | copy-start | bytes 24580
  78.8 6.3 %copy-start.5 = (s32[1,2048]{1,0:T(1,128)S(1)}, s32[1,2048]{1,0:T(1,128)}, u32[]{:S(2)}) copy-start(s32[1,2048]{1,0:T(1,128)} %param.15) | copy-start | bytes 24580
  78.8 1.1 copy-start
  80.0 100.1 %all-to-all-start = ((bf16[32,128,512]{2,1,0:T(8,128)(2,1)}), bf16[32,128,512]{2,1,0:T(8,128)(2,1)}, u32[]{:S(2)}, u32[]{:S(2)}) async-start(bf16[32,128,512]{2,1,0:T(8,128)(2,1)} %shard_map.112), calls=%async_computation | async-start | bytes 8388608 | tf_op jit(solution)/shard_map/all_to_all | solution.py:284
where the time goes:
time: 202 us; the launch traced here: 201 us
  waiting for transfers between devices  100 us (50%)
  Pallas kernels  50.6 us (25%)
  starting transfers between devices  20.4 us (10%)
  blocking collectives  18.9 us (9%)
  local copies, waits for them, and re-layouts  8.62 us (4%)
    all_to_all x1, waiting for transfers between devices, on_device(): source = lax.all_to_all(outgoing, ('tm', 'chan'), 0, 0, tiled=True)  92.9 us
    pallas_call x1, Pallas kernels, correlate(): pl.pallas_call(correlate_kernel, grid=(pairs // block,), in_specs=[pl.Blo...  21.2 us
    all_gather x1, blocking collectives, on_device(): asked = lax.all_gather(send_rows[0], 'tm')  18.9 us
    pallas_call x1, Pallas kernels, decimate(): pl.pallas_call(decimate_kernel, grid=(width // chunk,), in_specs=[pl.Bloc...  9.84 us
    pallas_call x1, Pallas kernels, whiten(): pl.pallas_call(whiten_kernel, grid=(width // chunk,), in_specs=[pl.BlockS...  9.78 us
    ppermute x2, starting transfers between devices, from_neighbours(): before = lax.ppermute(high, 'tm', [(i, i + 1) for i in range(count - 1)])  9.15 us
    ppermute x2, waiting for transfers between devices, from_neighbours(): after = lax.ppermute(low, 'tm', [(i + 1, i) for i in range(count - 1)])  6.67 us
    pallas_call x1, Pallas kernels, pick(): pl.pallas_call(pick_kernel, grid=(steps,), in_specs=[pl.BlockSpec((rows,...  6.06 us
  transfers between devices with their start and end apart: 6, of which 4 were waited for; matrix products, arithmetic and copies ran while one was open for 3% of the time, Pallas kernels for 5%

commit v1 on v0

v1 whole, which is shorter than its diff:
```python
import functools
import math

import jax
import jax.numpy as jnp
import numpy as np
from jax import lax
from jax.experimental import pallas as pl
from jax.experimental.pallas import tpu as pltpu
from jax.sharding import Mesh
from jax.sharding import PartitionSpec as P

Q = 5
TAPS = 40
RIM = TAPS // 2
SEG = 1024
NF = 256
WF = 32
F0 = 40
TW = 32
WT = 64
LAGS = 256
BINS = NF + 2 * WF
TB = 128
RAW = 64
LEAD = 32
BAND = 704
NH = NF // 2
BF = jnp.bfloat16
F32 = jnp.float32
VMEM = 56 * 1024 * 1024


def forward_table():
    phases = np.arange(F0 - WF, F0 + NF + WF)[:, None] * np.arange(SEG)[None, :] % SEG
    phases = phases * (2.0 * np.pi / SEG)
    return np.concatenate([np.cos(phases), -np.sin(phases)], axis=0).astype(BF)


def lag_table():
    phases = (F0 + np.arange(NF))[:, None] * (np.arange(LAGS) - LAGS // 2)[None, :] % SEG
    phases = phases * (2.0 * np.pi / SEG)
    return np.concatenate([np.cos(phases), -np.sin(phases)], axis=0).astype(BF)


def taper():
    bins = np.arange(NF)
    edge = np.minimum(bins, NF - 1 - bins)
    return np.where(edge < TW, 0.5 - 0.5 * np.cos(np.pi * (edge + 0.5) / TW), 1.0).astype(np.float32)


def ones_band(rows, columns, width):
    lag = np.arange(columns)[None, :] - np.arange(rows)[:, None]
    return ((lag >= 0) & (lag < width)).astype(BF)


def whole(shape):
    return pl.BlockSpec(shape, lambda *_: (0,) * len(shape))


def params():
    return pltpu.CompilerParams(vmem_limit_bytes=VMEM)


def fill_band(band_ref, taps_ref, work_ref, rows, shift):
    lanes = work_ref.shape[1]
    tap = lax.broadcasted_iota(jnp.int32, (8, 128), 1) - Q * lax.broadcasted_iota(jnp.int32, (8, 128), 0)
    pattern = jnp.zeros((8, 128), F32)
    for k in range(TAPS):
        pattern = jnp.where(tap == k, taps_ref[k], pattern)
    pattern = jnp.concatenate([pattern, jnp.zeros((8, lanes - 128), F32)], axis=1)
    for m in range(0, rows, 8):
        work_ref[m : m + 8] = pltpu.roll(pattern, (Q * m + shift) % lanes, 1)
    values = work_ref[:rows, : band_ref.shape[1]]
    upper = values.astype(BF)
    band_ref[:rows] = upper
    band_ref[rows:] = (values - upper.astype(F32)).astype(BF)


def filtered(band, x):
    both = jnp.dot(band, x, preferred_element_type=F32)
    rows = both.shape[0] // 2
    return (both[:rows] + both[rows:]).astype(BF)


EDGE_ROWS = 512
EDGE_READ = 352


def edge_kernel(taps_ref, first_ref, last_ref, low_ref, high_ref, fix_ref, low_band, high_band, work):
    fill_band(low_band, taps_ref, work, WT, -RIM)
    fill_band(high_band, taps_ref, work, WT, EDGE_READ - Q * WT - RIM)
    fill_band(fix_ref, taps_ref, work, 16, RAW - Q * 8 - RIM)
    low_ref[:RAW] = first_ref[:RAW]
    low_ref[RAW:] = filtered(low_band[...], first_ref[:EDGE_READ])
    high_ref[:RAW] = last_ref[EDGE_ROWS - RAW :]
    high_ref[RAW:] = filtered(high_band[...], last_ref[EDGE_ROWS - EDGE_READ :])


def edges(x, taps):
    rows, width = x.shape
    last = rows // EDGE_ROWS - 1
    return pl.pallas_call(
        edge_kernel,
        grid=(1,),
        in_specs=[
            pl.BlockSpec(memory_space=pltpu.SMEM),
            pl.BlockSpec((EDGE_ROWS, width), lambda c: (0, 0)),
            pl.BlockSpec((EDGE_ROWS, width), lambda c: (last, 0)),
        ],
        out_specs=[whole((RAW + WT, width)), whole((RAW + WT, width)), whole((32, 2 * RAW))],
        out_shape=[
            jax.ShapeDtypeStruct((RAW + WT, width), BF),
            jax.ShapeDtypeStruct((RAW + WT, width), BF),
            jax.ShapeDtypeStruct((32, 2 * RAW), BF),
        ],
        scratch_shapes=[
            pltpu.VMEM((2 * WT, EDGE_READ), BF),
            pltpu.VMEM((2 * WT, EDGE_READ), BF),
            pltpu.VMEM((WT, 512), F32),
        ],
        compiler_params=params(),
    )(taps, x, x)


def decimate_kernel(taps_ref, x_ref, out_ref, main, first, work):
    @pl.when(pl.program_id(0) == 0)
    def _():
        fill_band(main, taps_ref, work, TB, LEAD - RIM)
        fill_band(first, taps_ref, work, TB, -RIM)

    blocks = out_ref.shape[0] // TB
    for b in range(blocks):
        if b == 0:
            band, rows = first[...], x_ref[: BAND - LEAD]
        elif b < blocks - 1:
            band, rows = main[...], x_ref[Q * TB * b - LEAD : Q * TB * b - LEAD + BAND]
        else:
            band, rows = main[:, : LEAD + Q * TB], x_ref[Q * TB * b - LEAD :]
        out_ref[TB * b : TB * (b + 1)] = filtered(band, rows)


def lane_chunk(width):
    return next(chunk for chunk in (256, 640, 128) if width % chunk == 0)


def decimate(x, taps):
    rows, width = x.shape
    chunk = lane_chunk(width)
    return pl.pallas_call(
        decimate_kernel,
        grid=(width // chunk,),
        in_specs=[
            pl.BlockSpec(memory_space=pltpu.SMEM),
            pl.BlockSpec((rows, chunk), lambda c: (0, c)),
        ],
        out_specs=pl.BlockSpec((rows // Q, chunk), lambda c: (0, c)),
        out_shape=jax.ShapeDtypeStruct((rows // Q, width), BF),
        scratch_shapes=[
            pltpu.VMEM((2 * TB, BAND), BF),
            pltpu.VMEM((2 * TB, BAND - LEAD), BF),
            pltpu.VMEM((TB, 768), F32),
        ],
        compiler_params=params(),
    )(taps, x)


def inverse(values):
    guess = pl.reciprocal(values, approx=True)
    return guess * (2.0 - values * guess)


def whiten_kernel(
    place_ref, dec_ref, first_ref, last_ref, before_ref, after_ref, fix_ref, ones_ref, table_ref, smooth_ref,
    taper_ref, low_ref, high_ref, size, flat
):
    length = dec_ref.shape[0]
    blocks = length // TB
    place, count = place_ref[0], place_ref[1]
    low = filtered(fix_ref[...], jnp.concatenate([before_ref[:RAW], first_ref[...]])).astype(F32)
    high = filtered(fix_ref[...], jnp.concatenate([last_ref[...], after_ref[:RAW]])).astype(F32)
    before = jnp.concatenate([before_ref[RAW:].astype(F32)[:-8], low[:8]])
    after = jnp.concatenate([high[8:], after_ref[RAW:].astype(F32)[8:]])
    size[:WT] = jnp.abs(jnp.where(place > 0, before, 0.0)).astype(BF)
    size[WT + length :] = jnp.abs(jnp.where(place < count - 1, after, 0.0)).astype(BF)
    flat[...] = dec_ref[...]
    flat[:TB] = jnp.concatenate([low[8:], dec_ref[:TB].astype(F32)[8:]]).astype(BF)
    flat[length - TB :] = jnp.concatenate([dec_ref[length - TB :].astype(F32)[:-8], high[:8]]).astype(BF)
    size[WT : WT + length] = jnp.abs(flat[...])
    for b in range(blocks):
        mean = jnp.dot(ones_ref[...], size[TB * b : TB * b + TB + 2 * WT], preferred_element_type=F32)
        if b == 0 or b == blocks - 1:
            sample = place * length + TB * b + lax.broadcasted_iota(jnp.int32, (TB, 1), 0)
            total = jnp.minimum(sample + WT, count * length - 1) - jnp.maximum(sample - WT, 0) + 1
            mean = mean / total.astype(F32)
        else:
            mean = mean * (1.0 / (2 * WT + 1))
        rows = slice(TB * b, TB * (b + 1))
        flat[rows] = (flat[rows].astype(F32) * inverse(mean + 1e-05)).astype(BF)
    spectrum = jnp.dot(table_ref[...], flat[...], preferred_element_type=F32)
    real, imag = spectrum[:BINS], spectrum[BINS:]
    magnitude = jnp.sqrt(real * real + imag * imag)
    upper = magnitude.astype(BF)
    lower = (magnitude - upper.astype(F32)).astype(BF)
    smooth = jnp.dot(smooth_ref[...], upper, preferred_element_type=F32)
    smooth += jnp.dot(smooth_ref[...], lower, preferred_element_type=F32)
    factor = taper_ref[...] * inverse(smooth * (1.0 / (2 * WF + 1)) + 1e-05)
    real, imag = real[WF : WF + NF] * factor, imag[WF : WF + NF] * factor
    low_ref[:, :NH] = real[:NH].T.astype(BF)
    low_ref[:, NH:] = imag[:NH].T.astype(BF)
    high_ref[:, :NH] = real[NH:].T.astype(BF)
    high_ref[:, NH:] = imag[NH:].T.astype(BF)


def whiten(place, dec, x, before, after, fix, part, parts):
    rows, width = x.shape
    length = dec.shape[0]
    held = width // parts
    chunk = lane_chunk(held)
    steps = held // chunk
    first = part * steps
    tables = (
        ones_band(TB, TB + 2 * WT, 2 * WT + 1),
        forward_table(),
        ones_band(NF, BINS, 2 * WF + 1),
        taper()[:, None],
    )
    column = lambda c: (0, first + c)
    last = rows // RAW - 1
    return pl.pallas_call(
        whiten_kernel,
        grid=(steps,),
        in_specs=[
            pl.BlockSpec(memory_space=pltpu.SMEM),
            pl.BlockSpec((length, chunk), column),
            pl.BlockSpec((RAW, chunk), column),
            pl.BlockSpec((RAW, chunk), lambda c: (last, first + c)),
            pl.BlockSpec((RAW + WT, chunk), column),
            pl.BlockSpec((RAW + WT, chunk), column),
            whole(fix.shape),
        ]
        + [whole(table.shape) for table in tables],
        out_specs=[pl.BlockSpec((chunk, 2 * NH), lambda c: (c, 0))] * 2,
        out_shape=[jax.ShapeDtypeStruct((held, 2 * NH), BF)] * 2,
        scratch_shapes=[pltpu.VMEM((length + 2 * WT, chunk), BF), pltpu.VMEM((length, chunk), BF)],
        compiler_params=params(),
    )(place, dec, x, x, before, after, fix, *tables)


def one_hot(ids, columns):
    hits = ids == lax.broadcasted_iota(jnp.int32, (ids.shape[0], columns), 1)
    return jnp.where(hits, 1.0, 0.0).astype(BF)


def pick_kernel(each, ids_ref, *refs):
    out_ref = refs[-1]
    owners, rows, _ = out_ref.shape
    parts = refs[:-1]
    step = pl.program_id(0)
    for p in range(len(parts) // (out_ref.shape[2] // (2 * NH))):
        halves = parts[p :: len(parts) // (out_ref.shape[2] // (2 * NH))]

        @pl.when(step // each == p)
        def _(halves=halves):
            hot = one_hot(ids_ref[...], halves[0].shape[0])
            for h, ref in enumerate(halves):
                picked = jnp.dot(hot, ref[...], preferred_element_type=F32)
                out_ref[:, :, 2 * NH * h : 2 * NH * (h + 1)] = picked.astype(BF).reshape(owners, rows, 2 * NH)


def pick(ids, halves):
    groups, owners, capacity = ids.shape
    parts = len(halves[0])
    held_all = parts * halves[0][0].shape[0]
    join = 1
    while join * capacity % 16 != 0:
        join *= 2
    steps = groups // join
    each = steps // parts
    held = held_all // steps
    local = ids.reshape(steps, join, owners, capacity).transpose(0, 2, 1, 3)
    local = local + (jnp.arange(join, dtype=jnp.int32) * (held // join))[None, None, :, None]
    rows = owners * join * capacity
    specs = [
        pl.BlockSpec((held, 2 * NH), lambda g, p=p: (jnp.clip(g - p * each, 0, each - 1), 0))
        for _ in halves
        for p in range(parts)
    ]
    return pl.pallas_call(
        functools.partial(pick_kernel, each),
        grid=(steps,),
        in_specs=[pl.BlockSpec((rows, 1), lambda g: (g, 0))] + specs,
        out_specs=pl.BlockSpec((owners, join * capacity, 2 * NH * len(halves)), lambda g: (0, g, 0)),
        out_shape=jax.ShapeDtypeStruct((owners, groups * capacity, 2 * NH * len(halves)), BF),
        compiler_params=params(),
    )(local.reshape(steps * rows, 1), *[part for half in halves for part in half])


def correlate_kernel(segments, scalar_ref, ids_ref, own_ref, mirrored_ref, table_ref, *refs):
    receivers, rest = refs[:segments], refs[segments:]
    out_ref = rest[-1]
    pairs = out_ref.shape[0]
    held = own_ref.shape[1]
    slots = ids_ref[:, :1]
    pick_own = one_hot(slots, held)
    pick_mirrored = one_hot(slots - held, held)
    pick_receiver = one_hot(ids_ref[:, 1:], receivers[0].shape[0])
    real = imag = None
    for k in range(segments):
        s = scalar_ref[1 + k]
        a = jnp.dot(pick_own, own_ref[s], preferred_element_type=F32)
        a += jnp.dot(pick_mirrored, mirrored_ref[s], preferred_element_type=F32)
        b = jnp.dot(pick_receiver, receivers[k][...], preferred_element_type=F32)
        a_re, a_im, b_re, b_im = a[:, :NH], a[:, NH:], b[:, :NH], b[:, NH:]
        re = a_re * b_re + a_im * b_im
        im = a_im * b_re - a_re * b_im
        real = re if k == 0 else real + re
        imag = im if k == 0 else imag + im
    values = jnp.dot(real.astype(BF), table_ref[:NH], preferred_element_type=F32)
    values += jnp.dot(imag.astype(BF), table_ref[NH:], preferred_element_type=F32)
    if len(rest) == 1:
        out_ref[...] = values
    else:
        place = pl.program_id(0) * pairs + lax.broadcasted_iota(jnp.int32, values.shape, 0)
        scale = 1.0 / math.sqrt(segments * NF)
        out_ref[...] = jnp.where(place < scalar_ref[0], (rest[0][...] + values) * scale, 0.0)


def correlate(scalars, ids, own, mirrored, receivers, half, partial):
    pairs = ids.shape[0]
    segments = len(receivers)
    block = min(pairs, 1024)
    table = lag_table().reshape(2, 2, NH, LAGS)[:, half].reshape(2 * NH, LAGS)
    once = pl.Buffered(1)
    row = pl.BlockSpec((block, LAGS), lambda p: (p, 0))
    lanes = lambda p: (0, half)
    return pl.pallas_call(
        functools.partial(correlate_kernel, segments),
        grid=(pairs // block,),
        in_specs=[
            pl.BlockSpec(memory_space=pltpu.SMEM),
            pl.BlockSpec((block, 2), lambda p: (p, 0)),
            pl.BlockSpec(own.shape[:2] + (2 * NH,), lambda p: (0, 0, half), pipeline_mode=once),
            pl.BlockSpec(mirrored.shape, lambda p: (0, 0, 0), pipeline_mode=once),
            whole(table.shape),
        ]
        + [pl.BlockSpec((r.shape[0], 2 * NH), lanes, pipeline_mode=once) for r in receivers]
        + [row for _ in partial],
        out_specs=row,
        out_shape=jax.ShapeDtypeStruct((pairs, LAGS), F32),
        compiler_params=params(),
    )(scalars, ids, own, mirrored, table, *receivers, *partial)


def on_device(strain, taps, send_rows, pair_source, pair_receiver, pair_count):
    n_tm, n_sub = lax.axis_size("tm"), lax.axis_size("sub")
    my_tm, my_half = lax.axis_index("tm"), lax.axis_index("half")
    capacity = send_rows.shape[3]
    width = strain.shape[1]
    parts = 2 if width % 256 == 0 and n_tm % 2 == 0 and width // 2 % 128 == 0 else 1
    swap = [(0, 1), (1, 0)]

    def shifted(array, by):
        return lax.ppermute(array, "tm", [(i, (i + by) % n_tm) for i in range(n_tm)])

    low, high, fix = edges(strain, taps)
    before = lax.ppermute(high, "tm", [(i, i + 1) for i in range(n_tm - 1)])
    after = lax.ppermute(low, "tm", [(i + 1, i) for i in range(n_tm - 1)])
    dec = decimate(strain, taps)

    asked = send_rows[0].reshape(n_tm, 2, n_sub, capacity).transpose(1, 0, 2, 3).reshape(1, 2, -1)
    asked = jnp.broadcast_to(asked, (n_tm,) + asked.shape[1:]).reshape(2 * n_tm, -1)
    asked = lax.all_to_all(asked, ("tm", "half"), 0, 0, tiled=True)
    asked = asked.reshape(n_tm, 2, n_tm * n_sub, capacity)
    asked_own = lax.dynamic_index_in_dim(asked, my_half, 1, keepdims=False)
    asked_mirrored = lax.dynamic_index_in_dim(asked, 1 - my_half, 1, keepdims=False)

    place = jnp.stack([my_tm, jnp.int32(n_tm)]).astype(jnp.int32)
    held = [whiten(place, dec, strain, before, after, fix, p, parts) for p in range(parts)]
    held = [list(half) for half in zip(*held)]
    mirrored = [[lax.ppermute(part, "half", swap) for part in half] for half in held]

    exchange = functools.partial(
        lax.all_to_all, axis_name=("tm", "sub"), split_axis=0, concat_axis=0, tiled=True
    )

    def by_segment(received):
        return received.reshape(n_tm, -1, received.shape[2])

    own = exchange(pick(asked_own, held))
    rows = jnp.concatenate([jnp.concatenate(half, axis=0) for half in held], axis=1)
    rows = rows.reshape(n_tm, -1, 4 * NH)
    receivers = [lax.dynamic_index_in_dim(rows, my_tm, 0, keepdims=False)]
    for a in range(1, n_tm):
        receivers.append(shifted(lax.dynamic_index_in_dim(rows, (my_tm + a) % n_tm, 0, keepdims=False), a))
    segment = (my_tm - jnp.arange(n_tm, dtype=jnp.int32)) % n_tm
    scalars = jnp.concatenate([pair_count, segment]).astype(jnp.int32)

    sender, column = pair_source[0] // capacity, pair_source[0] % capacity
    group, chan = sender // (2 * n_sub), sender % (2 * n_sub)
    half, sub = chan // n_sub, chan % n_sub
    slot = (sub * n_tm + group) * capacity + column
    slot += jnp.where(half == my_half, 0, n_sub * n_tm * capacity)
    ids = jnp.stack([slot, pair_receiver[0]], axis=1)

    outgoing = pick(asked_mirrored, [mirrored[0]])
    outgoing, own, mirrored[1][0], *receivers = lax.optimization_barrier((outgoing, own, mirrored[1][0], *receivers))
    others = exchange(outgoing)
    outgoing = pick(asked_mirrored, [mirrored[1]])
    outgoing, others = lax.optimization_barrier((outgoing, others))
    own = by_segment(own)
    partial = [correlate(scalars, ids, own, by_segment(others), receivers, 0, [])]
    others = exchange(outgoing)
    return correlate(scalars, ids, own, by_segment(others), receivers, 1, partial)[None]


def solution(mesh):
    n_tm, n_chan = mesh.devices.shape
    split = Mesh(mesh.devices.reshape(n_tm, 2, n_chan // 2), ("tm", "half", "sub"))
    device = ("tm", "half", "sub")
    return jax.shard_map(
        on_device,
        mesh=split,
        in_specs=(
            P("tm", ("half", "sub")),
            P(),
            P(device, None, None, None),
            P(device, None),
            P(device, None),
            P(device),
        ),
        out_specs=P(device, None, None),
        check_vma=False,
    )
```

time: 202 us -> 168 us (0.83)
  waiting for transfers between devices: 100 us -> 54.2 us
  blocking collectives: 18.9 us -> 0 us
  starting transfers between devices: 20.4 us -> 36.7 us
  Pallas kernels: 50.6 us -> 61.4 us
  local copies, waits for them, and re-layouts: 8.62 us -> 11.5 us
    all_to_all x2 -> x4, waiting for transfers between devices: 92.9 us -> 2.02 us  [the longest x2 2.01 us: on_device(): others = exchange(outgoing)]
    ppermute x4 -> x9, waiting for transfers between devices: 7.51 us -> 52.2 us  [the longest x4 48.4 us: on_device(): lax.ppermute(part, 'half', swap)]
    all_gather x1 -> x0, blocking collectives: 18.9 us -> none  [on_device(): asked = lax.all_gather(send_rows[0], 'tm')]
    all_to_all x2 -> x4, starting transfers between devices: 8.66 us -> 21.7 us  [the longest x2 9.34 us: on_device(): others = exchange(outgoing)]
    pallas_call x4 -> x8, Pallas kernels: 40.8 us -> 51.7 us  [the longest x2 22.8 us: correlate(): pl.pallas_call(functools.partial(correlate_kernel, segments), grid=(pairs...]
    ppermute x4 -> x9, starting transfers between devices: 11.7 us -> 15 us  [the longest x4 5.52 us: on_device(): lax.ppermute(part, 'half', swap)]
    unnamed x12 -> x32, local copies, waits for them, and re-layouts: 1.81 us -> 4.04 us
    another operation x1 -> x2, local copies, waits for them, and re-layouts: 3.48 us -> 4.14 us  [pick(): local.reshape(steps * rows, 1)]
  transfers between devices with their start and end apart: 6 -> 13, of which waited for: 4 -> 6; matrix products, arithmetic and copies ran while one was open for 3% -> 6% of each run, Pallas kernels for 5% -> 18%
where the time goes in v1:
time: 168 us; the launch traced here: 167 us
  Pallas kernels  61.4 us (37%)
  waiting for transfers between devices  54.2 us (32%)
  starting transfers between devices  36.7 us (22%)
  local copies, waits for them, and re-layouts  11.5 us (7%)
  other arithmetic  2.57 us (2%)
    ppermute x4, waiting for transfers between devices, on_device(): lax.ppermute(part, 'half', swap)  48.4 us
    pallas_call x2, Pallas kernels, correlate(): pl.pallas_call(functools.partial(correlate_kernel, segments), grid=(pairs...  22.8 us
    pallas_call x3, Pallas kernels, pick(): pl.pallas_call(functools.partial(pick_kernel, each), grid=(steps,), in_sp...  13.3 us
    pallas_call x2, Pallas kernels, whiten(): pl.pallas_call(whiten_kernel, grid=(steps,), in_specs=[pl.BlockSpec(memor...  12.6 us
    pallas_call x1, Pallas kernels, decimate(): pl.pallas_call(decimate_kernel, grid=(width // chunk,), in_specs=[pl.Bloc...  9.63 us
    all_to_all x2, starting transfers between devices, on_device(): others = exchange(outgoing)  9.34 us
    all_to_all x1, starting transfers between devices, on_device(): asked = lax.all_to_all(asked, ('tm', 'half'), 0, 0, tiled=True)  6.9 us
    ppermute x4, starting transfers between devices, on_device(): lax.ppermute(part, 'half', swap)  5.52 us
  transfers between devices with their start and end apart: 13, of which 6 were waited for; matrix products, arithmetic and copies ran while one was open for 6% of the time, Pallas kernels for 18%

profile of v1, /device:TPU:0, one launch (start us, length us, event | category | flops | bytes accessed | tf_op | source)
XLA Modules:
  0.0 167.2 jit_solution(10568159100572573891)
XLA Ops:
  0.0 3.1 %shard_map.155 = (bf16[128,1280]{1,0:T(8,128)(2,1)}, bf16[128,1280]{1,0:T(8,128)(2,1)}, bf16[32,128]{1,0:T(8,128)(2,1)}) custom-call(f32[40]{0:T(128)} %taps_ref.3, bf16[5120,1280]{1,0:T(8,128)(2,1)} %last_ref.5, bf16[5120,1280]{1,0:T(8,128)(2,1)} %last_ref.5), custom_call_target="tpu_custom_call" | custom-call | tf_op jit(solution)/shard_map/pallas_call | solution.py:103
  3.1 4.8 %collective-permute-start = (bf16[128,1280]{1,0:T(8,128)(2,1)}, bf16[128,1280]{1,0:T(8,128)(2,1)S(1)}, u32[]{:S(2)}, u32[]{:S(2)}) collective-permute-start(bf16[128,1280]{1,0:T(8,128)(2,1)} %get-tuple-element.21), channel_id=1, source_target_pairs={{0,8},{8,16},{16,24},{1,9},{9,17},{17,25},{2,10},{10,18},{18,26},{... | collective-permute-start | bytes 983048 | tf_op jit(solution)/shard_map/ppermute | solution.py:367
  7.9 1.3 collective-permute-start.1
  10.0 6.9 %all-to-all-start = ((s32[8,1,512]{2,1,0:T(1,128)}), s32[8,1,512]{2,1,0:T(1,128)S(1)}, u32[]{:S(2)}, u32[]{:S(2)}) async-start(s32[8,1,512]{2,1,0:T(1,128)} %all_to_all.15), calls=%async_computation | async-start | bytes 32768 | tf_op jit(solution)/shard_map/all_to_all | solution.py:373
  17.5 9.6 %shard_map.154.dec_ref = bf16[1024,1280]{1,0:T(8,128)(2,1)} custom-call(f32[40]{0:T(128)} %taps_ref.3, bf16[5120,1280]{1,0:T(8,128)(2,1)} %last_ref.5), custom_call_target="tpu_custom_call" | custom-call | tf_op jit(solution)/shard_map/pallas_call | solution.py:150
  27.3 2.1 %reshape_transpose_reshape.10.ids_ref = s32[2048,1]{1,0:T(8,128)} reshape(s32[4,1,16,32]{3,2,1,0:T(8,128)S(1)} %get-tuple-element.41) | data formatting | bytes 16384 | tf_op jit(solution)/shard_map/reshape;transpose;reshape | solution.py:296
  30.2 6.3 %shard_map.157 = (bf16[640,256]{1,0:T(8,128)(2,1)}, bf16[640,256]{1,0:T(8,128)(2,1)}) custom-call(s32[2]{0:T(128)} %pad_add_fusion.2.place_ref, bf16[1024,1280]{1,0:T(8,128)(2,1)} %shard_map.154.dec_ref, bf16[5120,1280]{1,0:T(8,128)(2,1)} %last_ref.5, bf16[5120,1280]{1,0:T(8,128)(2,1)} %last_ref.5, bf16[128,1280]{1,0:T(8,128)(2,1)} %copy-done.3, ...), custom_call_target="tpu_custom_call" | custom-call | tf_op jit(solution)/shard_map/pallas_call | solution.py:230
  36.5 6.3 %shard_map.156 = (bf16[640,256]{1,0:T(8,128)(2,1)}, bf16[640,256]{1,0:T(8,128)(2,1)}) custom-call(s32[2]{0:T(128)} %pad_add_fusion.2.place_ref, bf16[1024,1280]{1,0:T(8,128)(2,1)} %shard_map.154.dec_ref, bf16[5120,1280]{1,0:T(8,128)(2,1)} %last_ref.5, bf16[5120,1280]{1,0:T(8,128)(2,1)} %last_ref.5, bf16[128,1280]{1,0:T(8,128)(2,1)} %copy-done.3, ...), custom_call_target="tpu_custom_call" | custom-call | tf_op jit(solution)/shard_map/pallas_call | solution.py:230
  42.8 4.8 %shard_map.159 = bf16[16,128,512]{2,1,0:T(8,128)(2,1)} custom-call(s32[2048,1]{1,0:T(8,128)} %reshape_transpose_reshape.10.ids_ref, bf16[640,256]{1,0:T(8,128)(2,1)} %get-tuple-element.24.refs_0_, bf16[640,256]{1,0:T(8,128)(2,1)} %get-tuple-element.25.refs_1_, bf16[640,256]{1,0:T(8,128)(2,1)} %get-tuple-element.26.refs_2_, ...), custom_call_target="tpu_custom_call" | custom-call | tf_op jit(solution)/shard_map/pallas_call | solution.py:289
  47.6 5.4 %all-to-all-start.1 = ((bf16[16,128,512]{2,1,0:T(8,128)(2,1)}), bf16[16,128,512]{2,1,0:T(8,128)(2,1)S(1)}, u32[]{:S(2)}, u32[]{:S(2)}) async-start(bf16[16,128,512]{2,1,0:T(8,128)(2,1)} %shard_map.159), calls=%async_computation.1 | async-start | bytes 4194304 | tf_op jit(solution)/shard_map/all_to_all | solution.py:390
  53.1 2.5 %collective-permute-start.3 = (bf16[640,256]{1,0:T(8,128)(2,1)S(1)}, bf16[640,256]{1,0:T(8,128)(2,1)S(1)}, u32[]{:S(2)}, u32[]{:S(2)}) collective-permute-start(bf16[640,256]{1,0:T(8,128)(2,1)S(1)} %copy-done.10), channel_id=1, source_target_pairs={{0,4},{4,0},{1,5},{5,1},{2,6},{6,2},{3,7},{7,3},{8,12},{12,8},{9,1... | collective-permute-start | bytes 983048 | tf_op jit(solution)/shard_map/ppermute | solution.py:381
  56.1 2.4 %collective-permute-start.4 = (bf16[640,256]{1,0:T(8,128)(2,1)S(1)}, bf16[640,256]{1,0:T(8,128)(2,1)}, u32[]{:S(2)}, u32[]{:S(2)}) collective-permute-start(bf16[640,256]{1,0:T(8,128)(2,1)S(1)} %copy-done.9), channel_id=1, source_target_pairs={{0,4},{4,0},{1,5},{5,1},{2,6},{6,2},{3,7},{7,3},{8,12},{12,8},{9,1... | collective-permute-start | bytes 983048 | tf_op jit(solution)/shard_map/ppermute | solution.py:381
  58.5 1.1 maximum_maximum_fusion
  59.6 1.1 dynamic-slice_bitcast_fusion
  60.7 2.8 %collective-permute-start.7 = (bf16[320,512]{1,0:T(8,128)(2,1)}, bf16[320,512]{1,0:T(8,128)(2,1)S(1)}, u32[]{:S(2)}, u32[]{:S(2)}) collective-permute-start(bf16[320,512]{1,0:T(8,128)(2,1)} %get-tuple-element.37), channel_id=1, source_target_pairs={{0,24},{8,0},{16,8},{24,16},{1,25},{9,1},{17,9},{25,17},{2,26},{10... | collective-permute-start | bytes 983048 | tf_op jit(solution)/shard_map/ppermute | solution.py:364
  64.0 22.6 %collective-permute-done.3.refs_1_ = bf16[640,256]{1,0:T(8,128)(2,1)S(1)} collective-permute-done((bf16[640,256]{1,0:T(8,128)(2,1)S(1)}, bf16[640,256]{1,0:T(8,128)(2,1)S(1)}, u32[]{:S(2)}, u32[]{:S(2)}) %collective-permute-start.3) | collective-permute-done | bytes 327712 | tf_op jit(solution)/shard_map/ppermute | solution.py:381
  86.7 0.7 copy-done.11
  87.4 2.1 %reshape_transpose_reshape.9.ids_ref = s32[2048,1]{1,0:T(8,128)} reshape(s32[4,1,16,32]{3,2,1,0:T(8,128)S(1)} %get-tuple-element.42) | data formatting | bytes 16384 | tf_op jit(solution)/shard_map/reshape;transpose;reshape | solution.py:296
  89.5 4.3 %collective-permute-done.2.refs_0_ = bf16[640,256]{1,0:T(8,128)(2,1)} collective-permute-done((bf16[640,256]{1,0:T(8,128)(2,1)}, bf16[640,256]{1,0:T(8,128)(2,1)}, u32[]{:S(2)}, u32[]{:S(2)}) %collective-permute-start.2) | collective-permute-done | bytes 327712 | tf_op jit(solution)/shard_map/ppermute | solution.py:381
  93.8 4.3 %shard_map.158 = bf16[16,128,256]{2,1,0:T(8,128)(2,1)} custom-call(s32[2048,1]{1,0:T(8,128)} %reshape_transpose_reshape.9.ids_ref, bf16[640,256]{1,0:T(8,128)(2,1)} %collective-permute-done.2.refs_0_, bf16[640,256]{1,0:T(8,128)(2,1)} %copy-done.11), custom_call_target="tpu_custom_call" | custom-call | tf_op jit(solution)/shard_map/pallas_call | solution.py:289
  98.1 2.5 %collective-permute-done.4.refs_0_ = bf16[640,256]{1,0:T(8,128)(2,1)} collective-permute-done((bf16[640,256]{1,0:T(8,128)(2,1)S(1)}, bf16[640,256]{1,0:T(8,128)(2,1)}, u32[]{:S(2)}, u32[]{:S(2)}) %collective-permute-start.4) | collective-permute-done | bytes 327712 | tf_op jit(solution)/shard_map/ppermute | solution.py:381
  100.5 3.7 %collective-permute-done.5.refs_1_ = bf16[320,512]{1,0:T(8,128)(2,1)S(1)} collective-permute-done((bf16[320,512]{1,0:T(8,128)(2,1)}, bf16[320,512]{1,0:T(8,128)(2,1)S(1)}, u32[]{:S(2)}, u32[]{:S(2)}) %collective-permute-start.5) | collective-permute-done | bytes 327712 | tf_op jit(solution)/shard_map/ppermute | solution.py:364
  105.0 3.8 %all-to-all-start.2 = ((bf16[16,128,256]{2,1,0:T(8,128)(2,1)}), bf16[16,128,256]{2,1,0:T(8,128)(2,1)S(1)}, u32[]{:S(2)}, u32[]{:S(2)}) async-start(bf16[16,128,256]{2,1,0:T(8,128)(2,1)} %shard_map.158), calls=%async_computation.2 | async-start | bytes 2097152 | tf_op jit(solution)/shard_map/all_to_all | solution.py:408
  109.0 19.0 %collective-permute-done.8.refs_1_ = bf16[640,256]{1,0:T(8,128)(2,1)S(1)} collective-permute-done((bf16[640,256]{1,0:T(8,128)(2,1)}, bf16[640,256]{1,0:T(8,128)(2,1)S(1)}, u32[]{:S(2)}, u32[]{:S(2)}) %collective-permute-start.8) | collective-permute-done | bytes 327712 | tf_op jit(solution)/shard_map/ppermute | solution.py:381
  128.0 0.7 copy-done.12
  128.7 4.2 %shard_map.160 = bf16[16,128,256]{2,1,0:T(8,128)(2,1)} custom-call(s32[2048,1]{1,0:T(8,128)} %reshape_transpose_reshape.9.ids_ref, bf16[640,256]{1,0:T(8,128)(2,1)} %collective-permute-done.4.refs_0_, bf16[640,256]{1,0:T(8,128)(2,1)} %copy-done.12), custom_call_target="tpu_custom_call" | custom-call | tf_op jit(solution)/shard_map/pallas_call | solution.py:289
  132.9 5.5 %all-to-all-start.3 = ((bf16[16,128,256]{2,1,0:T(8,128)(2,1)}), bf16[16,128,256]{2,1,0:T(8,128)(2,1)S(1)}, u32[]{:S(2)}, u32[]{:S(2)}) async-start(bf16[16,128,256]{2,1,0:T(8,128)(2,1)} %shard_map.160), calls=%async_computation.3 | async-start | bytes 2097152 | tf_op jit(solution)/shard_map/all_to_all | solution.py:413
  139.3 1.4 copy.31.ids_ref
  141.4 11.2 %shard_map.161.refs_4_ = f32[2048,256]{1,0:T(8,128)} custom-call(s32[5]{0:T(128)} %pad_add_fusion.1.scalar_ref, s32[2048,2]{1,0:T(8,128)} %copy.31.ids_ref, bf16[4,512,512]{2,1,0:T(8,128)(2,1)} %bitcast.36, bf16[4,512,256]{2,1,0:T(8,128)(2,1)} %bitcast.40, bf16[256,256]{1,0:T(8,128)(2,1)} %constant.142.clone.table_ref, ...), custom_call_target="tpu_custom_call" | custom-call | tf_op jit(solution)/shard_map/pallas_call | solution.py:337
  152.6 2.0 %all-to-all-done.3 = bf16[16,128,256]{2,1,0:T(8,128)(2,1)S(1)} async-done(((bf16[16,128,256]{2,1,0:T(8,128)(2,1)}), bf16[16,128,256]{2,1,0:T(8,128)(2,1)S(1)}, u32[]{:S(2)}, u32[]{:S(2)}) %all-to-all-start.3) | async-done | bytes 1048608 | tf_op jit(solution)/shard_map/all_to_all | solution.py:413
  154.6 1.0 copy-done.1
  155.6 11.6 %shard_map.162 = f32[2048,256]{1,0:T(8,128)} custom-call(s32[5]{0:T(128)} %pad_add_fusion.1.scalar_ref, s32[2048,2]{1,0:T(8,128)} %copy.31.ids_ref, bf16[4,512,512]{2,1,0:T(8,128)(2,1)} %bitcast.37, bf16[4,512,256]{2,1,0:T(8,128)(2,1)} %bitcast.39, bf16[256,256]{1,0:T(8,128)(2,1)} %constant.143.clone.table_ref, bf16[320,512]{1,0:T(8,128)(2,1)} %get-tuple-element.32.refs_0_, ...), custom_call_target="tpu_custom_call" | custom-call | tf_op jit(solution)/shard_map/pallas_call | solution.py:337
  (52 shorter events, 5.2 us)
Async XLA Ops:
  0.0 9.2 %copy-start.13 = (s32[1,4,8,32]{3,2,1,0:T(8,128)S(1)}, s32[1,4,8,32]{3,2,1,0:T(8,128)}, u32[]{:S(2)}) copy-start(s32[1,4,8,32]{3,2,1,0:T(8,128)} %param.18) | copy-start | bytes 12292
  3.1 26.3 %collective-permute-start = (bf16[128,1280]{1,0:T(8,128)(2,1)}, bf16[128,1280]{1,0:T(8,128)(2,1)S(1)}, u32[]{:S(2)}, u32[]{:S(2)}) collective-permute-start(bf16[128,1280]{1,0:T(8,128)(2,1)} %get-tuple-element.21), channel_id=1, source_target_pairs={{0,8},{8,16},{16,24},{1,9},{9,17},{17,25},{2,10},{10,18},{18,26},{... | collective-permute-start | bytes 983048 | tf_op jit(solution)/shard_map/ppermute | solution.py:367
  7.9 21.4 %collective-permute-start.1 = (bf16[128,1280]{1,0:T(8,128)(2,1)}, bf16[128,1280]{1,0:T(8,128)(2,1)S(1)}, u32[]{:S(2)}, u32[]{:S(2)}) collective-permute-start(bf16[128,1280]{1,0:T(8,128)(2,1)} %get-tuple-element.22), channel_id=1, source_target_pairs={{8,0},{16,8},{24,16},{9,1},{17,9},{25,17},{10,2},{18,10},{26,18},{... | collective-permute-start | bytes 983048 | tf_op jit(solution)/shard_map/ppermute | solution.py:368
  10.0 17.2 %all-to-all-start = ((s32[8,1,512]{2,1,0:T(1,128)}), s32[8,1,512]{2,1,0:T(1,128)S(1)}, u32[]{:S(2)}, u32[]{:S(2)}) async-start(s32[8,1,512]{2,1,0:T(1,128)} %all_to_all.15), calls=%async_computation | async-start | bytes 32768 | tf_op jit(solution)/shard_map/all_to_all | solution.py:373
  29.4 0.7 copy-start.3
  29.4 0.8 copy-start.4
  47.6 5.5 %copy-start.10 = (bf16[640,256]{1,0:T(8,128)(2,1)S(1)}, bf16[640,256]{1,0:T(8,128)(2,1)}, u32[]{:S(2)}) copy-start(bf16[640,256]{1,0:T(8,128)(2,1)} %get-tuple-element.25.refs_1_) | copy-start | bytes 983044
  47.6 8.5 %copy-start.9 = (bf16[640,256]{1,0:T(8,128)(2,1)S(1)}, bf16[640,256]{1,0:T(8,128)(2,1)}, u32[]{:S(2)}) copy-start(bf16[640,256]{1,0:T(8,128)(2,1)} %get-tuple-element.26.refs_2_) | copy-start | bytes 983044
  47.6 10.9 %copy-start.8 = (bf16[640,256]{1,0:T(8,128)(2,1)S(1)}, bf16[640,256]{1,0:T(8,128)(2,1)}, u32[]{:S(2)}) copy-start(bf16[640,256]{1,0:T(8,128)(2,1)} %get-tuple-element.27.refs_3_) | copy-start | bytes 983044
  47.6 56.7 %all-to-all-start.1 = ((bf16[16,128,512]{2,1,0:T(8,128)(2,1)}), bf16[16,128,512]{2,1,0:T(8,128)(2,1)S(1)}, u32[]{:S(2)}, u32[]{:S(2)}) async-start(bf16[16,128,512]{2,1,0:T(8,128)(2,1)} %shard_map.159), calls=%async_computation.1 | async-start | bytes 4194304 | tf_op jit(solution)/shard_map/all_to_all | solution.py:390
  53.1 33.6 %collective-permute-start.3 = (bf16[640,256]{1,0:T(8,128)(2,1)S(1)}, bf16[640,256]{1,0:T(8,128)(2,1)S(1)}, u32[]{:S(2)}, u32[]{:S(2)}) collective-permute-start(bf16[640,256]{1,0:T(8,128)(2,1)S(1)} %copy-done.10), channel_id=1, source_target_pairs={{0,4},{4,0},{1,5},{5,1},{2,6},{6,2},{3,7},{7,3},{8,12},{12,8},{9,1... | collective-permute-start | bytes 983048 | tf_op jit(solution)/shard_map/ppermute | solution.py:381
  55.6 38.2 %collective-permute-start.2 = (bf16[640,256]{1,0:T(8,128)(2,1)}, bf16[640,256]{1,0:T(8,128)(2,1)}, u32[]{:S(2)}, u32[]{:S(2)}) collective-permute-start(bf16[640,256]{1,0:T(8,128)(2,1)} %get-tuple-element.24.refs_0_), channel_id=1, source_target_pairs={{0,4},{4,0},{1,5},{5,1},{2,6},{6,2},{3,7},{7,3},{8,12},{12,8},{9,1... | collective-permute-start | bytes 983048 | tf_op jit(solution)/shard_map/ppermute | solution.py:381
  56.1 44.4 %collective-permute-start.4 = (bf16[640,256]{1,0:T(8,128)(2,1)S(1)}, bf16[640,256]{1,0:T(8,128)(2,1)}, u32[]{:S(2)}, u32[]{:S(2)}) collective-permute-start(bf16[640,256]{1,0:T(8,128)(2,1)S(1)} %copy-done.9), channel_id=1, source_target_pairs={{0,4},{4,0},{1,5},{5,1},{2,6},{6,2},{3,7},{7,3},{8,12},{12,8},{9,1... | collective-permute-start | bytes 983048 | tf_op jit(solution)/shard_map/ppermute | solution.py:381
  60.7 39.8 %collective-permute-start.7 = (bf16[320,512]{1,0:T(8,128)(2,1)}, bf16[320,512]{1,0:T(8,128)(2,1)S(1)}, u32[]{:S(2)}, u32[]{:S(2)}) collective-permute-start(bf16[320,512]{1,0:T(8,128)(2,1)} %get-tuple-element.37), channel_id=1, source_target_pairs={{0,24},{8,0},{16,8},{24,16},{1,25},{9,1},{17,9},{25,17},{2,26},{10... | collective-permute-start | bytes 983048 | tf_op jit(solution)/shard_map/ppermute | solution.py:364
  63.5 37.1 %collective-permute-start.6 = (bf16[320,512]{1,0:T(8,128)(2,1)}, bf16[320,512]{1,0:T(8,128)(2,1)S(1)}, u32[]{:S(2)}, u32[]{:S(2)}) collective-permute-start(bf16[320,512]{1,0:T(8,128)(2,1)} %get-tuple-element.38), channel_id=1, source_target_pairs={{0,16},{8,24},{16,0},{24,8},{1,17},{9,25},{17,1},{25,9},{2,18},{10... | collective-permute-start | bytes 983048 | tf_op jit(solution)/shard_map/ppermute | solution.py:364
  86.7 0.7 copy-start.11
  87.4 16.9 %collective-permute-start.5 = (bf16[320,512]{1,0:T(8,128)(2,1)}, bf16[320,512]{1,0:T(8,128)(2,1)S(1)}, u32[]{:S(2)}, u32[]{:S(2)}) collective-permute-start(bf16[320,512]{1,0:T(8,128)(2,1)} %get-tuple-element.39), channel_id=1, source_target_pairs={{0,8},{8,16},{16,24},{24,0},{1,9},{9,17},{17,25},{25,1},{2,10},{10... | collective-permute-start | bytes 983048 | tf_op jit(solution)/shard_map/ppermute | solution.py:364
  100.5 32.4 %copy-start.5 = (bf16[320,512]{1,0:T(8,128)(2,1)}, bf16[320,512]{1,0:T(8,128)(2,1)S(1)}, u32[]{:S(2)}) copy-start(bf16[320,512]{1,0:T(8,128)(2,1)S(1)} %collective-permute-done.7.refs_3_) | copy-start | bytes 983044
  100.5 3.8 %copy-start.6 = (bf16[320,512]{1,0:T(8,128)(2,1)}, bf16[320,512]{1,0:T(8,128)(2,1)S(1)}, u32[]{:S(2)}) copy-start(bf16[320,512]{1,0:T(8,128)(2,1)S(1)} %collective-permute-done.6.refs_2_) | copy-start | bytes 983044
  104.3 0.7 copy-start.7
  104.3 28.6 %copy-start = (bf16[16,128,512]{2,1,0:T(8,128)(2,1)}, bf16[16,128,512]{2,1,0:T(8,128)(2,1)S(1)}, u32[]{:S(2)}) copy-start(bf16[16,128,512]{2,1,0:T(8,128)(2,1)S(1)} %all-to-all-done.1) | copy-start | bytes 6291460
  105.0 27.9 %all-to-all-start.2 = ((bf16[16,128,256]{2,1,0:T(8,128)(2,1)}), bf16[16,128,256]{2,1,0:T(8,128)(2,1)S(1)}, u32[]{:S(2)}, u32[]{:S(2)}) async-start(bf16[16,128,256]{2,1,0:T(8,128)(2,1)} %shard_map.158), calls=%async_computation.2 | async-start | bytes 2097152 | tf_op jit(solution)/shard_map/all_to_all | solution.py:408
  108.9 30.3 %copy-start.14 = (s32[1,2048]{1,0:T(1,128)S(1)}, s32[1,2048]{1,0:T(1,128)}, u32[]{:S(2)}) copy-start(s32[1,2048]{1,0:T(1,128)} %param.19) | copy-start | bytes 24580
  108.9 30.4 %copy-start.15 = (s32[1,2048]{1,0:T(1,128)S(1)}, s32[1,2048]{1,0:T(1,128)}, u32[]{:S(2)}) copy-start(s32[1,2048]{1,0:T(1,128)} %param.20) | copy-start | bytes 24580
  108.9 19.1 %collective-permute-start.8 = (bf16[640,256]{1,0:T(8,128)(2,1)}, bf16[640,256]{1,0:T(8,128)(2,1)S(1)}, u32[]{:S(2)}, u32[]{:S(2)}) collective-permute-start(bf16[640,256]{1,0:T(8,128)(2,1)} %get-tuple-element.27.refs_3_), channel_id=1, source_target_pairs={{0,4},{4,0},{1,5},{5,1},{2,6},{6,2},{3,7},{7,3},{8,12},{12,8},{9,1... | collective-permute-start | bytes 983048 | tf_op jit(solution)/shard_map/ppermute | solution.py:381
  128.0 0.7 copy-start.12
  132.9 8.4 %copy-start.2 = (bf16[16,128,256]{2,1,0:T(8,128)(2,1)}, bf16[16,128,256]{2,1,0:T(8,128)(2,1)S(1)}, u32[]{:S(2)}) copy-start(bf16[16,128,256]{2,1,0:T(8,128)(2,1)S(1)} %all-to-all-done.2) | copy-start | bytes 3145732
  132.9 21.7 %all-to-all-start.3 = ((bf16[16,128,256]{2,1,0:T(8,128)(2,1)}), bf16[16,128,256]{2,1,0:T(8,128)(2,1)S(1)}, u32[]{:S(2)}, u32[]{:S(2)}) async-start(bf16[16,128,256]{2,1,0:T(8,128)(2,1)} %shard_map.160), calls=%async_computation.3 | async-start | bytes 2097152 | tf_op jit(solution)/shard_map/all_to_all | solution.py:413
  154.6 1.0 copy-start.1

commit v2 on v1

v2 whole, which is shorter than its diff:
```python
import functools
import math

import jax
import jax.numpy as jnp
import numpy as np
from jax import lax
from jax.experimental import pallas as pl
from jax.experimental.pallas import tpu as pltpu
from jax.sharding import Mesh
from jax.sharding import PartitionSpec as P

Q = 5
TAPS = 40
RIM = TAPS // 2
SEG = 1024
NF = 256
WF = 32
F0 = 40
TW = 32
WT = 64
LAGS = 256
BINS = NF + 2 * WF
TB = 128
FB = 64
RAW = 64
LEAD = 32
BAND = 384
NH = NF // 2
BF = jnp.bfloat16
F32 = jnp.float32
VMEM = 56 * 1024 * 1024
MOST = 52 * 1024 * 1024
PART = 24 * 1024 * 1024
TAIL = 59 * 1024 * 1024


def forward_table():
    phases = np.arange(F0 - WF, F0 + NF + WF)[:, None] * np.arange(SEG)[None, :] % SEG
    phases = phases * (2.0 * np.pi / SEG)
    return np.concatenate([np.cos(phases), -np.sin(phases)], axis=0).astype(BF)


def lag_table():
    phases = (F0 + np.arange(NF))[:, None] * (np.arange(LAGS) - LAGS // 2)[None, :] % SEG
    phases = phases * (2.0 * np.pi / SEG)
    return np.concatenate([np.cos(phases), -np.sin(phases)], axis=0).astype(BF)


def taper():
    bins = np.arange(NF)
    edge = np.minimum(bins, NF - 1 - bins)
    return np.where(edge < TW, 0.5 - 0.5 * np.cos(np.pi * (edge + 0.5) / TW), 1.0).astype(np.float32)


def ones_band(rows, columns, width):
    lag = np.arange(columns)[None, :] - np.arange(rows)[:, None]
    return ((lag >= 0) & (lag < width)).astype(BF)


def whole(shape):
    return pl.BlockSpec(shape, lambda *_: (0,) * len(shape))


def params(limit=VMEM):
    return pltpu.CompilerParams(vmem_limit_bytes=limit)


def fill_band(band_ref, taps_ref, work_ref, rows, shift):
    lanes = work_ref.shape[1]
    tap = lax.broadcasted_iota(jnp.int32, (8, 128), 1) - Q * lax.broadcasted_iota(jnp.int32, (8, 128), 0)
    pattern = jnp.zeros((8, 128), F32)
    for k in range(TAPS):
        pattern = jnp.where(tap == k, taps_ref[k], pattern)
    pattern = jnp.concatenate([pattern, jnp.zeros((8, lanes - 128), F32)], axis=1)
    for m in range(0, rows, 8):
        work_ref[m : m + 8] = pltpu.roll(pattern, (Q * m + shift) % lanes, 1)
    values = work_ref[:rows, : band_ref.shape[1]]
    upper = values.astype(BF)
    band_ref[:rows] = upper
    band_ref[rows:] = (values - upper.astype(F32)).astype(BF)


def filtered(band, x):
    both = jnp.dot(band, x, preferred_element_type=F32)
    rows = both.shape[0] // 2
    return (both[:rows] + both[rows:]).astype(BF)


EDGE = 352


def edge_kernel(taps_ref, x_ref, low_ref, high_ref, fix_ref, low, high, low_band, high_band, work, arrived):
    fetch_low = pltpu.make_async_copy(x_ref.at[pl.ds(0, EDGE)], low, arrived.at[0])
    fetch_high = pltpu.make_async_copy(x_ref.at[pl.ds(x_ref.shape[0] - EDGE, EDGE)], high, arrived.at[1])
    fetch_low.start()
    fetch_high.start()
    fill_band(low_band, taps_ref, work, WT, -RIM)
    fill_band(high_band, taps_ref, work, WT, EDGE - Q * WT - RIM)
    fill_band(fix_ref, taps_ref, work, 16, RAW - Q * 8 - RIM)
    fetch_low.wait()
    low_ref[:RAW] = low[:RAW]
    low_ref[RAW:] = filtered(low_band[...], low[...])
    fetch_high.wait()
    high_ref[:RAW] = high[EDGE - RAW :]
    high_ref[RAW:] = filtered(high_band[...], high[...])


def edges(x, taps):
    width = x.shape[1]
    in_vmem = pl.BlockSpec(memory_space=pltpu.VMEM)
    return pl.pallas_call(
        edge_kernel,
        in_specs=[pl.BlockSpec(memory_space=pltpu.SMEM), pl.BlockSpec(memory_space=pl.ANY)],
        out_specs=[in_vmem] * 3,
        out_shape=[
            jax.ShapeDtypeStruct((RAW + WT, width), BF),
            jax.ShapeDtypeStruct((RAW + WT, width), BF),
            jax.ShapeDtypeStruct((32, 2 * RAW), BF),
        ],
        scratch_shapes=[
            pltpu.VMEM((EDGE, width), BF),
            pltpu.VMEM((EDGE, width), BF),
            pltpu.VMEM((2 * WT, EDGE), BF),
            pltpu.VMEM((2 * WT, EDGE), BF),
            pltpu.VMEM((WT, 512), F32),
            pltpu.SemaphoreType.DMA((2,)),
        ],
        compiler_params=params(MOST),
    )(taps, x)


def decimate_kernel(taps_ref, x_ref, out_ref, x, main, first, work, arrived):
    length = out_ref.shape[0]
    fetches = arrived.shape[0]
    each = Q * length // fetches

    def fetch(k):
        rows = pl.ds(each * k, each)
        return pltpu.make_async_copy(x_ref.at[rows], x.at[rows], arrived.at[k])

    for k in range(fetches):
        fetch(k).start()
    fill_band(main, taps_ref, work, FB, LEAD - RIM)
    fill_band(first, taps_ref, work, FB, -RIM)
    here = 0
    for b in range(length // FB):
        start = max(Q * FB * b - LEAD, 0)
        stop = min(Q * FB * b - LEAD + BAND, Q * length)
        while each * here < stop:
            fetch(here).wait()
            here += 1
        band = first[...] if b == 0 else main[:, : stop - start]
        out_ref[FB * b : FB * (b + 1)] = filtered(band, x[start:stop])


def decimate(x, taps):
    rows, width = x.shape
    return pl.pallas_call(
        decimate_kernel,
        in_specs=[pl.BlockSpec(memory_space=pltpu.SMEM), pl.BlockSpec(memory_space=pl.ANY)],
        out_specs=pl.BlockSpec(memory_space=pltpu.VMEM),
        out_shape=jax.ShapeDtypeStruct((rows // Q, width), BF),
        scratch_shapes=[
            pltpu.VMEM((rows, width), BF),
            pltpu.VMEM((2 * FB, BAND), BF),
            pltpu.VMEM((2 * FB, BAND - LEAD), BF),
            pltpu.VMEM((FB, 512), F32),
            pltpu.SemaphoreType.DMA((8,)),
        ],
        compiler_params=params(MOST),
    )(taps, x)


def inverse(values):
    guess = pl.reciprocal(values, approx=True)
    return guess * (2.0 - values * guess)


def whiten_kernel(
    place_ref, dec_ref, first_ref, last_ref, before_ref, after_ref, fix_ref, ones_ref, table_ref, smooth_ref,
    taper_ref, low_ref, high_ref, size, flat
):
    length = dec_ref.shape[0]
    blocks = length // TB
    place, count = place_ref[0], place_ref[1]
    low = filtered(fix_ref[...], jnp.concatenate([before_ref[:RAW], first_ref[...]])).astype(F32)
    high = filtered(fix_ref[...], jnp.concatenate([last_ref[...], after_ref[:RAW]])).astype(F32)
    before = jnp.concatenate([before_ref[RAW:].astype(F32)[:-8], low[:8]])
    after = jnp.concatenate([high[8:], after_ref[RAW:].astype(F32)[8:]])
    size[:WT] = jnp.abs(jnp.where(place > 0, before, 0.0)).astype(BF)
    size[WT + length :] = jnp.abs(jnp.where(place < count - 1, after, 0.0)).astype(BF)
    flat[...] = dec_ref[...]
    flat[:TB] = jnp.concatenate([low[8:], dec_ref[:TB].astype(F32)[8:]]).astype(BF)
    flat[length - TB :] = jnp.concatenate([dec_ref[length - TB :].astype(F32)[:-8], high[:8]]).astype(BF)
    size[WT : WT + length] = jnp.abs(flat[...])
    for b in range(blocks):
        mean = jnp.dot(ones_ref[...], size[TB * b : TB * b + TB + 2 * WT], preferred_element_type=F32)
        if b == 0 or b == blocks - 1:
            sample = place * length + TB * b + lax.broadcasted_iota(jnp.int32, (TB, 1), 0)
            total = jnp.minimum(sample + WT, count * length - 1) - jnp.maximum(sample - WT, 0) + 1
            mean = mean / total.astype(F32)
        else:
            mean = mean * (1.0 / (2 * WT + 1))
        rows = slice(TB * b, TB * (b + 1))
        flat[rows] = (flat[rows].astype(F32) * inverse(mean + 1e-05)).astype(BF)
    spectrum = jnp.dot(table_ref[...], flat[...], preferred_element_type=F32)
    real, imag = spectrum[:BINS], spectrum[BINS:]
    magnitude = jnp.sqrt(real * real + imag * imag)
    smooth = jnp.dot(smooth_ref[...], magnitude.astype(BF), preferred_element_type=F32)
    factor = taper_ref[...] * inverse(smooth * (1.0 / (2 * WF + 1)) + 1e-05)
    real, imag = real[WF : WF + NF] * factor, imag[WF : WF + NF] * factor
    low_ref[:, :NH] = real[:NH].T.astype(BF)
    low_ref[:, NH:] = imag[:NH].T.astype(BF)
    high_ref[:, :NH] = real[NH:].T.astype(BF)
    high_ref[:, NH:] = imag[NH:].T.astype(BF)


def whiten(place, dec, low, high, before, after, fix, start, held):
    length, width = dec.shape
    chunk = 256 if width % 256 == 0 else 128
    first = start // chunk
    tables = (
        ones_band(TB, TB + 2 * WT, 2 * WT + 1),
        forward_table(),
        ones_band(NF, BINS, 2 * WF + 1),
        taper()[:, None],
    )
    column = lambda c: (0, first + c)
    return pl.pallas_call(
        whiten_kernel,
        grid=(held // chunk,),
        in_specs=[
            pl.BlockSpec(memory_space=pltpu.SMEM),
            pl.BlockSpec((length, chunk), column),
            pl.BlockSpec((RAW, chunk), column),
            pl.BlockSpec((RAW, chunk), column),
            pl.BlockSpec((RAW + WT, chunk), column),
            pl.BlockSpec((RAW + WT, chunk), column),
            whole(fix.shape),
        ]
        + [whole(table.shape) for table in tables],
        out_specs=[pl.BlockSpec((chunk, 2 * NH), lambda c: (c, 0))] * 2,
        out_shape=[jax.ShapeDtypeStruct((held, 2 * NH), BF)] * 2,
        scratch_shapes=[pltpu.VMEM((length + 2 * WT, chunk), BF), pltpu.VMEM((length, chunk), BF)],
        compiler_params=params(PART),
    )(place, dec, low, high, before, after, fix, *tables)


def one_hot(ids, columns):
    wide = -(-columns // 128)
    lane = lax.broadcasted_iota(jnp.int32, (128, 128 * wide), 1)
    parts = []
    for r in range(ids.shape[0]):
        column = jnp.broadcast_to(ids[r : r + 1].astype(F32), (128, 128)).T.astype(jnp.int32)
        hits = jnp.concatenate([column] * wide, axis=1) == lane
        parts.append(jnp.where(hits, 1.0, 0.0).astype(BF)[:, :columns])
    return jnp.concatenate(parts, axis=0)


def pick_kernel(ids_ref, *refs):
    *halves, out_ref = refs
    owners, rows, _ = out_ref.shape
    hot = one_hot(ids_ref[0], halves[0].shape[0])
    for h, half in enumerate(halves):
        picked = jnp.dot(hot, half[...], preferred_element_type=F32).astype(BF)
        out_ref[:, :, 2 * NH * h : 2 * NH * (h + 1)] = picked.reshape(owners, rows, 2 * NH)


def pick(ids, halves, capacity):
    groups = ids.shape[0]
    owners = ids.size // groups // capacity
    width = 2 * NH * len(halves)
    join = 1
    while join * capacity % 16 != 0:
        join *= 2
    steps = groups // join
    held = halves[0].shape[0] // steps
    rows = owners * join * capacity
    if join > 1:
        ids = ids.reshape(steps, join, owners, capacity).transpose(0, 2, 1, 3)
        ids = ids + (jnp.arange(join, dtype=jnp.int32) * (held // join))[None, None, :, None]
    return pl.pallas_call(
        pick_kernel,
        grid=(steps,),
        in_specs=[pl.BlockSpec((1, rows // 128, 128), lambda g: (g, 0, 0))]
        + [pl.BlockSpec((held, 2 * NH), lambda g: (g, 0)) for _ in halves],
        out_specs=pl.BlockSpec((owners, join * capacity, width), lambda g: (0, g, 0)),
        out_shape=jax.ShapeDtypeStruct((owners, groups * capacity, width), BF),
        compiler_params=params(PART),
    )(ids.reshape(steps, rows // 128, 128), *halves)


def pair_block(pairs, segments):
    return min(pairs, 512 if segments <= 4 else 128)


def ids_spec(block):
    return pl.BlockSpec((1, block // 128, 128), lambda p: (p, 0, 0))


def once(shape):
    return pl.BlockSpec(shape, lambda p: (0,) * len(shape), pipeline_mode=pl.Buffered(1))


def receive_kernel(ids_ref, *refs):
    receivers, (low_ref, high_ref) = refs[:-2], refs[-2:]
    hot = one_hot(ids_ref[0], receivers[0].shape[0])
    for k, rows in enumerate(receivers):
        low_ref[k] = jnp.dot(hot, rows[:, : 2 * NH], preferred_element_type=F32).astype(BF)
        high_ref[k] = jnp.dot(hot, rows[:, 2 * NH :], preferred_element_type=F32).astype(BF)


def receive(ids, receivers):
    segments, pairs = len(receivers), ids.size
    block = pair_block(pairs, segments)
    rows = pl.BlockSpec((segments, block, 2 * NH), lambda p: (0, p, 0))
    return pl.pallas_call(
        receive_kernel,
        grid=(pairs // block,),
        in_specs=[ids_spec(block)] + [once(r.shape) for r in receivers],
        out_specs=[rows, rows],
        out_shape=[jax.ShapeDtypeStruct((segments, pairs, 2 * NH), BF)] * 2,
        compiler_params=params(),
    )(ids.reshape(-1, block // 128, 128), *receivers)


def cross(hot, segment_ref, rows_ref, lanes, receiver_ref):
    real = imag = None
    for k in range(receiver_ref.shape[0]):
        a = jnp.dot(hot, rows_ref[segment_ref[k], :, lanes], preferred_element_type=F32)
        b = receiver_ref[k].astype(F32)
        a_re, a_im, b_re, b_im = a[:, :NH], a[:, NH:], b[:, :NH], b[:, NH:]
        re = a_re * b_re + a_im * b_im
        im = a_im * b_re - a_re * b_im
        real = re if k == 0 else real + re
        imag = im if k == 0 else imag + im
    return jnp.concatenate([real, imag], axis=1).astype(BF)


def own_kernel(segment_ref, ids_ref, own_ref, low_ref, high_ref, low_out, high_out):
    hot = one_hot(ids_ref[0], own_ref.shape[1])
    low_out[...] = cross(hot, segment_ref, own_ref, slice(0, 2 * NH), low_ref)
    high_out[...] = cross(hot, segment_ref, own_ref, slice(2 * NH, 4 * NH), high_ref)


def cross_own(segment, ids, own, low, high):
    segments, pairs, _ = low.shape
    block = pair_block(pairs, segments)
    rows = pl.BlockSpec((segments, block, 2 * NH), lambda p: (0, p, 0))
    out = pl.BlockSpec((block, 2 * NH), lambda p: (p, 0))
    return pl.pallas_call(
        own_kernel,
        grid=(pairs // block,),
        in_specs=[pl.BlockSpec(memory_space=pltpu.SMEM), ids_spec(block), once(own.shape), rows, rows],
        out_specs=[out, out],
        out_shape=[jax.ShapeDtypeStruct((pairs, 2 * NH), BF)] * 2,
        compiler_params=params(),
    )(segment, ids.reshape(-1, block // 128, 128), own, low, high)


def mirrored_kernel(segment_ref, ids_ref, rows_ref, receiver_ref, own_ref, out_ref):
    held = rows_ref.shape[1]
    hot = one_hot(ids_ref[0] - held, held)
    out_ref[...] = own_ref[...] + cross(hot, segment_ref, rows_ref, slice(None), receiver_ref)


def cross_mirrored(segment, ids, rows, receiver, own):
    segments, pairs, _ = receiver.shape
    block = pair_block(pairs, segments)
    out = pl.BlockSpec((block, 2 * NH), lambda p: (p, 0))
    return pl.pallas_call(
        mirrored_kernel,
        grid=(pairs // block,),
        in_specs=[
            pl.BlockSpec(memory_space=pltpu.SMEM),
            ids_spec(block),
            once(rows.shape),
            pl.BlockSpec((segments, block, 2 * NH), lambda p: (0, p, 0)),
            out,
        ],
        out_specs=out,
        out_shape=jax.ShapeDtypeStruct((pairs, 2 * NH), BF),
        compiler_params=params(TAIL),
    )(segment, ids.reshape(-1, block // 128, 128), rows, receiver, own)


def lags_kernel(segment_ref, count_ref, ids_ref, rows_ref, receiver_ref, own_ref, low_ref, table_ref, out_ref):
    pairs = out_ref.shape[0]
    held = rows_ref.shape[1]
    hot = one_hot(ids_ref[0] - held, held)
    high = own_ref[...] + cross(hot, segment_ref, rows_ref, slice(None), receiver_ref)
    values = jnp.dot(low_ref[...], table_ref[: 2 * NH], preferred_element_type=F32)
    values += jnp.dot(high, table_ref[2 * NH :], preferred_element_type=F32)
    place = pl.program_id(0) * pairs + lax.broadcasted_iota(jnp.int32, values.shape, 0)
    scale = 1.0 / math.sqrt(receiver_ref.shape[0] * NF)
    out_ref[...] = jnp.where(place < count_ref[0], values * scale, 0.0)


def lags(segment, count, ids, rows, receiver, own, low):
    segments, pairs, _ = receiver.shape
    block = pair_block(pairs, segments)
    table = lag_table().reshape(2, 2, NH, LAGS).transpose(1, 0, 2, 3).reshape(4 * NH, LAGS)
    bins = pl.BlockSpec((block, 2 * NH), lambda p: (p, 0))
    return pl.pallas_call(
        lags_kernel,
        grid=(pairs // block,),
        in_specs=[
            pl.BlockSpec(memory_space=pltpu.SMEM),
            pl.BlockSpec(memory_space=pltpu.SMEM),
            ids_spec(block),
            once(rows.shape),
            pl.BlockSpec((segments, block, 2 * NH), lambda p: (0, p, 0)),
            bins,
            bins,
            whole(table.shape),
        ],
        out_specs=pl.BlockSpec((block, LAGS), lambda p: (p, 0)),
        out_shape=jax.ShapeDtypeStruct((pairs, LAGS), F32),
        compiler_params=params(TAIL),
    )(segment, count, ids.reshape(-1, block // 128, 128), rows, receiver, own, low, table)


def on_device(strain, taps, send_rows, pair_source, pair_receiver, pair_count):
    n_tm, n_sub = lax.axis_size("tm"), lax.axis_size("sub")
    my_tm, my_half = lax.axis_index("tm"), lax.axis_index("half")
    capacity = send_rows.shape[3]
    width = strain.shape[1]
    split = [512, width - 512] if width % 256 == 0 and width > 512 else [width]
    order = (my_tm - jnp.arange(n_tm, dtype=jnp.int32)) % n_tm

    def shifted(array, by):
        return lax.ppermute(array, "tm", [(i, (i + by) % n_tm) for i in range(n_tm)])

    def across(array, by=0):
        pairs = [(2 * i + h, (i + by) % n_tm * 2 + 1 - h) for i in range(n_tm) for h in range(2)]
        return lax.ppermute(array, ("tm", "half"), pairs)

    def exchange(array):
        return lax.all_to_all(array, ("tm", "sub"), 0, 0, tiled=True)

    def by_segment(array):
        return array.reshape(n_tm, -1, array.shape[2])

    asked = send_rows[0].reshape(n_tm, 2, -1).transpose(1, 0, 2).reshape(1, 2, -1, 128)
    asked = jnp.broadcast_to(asked, (n_tm,) + asked.shape[1:]).reshape((2 * n_tm,) + asked.shape[2:])
    first, last, fix = edges(strain, taps)
    before = lax.ppermute(last, "tm", [(i, i + 1) for i in range(n_tm - 1)])
    after = lax.ppermute(first, "tm", [(i + 1, i) for i in range(n_tm - 1)])
    asked, first, last = lax.optimization_barrier((asked, first, last))
    asked = lax.all_to_all(asked, ("tm", "half"), 0, 0, tiled=True)
    asked = asked.reshape(n_tm, 2, -1, 128)

    dec = decimate(strain, taps)
    place = jnp.stack([my_tm, jnp.int32(n_tm)]).astype(jnp.int32)
    starts = [sum(split[:p]) for p in range(len(split))]
    parts = [whiten(place, dec, first, last, before, after, fix, *part) for part in zip(starts, split)]
    low, high = [list(half) for half in zip(*parts)]

    low_across = [across(part) for part in low]
    high_across = [across(part) for part in high[::-1]][::-1]

    low, high = jnp.concatenate(low, axis=0), jnp.concatenate(high, axis=0)
    asked_own = lax.dynamic_index_in_dim(asked, my_half, 1, keepdims=False)
    outgoing = pick(asked_own, [low, high], capacity)
    outgoing, low_across[0] = lax.optimization_barrier((outgoing, low_across[0]))
    own = exchange(outgoing)
    receivers = []
    for a in range(n_tm):
        at = (my_tm + a) % n_tm * (width // n_tm)
        rows = [lax.dynamic_slice_in_dim(half, at, width // n_tm, 0) for half in (low, high)]
        rows = jnp.concatenate(rows, axis=1)
        receivers.append(shifted(rows, a) if a else rows)

    asked_other = lax.dynamic_index_in_dim(asked, 1 - my_half, 1, keepdims=False)

    sender, column = pair_source[0] // capacity, pair_source[0] % capacity
    group, chan = sender // (2 * n_sub), sender % (2 * n_sub)
    slot = (chan % n_sub * n_tm + group) * capacity + column
    slot += jnp.where(chan // n_sub == my_half, 0, n_sub * n_tm * capacity)

    outgoing = pick(asked_other, [jnp.concatenate(low_across, axis=0)], capacity)
    outgoing, own, high_across[-1], *receivers = lax.optimization_barrier(
        (outgoing, own, high_across[-1], *receivers)
    )
    others = exchange(outgoing)
    receiver = receive(pair_receiver[0], receivers)
    bins = cross_own(order, slot, by_segment(own), *receiver)
    *bins, high_across[0] = lax.optimization_barrier((*bins, high_across[0]))
    outgoing = pick(asked_other, [jnp.concatenate(high_across, axis=0)], capacity)
    outgoing, others = lax.optimization_barrier((outgoing, others))
    bins[0] = cross_mirrored(order, slot, by_segment(others), receiver[0], bins[0])
    others = exchange(outgoing)
    return lags(order, pair_count, slot, by_segment(others), receiver[1], bins[1], bins[0])[None]


def solution(mesh):
    n_tm, n_chan = mesh.devices.shape
    split = Mesh(mesh.devices.reshape(n_tm, 2, n_chan // 2), ("tm", "half", "sub"))
    device = ("tm", "half", "sub")
    return jax.shard_map(
        on_device,
        mesh=split,
        in_specs=(
            P("tm", ("half", "sub")),
            P(),
            P(device, None, None, None),
            P(device, None),
            P(device, None),
            P(device),
        ),
        out_specs=P(device, None, None),
        check_vma=False,
    )
```

time: 168 us -> 152 us (0.905)
  waiting for transfers between devices: 54.2 us -> 42.5 us
  local copies, waits for them, and re-layouts: 11.5 us -> 7.76 us
  Pallas kernels: 61.4 us -> 58.6 us
    ppermute x6, waiting for transfers between devices: 48.4 us -> 30.2 us  [the longest x4 30.2 us: across(): return lax.ppermute(array, ('tm', 'half'), pairs)]
    all_to_all x3, waiting for transfers between devices: 2.01 us -> 10.7 us  [exchange(): return lax.all_to_all(array, ('tm', 'sub'), 0, 0, tiled=True)]
    another operation x4 -> x1, local copies, waits for them, and re-layouts: 5.55 us -> 0.08 us  [on_device(): send_rows[0].reshape(n_tm, 2, -1).transpose(1, 0, 2).reshape(1, 2, -1, 128)]
    pallas_call x9 -> x11, Pallas kernels: 61.4 us -> 58.6 us  [the longest x1 9.42 us: cross_own(): pl.pallas_call(own_kernel, grid=(pairs // block,), in_specs=[pl.BlockSpec...]
    unnamed x32 -> x53, local copies, waits for them, and re-layouts: 4.04 us -> 6.28 us
    ppermute x3, waiting for transfers between devices: 3.75 us -> 1.53 us  [shifted(): lax.ppermute(array, 'tm', [(i, (i + by) % n_tm) for i in range(n_tm)])]
  transfers between devices with their start and end apart: 13 -> 13, of which waited for: 6 -> 7; matrix products, arithmetic and copies ran while one was open for 6% -> 3% of each run, Pallas kernels for 18% -> 30%
where the time goes in v2:
time: 152 us; the launch traced here: 151 us
  Pallas kernels  58.6 us (39%)
  waiting for transfers between devices  42.5 us (28%)
  starting transfers between devices  38.2 us (25%)
  local copies, waits for them, and re-layouts  7.76 us (5%)
  other arithmetic  3.18 us (2%)
    ppermute x4, waiting for transfers between devices, across(): return lax.ppermute(array, ('tm', 'half'), pairs)  30.2 us
    all_to_all x3, starting transfers between devices, exchange(): return lax.all_to_all(array, ('tm', 'sub'), 0, 0, tiled=True)  15.1 us
    all_to_all x3, waiting for transfers between devices, exchange(): return lax.all_to_all(array, ('tm', 'sub'), 0, 0, tiled=True)  10.7 us
    pallas_call x1, Pallas kernels, cross_own(): pl.pallas_call(own_kernel, grid=(pairs // block,), in_specs=[pl.BlockSpec...  9.42 us
    pallas_call x2, Pallas kernels, whiten(): pl.pallas_call(whiten_kernel, grid=(held // chunk,), in_specs=[pl.BlockSp...  8.28 us
    pallas_call x3, Pallas kernels, pick(): pl.pallas_call(pick_kernel, grid=(steps,), in_specs=[pl.BlockSpec((1, row...  8.1 us
    pallas_call x1, Pallas kernels, receive(): pl.pallas_call(receive_kernel, grid=(pairs // block,), in_specs=[ids_spec...  7.97 us
    pallas_call x1, Pallas kernels, lags(): pl.pallas_call(lags_kernel, grid=(pairs // block,), in_specs=[pl.BlockSpe...  7.94 us
  transfers between devices with their start and end apart: 13, of which 7 were waited for; matrix products, arithmetic and copies ran while one was open for 3% of the time, Pallas kernels for 30%

profile of v2, /device:TPU:0, one launch (start us, length us, event | category | flops | bytes accessed | tf_op | source)
XLA Modules:
  0.0 151.4 jit_solution(17834101275501145227)
XLA Ops:
  0.0 0.7 copy-done.16
  0.7 2.5 %shard_map.145 = (bf16[128,1280]{1,0:T(8,128)(2,1)S(1)}, bf16[128,1280]{1,0:T(8,128)(2,1)S(1)}, bf16[32,128]{1,0:T(8,128)(2,1)S(1)}) custom-call(f32[40]{0:T(128)S(1)} %copy-done.16, bf16[5120,1280]{1,0:T(8,128)(2,1)} %x_ref.3), custom_call_target="tpu_custom_call" | custom-call | tf_op jit(solution)/shard_map/pallas_call | solution.py:112
  3.2 4.9 %collective-permute-start = (bf16[128,1280]{1,0:T(8,128)(2,1)S(1)}, bf16[128,1280]{1,0:T(8,128)(2,1)S(1)}, u32[]{:S(2)}, u32[]{:S(2)}) collective-permute-start(bf16[128,1280]{1,0:T(8,128)(2,1)S(1)} %get-tuple-element.37.last_ref), channel_id=1, source_target_pairs={{0,8},{8,16},{16,24},{1,9},{9,17},{17,25},{2,10},{10,18},{18,26},{... | collective-permute-start | bytes 983048 | tf_op jit(solution)/shard_map/ppermute | solution.py:448
  8.1 1.3 collective-permute-start.1
  10.1 6.9 %all-to-all-start = ((s32[8,4,128]{2,1,0:T(4,128)}), s32[8,4,128]{2,1,0:T(4,128)S(1)}, u32[]{:S(2)}, u32[]{:S(2)}) async-start(s32[8,4,128]{2,1,0:T(4,128)} %bitcast.2), calls=%async_computation | async-start | bytes 32768 | tf_op jit(solution)/shard_map/all_to_all | solution.py:451
  17.1 7.8 %shard_map.146.dec_ref = bf16[1024,1280]{1,0:T(8,128)(2,1)} custom-call(f32[40]{0:T(128)S(1)} %copy-done.17, bf16[5120,1280]{1,0:T(8,128)(2,1)} %x_ref.3), custom_call_target="tpu_custom_call" | custom-call | tf_op jit(solution)/shard_map/pallas_call | solution.py:159
  25.6 1.9 %copy-done = bf16[1024,1280]{1,0:T(8,128)(2,1)S(1)} copy-done((bf16[1024,1280]{1,0:T(8,128)(2,1)S(1)}, bf16[1024,1280]{1,0:T(8,128)(2,1)}, u32[]{:S(2)}) %copy-start) | copy-done | bytes 2621464
  27.5 3.4 %shard_map.147 = (bf16[512,256]{1,0:T(8,128)(2,1)S(1)}, bf16[512,256]{1,0:T(8,128)(2,1)S(1)}) custom-call(s32[2]{0:T(128)S(1)} %pad_add_fusion.place_ref, bf16[1024,1280]{1,0:T(8,128)(2,1)S(1)} %copy-done, bf16[128,1280]{1,0:T(8,128)(2,1)S(1)} %get-tuple-element.36.first_ref, bf16[128,1280]{1,0:T(8,128)(2,1)S(1)} %get-tuple-element.37.last_ref, ...), custom_call_target="tpu_custom_call" | custom-call | tf_op jit(solution)/shard_map/pallas_call | solution.py:230
  31.0 3.0 %collective-permute-start.2 = (bf16[512,256]{1,0:T(8,128)(2,1)S(1)}, bf16[512,256]{1,0:T(8,128)(2,1)}, u32[]{:S(2)}, u32[]{:S(2)}) collective-permute-start(bf16[512,256]{1,0:T(8,128)(2,1)S(1)} %get-tuple-element.39), channel_id=1, source_target_pairs={{0,4},{4,0},{8,12},{12,8},{16,20},{20,16},{24,28},{28,24},{1,5},{5... | collective-permute-start | bytes 786440 | tf_op jit(solution)/shard_map/ppermute | solution.py:437
  34.1 1.0 copy-done.3
  35.0 1.0 copy-done.5
  36.0 4.9 %shard_map.148 = (bf16[768,256]{1,0:T(8,128)(2,1)S(1)}, bf16[768,256]{1,0:T(8,128)(2,1)S(1)}) custom-call(s32[2]{0:T(128)S(1)} %pad_add_fusion.place_ref, bf16[1024,1280]{1,0:T(8,128)(2,1)S(1)} %copy-done, bf16[128,1280]{1,0:T(8,128)(2,1)S(1)} %get-tuple-element.36.first_ref, bf16[128,1280]{1,0:T(8,128)(2,1)S(1)} %get-tuple-element.37.last_ref, ...), custom_call_target="tpu_custom_call" | custom-call | tf_op jit(solution)/shard_map/pallas_call | solution.py:230
  41.6 3.1 %shard_map.149 = bf16[16,128,512]{2,1,0:T(8,128)(2,1)} custom-call(s32[4,4,128]{2,1,0:T(4,128)S(1)} %bitcast.20, bf16[1280,256]{1,0:T(8,128)(2,1)S(1)} %constant_dynamic-update-slice_fusion.refs_0_, bf16[1280,256]{1,0:T(8,128)(2,1)S(1)} %constant_dynamic-update-slice_fusion.2.refs_1_), custom_call_target="tpu_custom_call" | custom-call | tf_op jit(solution)/shard_map/pallas_call | solution.py:283
  44.9 4.8 %all-to-all-start.1 = ((bf16[16,128,512]{2,1,0:T(8,128)(2,1)}), bf16[16,128,512]{2,1,0:T(8,128)(2,1)}, u32[]{:S(2)}, u32[]{:S(2)}) async-start(bf16[16,128,512]{2,1,0:T(8,128)(2,1)} %shard_map.149), calls=%async_computation.1 | async-start | bytes 4194304 | tf_op jit(solution)/shard_map/all_to_all | solution.py:440
  49.8 2.8 %collective-permute-start.3 = (bf16[768,256]{1,0:T(8,128)(2,1)S(1)}, bf16[768,256]{1,0:T(8,128)(2,1)S(1)}, u32[]{:S(2)}, u32[]{:S(2)}) collective-permute-start(bf16[768,256]{1,0:T(8,128)(2,1)S(1)} %copy-done.12), channel_id=1, source_target_pairs={{0,4},{4,0},{8,12},{12,8},{16,20},{20,16},{24,28},{28,24},{1,5},{5... | collective-permute-start | bytes 1179656 | tf_op jit(solution)/shard_map/ppermute | solution.py:437
  52.9 2.8 %collective-permute-start.7 = (bf16[320,512]{1,0:T(8,128)(2,1)S(1)}, bf16[320,512]{1,0:T(8,128)(2,1)S(1)}, u32[]{:S(2)}, u32[]{:S(2)}) collective-permute-start(bf16[320,512]{1,0:T(8,128)(2,1)S(1)} %pad_maximum_fusion.5), channel_id=1, source_target_pairs={{0,24},{8,0},{16,8},{24,16},{1,25},{9,1},{17,9},{25,17},{2,26},{10... | collective-permute-start | bytes 983048 | tf_op jit(solution)/shard_map/ppermute | solution.py:433
  57.0 0.8 pad_maximum_fusion.2.refs_0_
  57.7 26.9 %collective-permute-done.3 = bf16[768,256]{1,0:T(8,128)(2,1)S(1)} collective-permute-done((bf16[768,256]{1,0:T(8,128)(2,1)S(1)}, bf16[768,256]{1,0:T(8,128)(2,1)S(1)}, u32[]{:S(2)}, u32[]{:S(2)}) %collective-permute-start.3) | collective-permute-done | bytes 393248 | tf_op jit(solution)/shard_map/ppermute | solution.py:437
  84.6 1.0 pad_maximum_fusion.refs_0_
  85.7 2.5 %shard_map.150 = bf16[16,128,256]{2,1,0:T(8,128)(2,1)} custom-call(s32[4,4,128]{2,1,0:T(4,128)S(1)} %bitcast.18, bf16[1280,256]{1,0:T(8,128)(2,1)S(1)} %pad_maximum_fusion.refs_0_), custom_call_target="tpu_custom_call" | custom-call | tf_op jit(solution)/shard_map/pallas_call | solution.py:283
  88.2 1.5 %collective-permute-done.5.refs_1_ = bf16[320,512]{1,0:T(8,128)(2,1)S(1)} collective-permute-done((bf16[320,512]{1,0:T(8,128)(2,1)S(1)}, bf16[320,512]{1,0:T(8,128)(2,1)S(1)}, u32[]{:S(2)}, u32[]{:S(2)}) %collective-permute-start.5) | collective-permute-done | bytes 327712 | tf_op jit(solution)/shard_map/ppermute | solution.py:433
  89.7 3.1 %collective-permute-done.4 = bf16[768,256]{1,0:T(8,128)(2,1)S(1)} collective-permute-done((bf16[768,256]{1,0:T(8,128)(2,1)S(1)}, bf16[768,256]{1,0:T(8,128)(2,1)S(1)}, u32[]{:S(2)}, u32[]{:S(2)}) %collective-permute-start.4) | collective-permute-done | bytes 393248 | tf_op jit(solution)/shard_map/ppermute | solution.py:437
  92.9 1.3 all-to-all-done.1
  94.2 5.7 %all-to-all-start.2 = ((bf16[16,128,256]{2,1,0:T(8,128)(2,1)}), bf16[16,128,256]{2,1,0:T(8,128)(2,1)S(1)}, u32[]{:S(2)}, u32[]{:S(2)}) async-start(bf16[16,128,256]{2,1,0:T(8,128)(2,1)} %shard_map.150), calls=%async_computation.2 | async-start | bytes 2097152 | tf_op jit(solution)/shard_map/all_to_all | solution.py:440
  101.3 8.0 %shard_map.151 = (bf16[4,2048,256]{2,1,0:T(8,128)(2,1)}, bf16[4,2048,256]{2,1,0:T(8,128)(2,1)}) custom-call(s32[4,4,128]{2,1,0:T(4,128)} %bitcast.25, bf16[320,512]{1,0:T(8,128)(2,1)} %pad_maximum_fusion.2.refs_0_, bf16[320,512]{1,0:T(8,128)(2,1)} %copy-done.22, bf16[320,512]{1,0:T(8,128)(2,1)} %copy-done.21, bf16[320,512]{1,0:T(8,128)(2,1)} %copy-done.20), custom_call_target="tpu_custom_call" | custom-call | tf_op jit(solution)/shard_map/pallas_call | solution.py:318
  109.3 9.4 %shard_map.152 = (bf16[2048,256]{1,0:T(8,128)(2,1)}, bf16[2048,256]{1,0:T(8,128)(2,1)}) custom-call(s32[4]{0:T(128)} %and_select_fusion.segment_ref, s32[4,4,128]{2,1,0:T(4,128)} %fusion.4.ids_ref, bf16[4,512,512]{2,1,0:T(8,128)(2,1)} %bitcast.7.own_ref, bf16[4,2048,256]{2,1,0:T(8,128)(2,1)} %get-tuple-element.50.low_ref.receiver_ref, ...), custom_call_target="tpu_custom_call" | custom-call | tf_op jit(solution)/shard_map/pallas_call | solution.py:352
  118.7 2.5 %shard_map.153 = bf16[16,128,256]{2,1,0:T(8,128)(2,1)} custom-call(s32[4,4,128]{2,1,0:T(4,128)S(1)} %bitcast.19, bf16[1280,256]{1,0:T(8,128)(2,1)S(1)} %pad_maximum_fusion.1.refs_0_), custom_call_target="tpu_custom_call" | custom-call | tf_op jit(solution)/shard_map/pallas_call | solution.py:283
  121.7 4.6 %all-to-all-start.3 = ((bf16[16,128,256]{2,1,0:T(8,128)(2,1)}), bf16[16,128,256]{2,1,0:T(8,128)(2,1)S(1)}, u32[]{:S(2)}, u32[]{:S(2)}) async-start(bf16[16,128,256]{2,1,0:T(8,128)(2,1)} %shard_map.153), calls=%async_computation.3 | async-start | bytes 2097152 | tf_op jit(solution)/shard_map/all_to_all | solution.py:440
  127.0 6.6 %shard_map.154.low_ref = bf16[2048,256]{1,0:T(8,128)(2,1)} custom-call(s32[4]{0:T(128)} %and_select_fusion.segment_ref, s32[4,4,128]{2,1,0:T(4,128)} %fusion.4.ids_ref, bf16[4,512,256]{2,1,0:T(8,128)(2,1)} %bitcast.22, bf16[4,2048,256]{2,1,0:T(8,128)(2,1)} %get-tuple-element.50.low_ref.receiver_ref, bf16[2048,256]{1,0:T(8,128)(2,1)} %get-tuple-element.60.own_ref), custom_call_target="tpu_custom_call" | custom-call | tf_op jit(solution)/shard_map/pallas_call | solution.py:372
  133.6 8.9 %all-to-all-done.3 = bf16[16,128,256]{2,1,0:T(8,128)(2,1)S(1)} async-done(((bf16[16,128,256]{2,1,0:T(8,128)(2,1)}), bf16[16,128,256]{2,1,0:T(8,128)(2,1)S(1)}, u32[]{:S(2)}, u32[]{:S(2)}) %all-to-all-start.3) | async-done | bytes 1048608 | tf_op jit(solution)/shard_map/all_to_all | solution.py:440
  142.5 1.0 copy-done.18
  143.5 7.9 %shard_map.155 = f32[2048,256]{1,0:T(8,128)} custom-call(s32[4]{0:T(128)} %and_select_fusion.segment_ref, s32[1]{0:T(128)S(6)} %copy.29.count_ref, s32[4,4,128]{2,1,0:T(4,128)} %fusion.4.ids_ref, bf16[4,512,256]{2,1,0:T(8,128)(2,1)} %bitcast.21, bf16[4,2048,256]{2,1,0:T(8,128)(2,1)} %get-tuple-element.51.high_ref.receiver_ref, ...), custom_call_target="tpu_custom_call" | custom-call | tf_op jit(solution)/shard_map/pallas_call | solution.py:405
  (78 shorter events, 6.0 us)
Async XLA Ops:
  0.7 8.7 %copy-start.24 = (s32[1,4,8,32]{3,2,1,0:T(8,128)S(1)}, s32[1,4,8,32]{3,2,1,0:T(8,128)}, u32[]{:S(2)}) copy-start(s32[1,4,8,32]{3,2,1,0:T(8,128)} %param.17) | copy-start | bytes 12292
  0.7 16.4 %copy-start.17 = (f32[40]{0:T(128)S(1)}, f32[40]{0:T(128)}, u32[]{:S(2)}) copy-start(f32[40]{0:T(128)} %taps_ref.3) | copy-start | bytes 484
  3.2 22.4 %collective-permute-start = (bf16[128,1280]{1,0:T(8,128)(2,1)S(1)}, bf16[128,1280]{1,0:T(8,128)(2,1)S(1)}, u32[]{:S(2)}, u32[]{:S(2)}) collective-permute-start(bf16[128,1280]{1,0:T(8,128)(2,1)S(1)} %get-tuple-element.37.last_ref), channel_id=1, source_target_pairs={{0,8},{8,16},{16,24},{1,9},{9,17},{17,25},{2,10},{10,18},{18,26},{... | collective-permute-start | bytes 983048 | tf_op jit(solution)/shard_map/ppermute | solution.py:448
  8.1 17.5 %collective-permute-start.1 = (bf16[128,1280]{1,0:T(8,128)(2,1)S(1)}, bf16[128,1280]{1,0:T(8,128)(2,1)S(1)}, u32[]{:S(2)}, u32[]{:S(2)}) collective-permute-start(bf16[128,1280]{1,0:T(8,128)(2,1)S(1)} %get-tuple-element.36.first_ref), channel_id=1, source_target_pairs={{8,0},{16,8},{24,16},{9,1},{17,9},{25,17},{10,2},{18,10},{26,18},{... | collective-permute-start | bytes 983048 | tf_op jit(solution)/shard_map/ppermute | solution.py:449
  10.1 14.8 %all-to-all-start = ((s32[8,4,128]{2,1,0:T(4,128)}), s32[8,4,128]{2,1,0:T(4,128)S(1)}, u32[]{:S(2)}, u32[]{:S(2)}) async-start(s32[8,4,128]{2,1,0:T(4,128)} %bitcast.2), calls=%async_computation | async-start | bytes 32768 | tf_op jit(solution)/shard_map/all_to_all | solution.py:451
  17.0 8.5 %copy-start.1 = (bf16[640,1024]{1,0:T(8,128)(2,1)S(1)}, bf16[640,1024]{1,0:T(8,128)(2,1)}, u32[]{:S(2)}) copy-start(bf16[640,1024]{1,0:T(8,128)(2,1)} %constant.135.clone.table_ref) | copy-start | bytes 3932164
  17.0 8.5 %copy-start.6 = (bf16[256,320]{1,0:T(8,128)(2,1)S(1)}, bf16[256,320]{1,0:T(8,128)(2,1)}, u32[]{:S(2)}) copy-start(bf16[256,320]{1,0:T(8,128)(2,1)} %constant.136.clone.smooth_ref) | copy-start | bytes 491524
  17.0 8.5 %copy-start.7 = (f32[256,1]{1,0:T(8,128)S(1)}, f32[256,1]{1,0:T(8,128)}, u32[]{:S(2)}) copy-start(f32[256,1]{1,0:T(8,128)} %constant.137.clone.taper_ref) | copy-start | bytes 3076
  17.1 8.6 %copy-start.13 = (bf16[128,256]{1,0:T(8,128)(2,1)S(1)}, bf16[128,256]{1,0:T(8,128)(2,1)}, u32[]{:S(2)}) copy-start(bf16[128,256]{1,0:T(8,128)(2,1)} %constant.134.clone.ones_ref) | copy-start | bytes 196612
  25.5 5.4 %copy-start.2 = (bf16[128,1280]{1,0:T(8,128)(2,1)}, bf16[128,1280]{1,0:T(8,128)(2,1)S(1)}, u32[]{:S(2)}) copy-start(bf16[128,1280]{1,0:T(8,128)(2,1)S(1)} %collective-permute-done.before_ref) | copy-start | bytes 983044
  25.6 5.4 %copy-start.4 = (bf16[128,1280]{1,0:T(8,128)(2,1)}, bf16[128,1280]{1,0:T(8,128)(2,1)S(1)}, u32[]{:S(2)}) copy-start(bf16[128,1280]{1,0:T(8,128)(2,1)S(1)} %collective-permute-done.1.after_ref) | copy-start | bytes 983044
  27.5 6.5 %copy-start.8 = (f32[256,1]{1,0:T(8,128)S(1)}, f32[256,1]{1,0:T(8,128)}, u32[]{:S(2)}) copy-start(f32[256,1]{1,0:T(8,128)} %constant.137.clone.taper_ref) | copy-start | bytes 3076
  31.0 13.9 %collective-permute-start.2 = (bf16[512,256]{1,0:T(8,128)(2,1)S(1)}, bf16[512,256]{1,0:T(8,128)(2,1)}, u32[]{:S(2)}, u32[]{:S(2)}) collective-permute-start(bf16[512,256]{1,0:T(8,128)(2,1)S(1)} %get-tuple-element.39), channel_id=1, source_target_pairs={{0,4},{4,0},{8,12},{12,8},{16,20},{20,16},{24,28},{28,24},{1,5},{5... | collective-permute-start | bytes 786440 | tf_op jit(solution)/shard_map/ppermute | solution.py:437
  40.9 3.8 %copy-start.11 = (bf16[768,256]{1,0:T(8,128)(2,1)}, bf16[768,256]{1,0:T(8,128)(2,1)S(1)}, u32[]{:S(2)}) copy-start(bf16[768,256]{1,0:T(8,128)(2,1)S(1)} %get-tuple-element.40) | copy-start | bytes 1179652
  44.7 5.0 %copy-start.23 = (s32[4,1,4,128]{3,1,0,2:T(1,128)S(1)}, s32[4,1,4,128]{3,1,0,2:T(1,128)}, u32[]{:S(2)}) copy-start(s32[4,1,4,128]{3,1,0,2:T(1,128)} %get-tuple-element.70) | copy-start | bytes 24580
  44.7 7.9 %copy-start.10 = (bf16[768,256]{1,0:T(8,128)(2,1)S(1)}, bf16[768,256]{1,0:T(8,128)(2,1)}, u32[]{:S(2)}) copy-start(bf16[768,256]{1,0:T(8,128)(2,1)} %copy-done.9) | copy-start | bytes 1179652
  44.9 4.9 %copy-start.12 = (bf16[768,256]{1,0:T(8,128)(2,1)S(1)}, bf16[768,256]{1,0:T(8,128)(2,1)}, u32[]{:S(2)}) copy-start(bf16[768,256]{1,0:T(8,128)(2,1)} %copy-done.11) | copy-start | bytes 1179652
  44.9 49.3 %all-to-all-start.1 = ((bf16[16,128,512]{2,1,0:T(8,128)(2,1)}), bf16[16,128,512]{2,1,0:T(8,128)(2,1)}, u32[]{:S(2)}, u32[]{:S(2)}) async-start(bf16[16,128,512]{2,1,0:T(8,128)(2,1)} %shard_map.149), calls=%async_computation.1 | async-start | bytes 4194304 | tf_op jit(solution)/shard_map/all_to_all | solution.py:440
  49.8 34.9 %collective-permute-start.3 = (bf16[768,256]{1,0:T(8,128)(2,1)S(1)}, bf16[768,256]{1,0:T(8,128)(2,1)S(1)}, u32[]{:S(2)}, u32[]{:S(2)}) collective-permute-start(bf16[768,256]{1,0:T(8,128)(2,1)S(1)} %copy-done.12), channel_id=1, source_target_pairs={{0,4},{4,0},{8,12},{12,8},{16,20},{20,16},{24,28},{28,24},{1,5},{5... | collective-permute-start | bytes 1179656 | tf_op jit(solution)/shard_map/ppermute | solution.py:437
  52.5 40.3 %collective-permute-start.4 = (bf16[768,256]{1,0:T(8,128)(2,1)S(1)}, bf16[768,256]{1,0:T(8,128)(2,1)S(1)}, u32[]{:S(2)}, u32[]{:S(2)}) collective-permute-start(bf16[768,256]{1,0:T(8,128)(2,1)S(1)} %copy-done.10), channel_id=1, source_target_pairs={{0,4},{4,0},{8,12},{12,8},{16,20},{20,16},{24,28},{28,24},{1,5},{5... | collective-permute-start | bytes 1179656 | tf_op jit(solution)/shard_map/ppermute | solution.py:437
  52.9 35.3 %collective-permute-start.7 = (bf16[320,512]{1,0:T(8,128)(2,1)S(1)}, bf16[320,512]{1,0:T(8,128)(2,1)S(1)}, u32[]{:S(2)}, u32[]{:S(2)}) collective-permute-start(bf16[320,512]{1,0:T(8,128)(2,1)S(1)} %pad_maximum_fusion.5), channel_id=1, source_target_pairs={{0,24},{8,0},{16,8},{24,16},{1,25},{9,1},{17,9},{25,17},{2,26},{10... | collective-permute-start | bytes 983048 | tf_op jit(solution)/shard_map/ppermute | solution.py:433
  55.7 32.5 %collective-permute-start.6 = (bf16[320,512]{1,0:T(8,128)(2,1)S(1)}, bf16[320,512]{1,0:T(8,128)(2,1)S(1)}, u32[]{:S(2)}, u32[]{:S(2)}) collective-permute-start(bf16[320,512]{1,0:T(8,128)(2,1)S(1)} %pad_maximum_fusion.4), channel_id=1, source_target_pairs={{0,16},{8,24},{16,0},{24,8},{1,17},{9,25},{17,1},{25,9},{2,18},{10... | collective-permute-start | bytes 983048 | tf_op jit(solution)/shard_map/ppermute | solution.py:433
  56.3 33.4 %collective-permute-start.5 = (bf16[320,512]{1,0:T(8,128)(2,1)S(1)}, bf16[320,512]{1,0:T(8,128)(2,1)S(1)}, u32[]{:S(2)}, u32[]{:S(2)}) collective-permute-start(bf16[320,512]{1,0:T(8,128)(2,1)S(1)} %pad_maximum_fusion.3), channel_id=1, source_target_pairs={{0,8},{8,16},{16,24},{24,0},{1,9},{9,17},{17,25},{25,1},{2,10},{10... | collective-permute-start | bytes 983048 | tf_op jit(solution)/shard_map/ppermute | solution.py:433
  85.6 14.3 %copy-start.15 = (bf16[512,256]{1,0:T(8,128)(2,1)S(1)}, bf16[512,256]{1,0:T(8,128)(2,1)}, u32[]{:S(2)}) copy-start(bf16[512,256]{1,0:T(8,128)(2,1)} %copy-done.14) | copy-start | bytes 786436
  85.6 15.0 %copy-start.25 = (s32[1,2048]{1,0:T(1,128)S(1)}, s32[1,2048]{1,0:T(1,128)}, u32[]{:S(2)}) copy-start(s32[1,2048]{1,0:T(1,128)} %param.18) | copy-start | bytes 24580
  88.2 13.1 %copy-start.20 = (bf16[320,512]{1,0:T(8,128)(2,1)}, bf16[320,512]{1,0:T(8,128)(2,1)S(1)}, u32[]{:S(2)}) copy-start(bf16[320,512]{1,0:T(8,128)(2,1)S(1)} %collective-permute-done.7.refs_3_) | copy-start | bytes 983044
  88.2 13.1 %copy-start.21 = (bf16[320,512]{1,0:T(8,128)(2,1)}, bf16[320,512]{1,0:T(8,128)(2,1)S(1)}, u32[]{:S(2)}) copy-start(bf16[320,512]{1,0:T(8,128)(2,1)S(1)} %collective-permute-done.6.refs_2_) | copy-start | bytes 983044
  89.7 4.5 %copy-start.22 = (bf16[320,512]{1,0:T(8,128)(2,1)}, bf16[320,512]{1,0:T(8,128)(2,1)S(1)}, u32[]{:S(2)}) copy-start(bf16[320,512]{1,0:T(8,128)(2,1)S(1)} %collective-permute-done.5.refs_1_) | copy-start | bytes 983044
  94.2 27.5 %all-to-all-start.2 = ((bf16[16,128,256]{2,1,0:T(8,128)(2,1)}), bf16[16,128,256]{2,1,0:T(8,128)(2,1)S(1)}, u32[]{:S(2)}, u32[]{:S(2)}) async-start(bf16[16,128,256]{2,1,0:T(8,128)(2,1)} %shard_map.150), calls=%async_computation.2 | async-start | bytes 2097152 | tf_op jit(solution)/shard_map/all_to_all | solution.py:440
  99.9 18.8 %collective-permute-start.8 = (bf16[512,256]{1,0:T(8,128)(2,1)S(1)}, bf16[512,256]{1,0:T(8,128)(2,1)S(1)}, u32[]{:S(2)}, u32[]{:S(2)}) collective-permute-start(bf16[512,256]{1,0:T(8,128)(2,1)S(1)} %copy-done.15), channel_id=1, source_target_pairs={{0,4},{4,0},{8,12},{12,8},{16,20},{20,16},{24,28},{28,24},{1,5},{5... | collective-permute-start | bytes 786440 | tf_op jit(solution)/shard_map/ppermute | solution.py:437
  121.7 5.3 %copy-start.19 = (bf16[16,128,256]{2,1,0:T(8,128)(2,1)}, bf16[16,128,256]{2,1,0:T(8,128)(2,1)S(1)}, u32[]{:S(2)}) copy-start(bf16[16,128,256]{2,1,0:T(8,128)(2,1)S(1)} %all-to-all-done.2) | copy-start | bytes 3145732
  121.7 20.8 %all-to-all-start.3 = ((bf16[16,128,256]{2,1,0:T(8,128)(2,1)}), bf16[16,128,256]{2,1,0:T(8,128)(2,1)S(1)}, u32[]{:S(2)}, u32[]{:S(2)}) async-start(bf16[16,128,256]{2,1,0:T(8,128)(2,1)} %shard_map.153), calls=%async_computation.3 | async-start | bytes 2097152 | tf_op jit(solution)/shard_map/all_to_all | solution.py:440
  (7 other events, 9.2 us)

commit v3 on v2

--- a/solution.py
+++ b/solution.py
@@ -58,6 +58,9 @@
     return ((lag >= 0) & (lag < width)).astype(BF)
 
 
+COST = (69000000000, 69000000000)
+
+
 def whole(shape):
     return pl.BlockSpec(shape, lambda *_: (0,) * len(shape))
 
@@ -179,7 +182,7 @@
 
 def whiten_kernel(
     place_ref, dec_ref, first_ref, last_ref, before_ref, after_ref, fix_ref, ones_ref, table_ref, smooth_ref,
-    taper_ref, low_ref, high_ref, size, flat
+    taper_ref, out_ref, size, flat
 ):
     length = dec_ref.shape[0]
     blocks = length // TB
@@ -210,15 +213,15 @@
     smooth = jnp.dot(smooth_ref[...], magnitude.astype(BF), preferred_element_type=F32)
     factor = taper_ref[...] * inverse(smooth * (1.0 / (2 * WF + 1)) + 1e-05)
     real, imag = real[WF : WF + NF] * factor, imag[WF : WF + NF] * factor
-    low_ref[:, :NH] = real[:NH].T.astype(BF)
-    low_ref[:, NH:] = imag[:NH].T.astype(BF)
-    high_ref[:, :NH] = real[NH:].T.astype(BF)
-    high_ref[:, NH:] = imag[NH:].T.astype(BF)
+    out_ref[:, :NH] = real[:NH].T.astype(BF)
+    out_ref[:, NH : 2 * NH] = imag[:NH].T.astype(BF)
+    out_ref[:, 2 * NH : 3 * NH] = real[NH:].T.astype(BF)
+    out_ref[:, 3 * NH :] = imag[NH:].T.astype(BF)
 
 
 def whiten(place, dec, low, high, before, after, fix, start, held):
     length, width = dec.shape
-    chunk = 256 if width % 256 == 0 else 128
+    chunk = held
     first = start // chunk
     tables = (
         ones_band(TB, TB + 2 * WT, 2 * WT + 1),
@@ -240,10 +243,10 @@
             whole(fix.shape),
         ]
         + [whole(table.shape) for table in tables],
-        out_specs=[pl.BlockSpec((chunk, 2 * NH), lambda c: (c, 0))] * 2,
-        out_shape=[jax.ShapeDtypeStruct((held, 2 * NH), BF)] * 2,
+        out_specs=pl.BlockSpec((chunk, 4 * NH), lambda c: (c, 0)),
+        out_shape=jax.ShapeDtypeStruct((held, 4 * NH), BF),
         scratch_shapes=[pltpu.VMEM((length + 2 * WT, chunk), BF), pltpu.VMEM((length, chunk), BF)],
-        compiler_params=params(PART),
+        compiler_params=params(VMEM),
     )(place, dec, low, high, before, after, fix, *tables)
 
 
@@ -258,37 +261,43 @@
     return jnp.concatenate(parts, axis=0)
 
 
-def pick_kernel(ids_ref, *refs):
-    *halves, out_ref = refs
-    owners, rows, _ = out_ref.shape
-    hot = one_hot(ids_ref[0], halves[0].shape[0])
-    for h, half in enumerate(halves):
-        picked = jnp.dot(hot, half[...], preferred_element_type=F32).astype(BF)
-        out_ref[:, :, 2 * NH * h : 2 * NH * (h + 1)] = picked.reshape(owners, rows, 2 * NH)
-
-
-def pick(ids, halves, capacity):
-    groups = ids.shape[0]
-    owners = ids.size // groups // capacity
-    width = 2 * NH * len(halves)
+def pick_kernel(ids_ref, rows_ref, *refs):
+    out_ref = refs[-1]
+    owners, rows, width = out_ref.shape
+    hot = one_hot(ids_ref[0], rows_ref.shape[0])
+    for lane in range(0, width, 2 * NH):
+        picked = jnp.dot(hot, rows_ref[:, lane : lane + 2 * NH], preferred_element_type=F32).astype(BF)
+        out_ref[:, :, lane : lane + 2 * NH] = picked.reshape(owners, rows, 2 * NH)
+
+
+def pick(ids, spectra, capacity, part, parts, filled, cost=None):
+    groups = ids.shape[0] // parts
+    owners = ids.size // ids.shape[0] // capacity
+    width = spectra.shape[1]
     join = 1
     while join * capacity % 16 != 0:
         join *= 2
     steps = groups // join
-    held = halves[0].shape[0] // steps
+    held = spectra.shape[0] // steps
     rows = owners * join * capacity
+    ids = ids[part * groups : (part + 1) * groups]
     if join > 1:
         ids = ids.reshape(steps, join, owners, capacity).transpose(0, 2, 1, 3)
         ids = ids + (jnp.arange(join, dtype=jnp.int32) * (held // join))[None, None, :, None]
     return pl.pallas_call(
         pick_kernel,
         grid=(steps,),
-        in_specs=[pl.BlockSpec((1, rows // 128, 128), lambda g: (g, 0, 0))]
-        + [pl.BlockSpec((held, 2 * NH), lambda g: (g, 0)) for _ in halves],
-        out_specs=pl.BlockSpec((owners, join * capacity, width), lambda g: (0, g, 0)),
-        out_shape=jax.ShapeDtypeStruct((owners, groups * capacity, width), BF),
+        in_specs=[
+            pl.BlockSpec((1, rows // 128, 128), lambda g: (g, 0, 0)),
+            pl.BlockSpec((held, width), lambda g: (g, 0)),
+        ]
+        + [pl.BlockSpec(memory_space=pl.ANY) for _ in filled],
+        out_specs=pl.BlockSpec((owners, join * capacity, width), lambda g: (0, part * steps + g, 0)),
+        out_shape=jax.ShapeDtypeStruct((owners, parts * groups * capacity, width), BF),
+        input_output_aliases={2: 0} if filled else {},
         compiler_params=params(PART),
-    )(ids.reshape(steps, rows // 128, 128), *halves)
+        cost_estimate=cost,
+    )(ids.reshape(steps, rows // 128, 128), spectra, *filled)
 
 
 def pair_block(pairs, segments):
@@ -359,66 +368,37 @@
     )(segment, ids.reshape(-1, block // 128, 128), own, low, high)
 
 
-def mirrored_kernel(segment_ref, ids_ref, rows_ref, receiver_ref, own_ref, out_ref):
-    held = rows_ref.shape[1]
-    hot = one_hot(ids_ref[0] - held, held)
-    out_ref[...] = own_ref[...] + cross(hot, segment_ref, rows_ref, slice(None), receiver_ref)
-
-
-def cross_mirrored(segment, ids, rows, receiver, own):
-    segments, pairs, _ = receiver.shape
-    block = pair_block(pairs, segments)
-    out = pl.BlockSpec((block, 2 * NH), lambda p: (p, 0))
-    return pl.pallas_call(
-        mirrored_kernel,
-        grid=(pairs // block,),
-        in_specs=[
-            pl.BlockSpec(memory_space=pltpu.SMEM),
-            ids_spec(block),
-            once(rows.shape),
-            pl.BlockSpec((segments, block, 2 * NH), lambda p: (0, p, 0)),
-            out,
-        ],
-        out_specs=out,
-        out_shape=jax.ShapeDtypeStruct((pairs, 2 * NH), BF),
-        compiler_params=params(TAIL),
-    )(segment, ids.reshape(-1, block // 128, 128), rows, receiver, own)
-
-
-def lags_kernel(segment_ref, count_ref, ids_ref, rows_ref, receiver_ref, own_ref, low_ref, table_ref, out_ref):
+def lags_kernel(
+    segment_ref, count_ref, ids_ref, rows_ref, low_ref, high_ref, low_own_ref, high_own_ref, table_ref, out_ref
+):
     pairs = out_ref.shape[0]
     held = rows_ref.shape[1]
     hot = one_hot(ids_ref[0] - held, held)
-    high = own_ref[...] + cross(hot, segment_ref, rows_ref, slice(None), receiver_ref)
-    values = jnp.dot(low_ref[...], table_ref[: 2 * NH], preferred_element_type=F32)
+    low = low_own_ref[...] + cross(hot, segment_ref, rows_ref, slice(0, 2 * NH), low_ref)
+    values = jnp.dot(low, table_ref[: 2 * NH], preferred_element_type=F32)
+    high = high_own_ref[...] + cross(hot, segment_ref, rows_ref, slice(2 * NH, 4 * NH), high_ref)
     values += jnp.dot(high, table_ref[2 * NH :], preferred_element_type=F32)
     place = pl.program_id(0) * pairs + lax.broadcasted_iota(jnp.int32, values.shape, 0)
-    scale = 1.0 / math.sqrt(receiver_ref.shape[0] * NF)
+    scale = 1.0 / math.sqrt(low_ref.shape[0] * NF)
     out_ref[...] = jnp.where(place < count_ref[0], values * scale, 0.0)
 
 
-def lags(segment, count, ids, rows, receiver, own, low):
-    segments, pairs, _ = receiver.shape
+def lags(segment, count, ids, rows, low, high, low_own, high_own):
+    segments, pairs, _ = low.shape
     block = pair_block(pairs, segments)
     table = lag_table().reshape(2, 2, NH, LAGS).transpose(1, 0, 2, 3).reshape(4 * NH, LAGS)
     bins = pl.BlockSpec((block, 2 * NH), lambda p: (p, 0))
+    receivers = pl.BlockSpec((segments, block, 2 * NH), lambda p: (0, p, 0))
+    in_smem = pl.BlockSpec(memory_space=pltpu.SMEM)
     return pl.pallas_call(
         lags_kernel,
         grid=(pairs // block,),
-        in_specs=[
-            pl.BlockSpec(memory_space=pltpu.SMEM),
-            pl.BlockSpec(memory_space=pltpu.SMEM),
-            ids_spec(block),
-            once(rows.shape),
-            pl.BlockSpec((segments, block, 2 * NH), lambda p: (0, p, 0)),
-            bins,
-            bins,
-            whole(table.shape),
-        ],
+        in_specs=[in_smem, in_smem, ids_spec(block), once(rows.shape), receivers, receivers, bins, bins]
+        + [whole(table.shape)],
         out_specs=pl.BlockSpec((block, LAGS), lambda p: (p, 0)),
         out_shape=jax.ShapeDtypeStruct((pairs, LAGS), F32),
         compiler_params=params(TAIL),
-    )(segment, count, ids.reshape(-1, block // 128, 128), rows, receiver, own, low, table)
+    )(segment, count, ids.reshape(-1, block // 128, 128), rows, low, high, low_own, high_own, table)
 
 
 def on_device(strain, taps, send_rows, pair_source, pair_receiver, pair_count):
@@ -426,7 +406,8 @@
     my_tm, my_half = lax.axis_index("tm"), lax.axis_index("half")
     capacity = send_rows.shape[3]
     width = strain.shape[1]
-    split = [512, width - 512] if width % 256 == 0 and width > 512 else [width]
+    parts = 2 if n_tm % 2 == 0 and width % 256 == 0 else 1
+    held = width // parts
     order = (my_tm - jnp.arange(n_tm, dtype=jnp.int32)) % n_tm
 
     def shifted(array, by):
@@ -453,45 +434,40 @@
 
     dec = decimate(strain, taps)
     place = jnp.stack([my_tm, jnp.int32(n_tm)]).astype(jnp.int32)
-    starts = [sum(split[:p]) for p in range(len(split))]
-    parts = [whiten(place, dec, first, last, before, after, fix, *part) for part in zip(starts, split)]
-    low, high = [list(half) for half in zip(*parts)]
-
-    low_across = [across(part) for part in low]
-    high_across = [across(part) for part in high[::-1]][::-1]
-
-    low, high = jnp.concatenate(low, axis=0), jnp.concatenate(high, axis=0)
+    asked, dec = lax.optimization_barrier((asked, dec))
     asked_own = lax.dynamic_index_in_dim(asked, my_half, 1, keepdims=False)
-    outgoing = pick(asked_own, [low, high], capacity)
-    outgoing, low_across[0] = lax.optimization_barrier((outgoing, low_across[0]))
-    own = exchange(outgoing)
+    asked_other = lax.dynamic_index_in_dim(asked, 1 - my_half, 1, keepdims=False)
+
+    spectra, mirrored, outgoing = [], [], []
+    for p in range(parts):
+        spectra.append(whiten(place, dec, first, last, before, after, fix, p * held, held))
+        mirrored.append(across(spectra[p]))
+        outgoing = [pick(asked_own, spectra[p], capacity, p, parts, outgoing)]
+    own = exchange(outgoing[0])
+
+    *spectra, outgoing[0] = lax.optimization_barrier((*spectra, outgoing[0]))
     receivers = []
     for a in range(n_tm):
-        at = (my_tm + a) % n_tm * (width // n_tm)
-        rows = [lax.dynamic_slice_in_dim(half, at, width // n_tm, 0) for half in (low, high)]
-        rows = jnp.concatenate(rows, axis=1)
+        group = (my_tm + a) % n_tm
+        each = n_tm // parts
+        cut = [lax.dynamic_slice_in_dim(part, group % each * (width // n_tm), width // n_tm, 0) for part in spectra]
+        rows = cut[0] if parts == 1 else jnp.where(group < each, cut[0], cut[1])
         receivers.append(shifted(rows, a) if a else rows)
-
-    asked_other = lax.dynamic_index_in_dim(asked, 1 - my_half, 1, keepdims=False)
 
     sender, column = pair_source[0] // capacity, pair_source[0] % capacity
     group, chan = sender // (2 * n_sub), sender % (2 * n_sub)
     slot = (chan % n_sub * n_tm + group) * capacity + column
     slot += jnp.where(chan // n_sub == my_half, 0, n_sub * n_tm * capacity)
 
-    outgoing = pick(asked_other, [jnp.concatenate(low_across, axis=0)], capacity)
-    outgoing, own, high_across[-1], *receivers = lax.optimization_barrier(
-        (outgoing, own, high_across[-1], *receivers)
-    )
+    outgoing = []
+    for p in range(parts):
+        cost = pl.CostEstimate(flops=COST[p], bytes_accessed=COST[p] // 300, transcendentals=0)
+        outgoing = [pick(asked_other, mirrored[p], capacity, p, parts, outgoing, cost)]
+    outgoing, own, *receivers = lax.optimization_barrier((*outgoing, own, *receivers))
     others = exchange(outgoing)
     receiver = receive(pair_receiver[0], receivers)
     bins = cross_own(order, slot, by_segment(own), *receiver)
-    *bins, high_across[0] = lax.optimization_barrier((*bins, high_across[0]))
-    outgoing = pick(asked_other, [jnp.concatenate(high_across, axis=0)], capacity)
-    outgoing, others = lax.optimization_barrier((outgoing, others))
-    bins[0] = cross_mirrored(order, slot, by_segment(others), receiver[0], bins[0])
-    others = exchange(outgoing)
-    return lags(order, pair_count, slot, by_segment(others), receiver[1], bins[1], bins[0])[None]
+    return lags(order, pair_count, slot, by_segment(others), *receiver, *bins)[None]
 
 
 def solution(mesh):

time: 152 us -> 150 us (0.987)
  waiting for transfers between devices: 42.5 us -> 54.4 us
  starting transfers between devices: 38.2 us -> 29.2 us
  local copies, waits for them, and re-layouts: 7.76 us -> 4.18 us
    all_to_all x3 -> x2, waiting for transfers between devices: 10.7 us -> 20 us  [exchange(): return lax.all_to_all(array, ('tm', 'sub'), 0, 0, tiled=True)]
    all_to_all x3 -> x2, starting transfers between devices: 15.1 us -> 9.37 us  [exchange(): return lax.all_to_all(array, ('tm', 'sub'), 0, 0, tiled=True)]
    ppermute x4 -> x2, waiting for transfers between devices: 30.2 us -> 34.3 us  [across(): return lax.ppermute(array, ('tm', 'half'), pairs)]
    pallas_call x2, Pallas kernels: 8.28 us -> 11.6 us  [whiten(): pl.pallas_call(whiten_kernel, grid=(held // chunk,), in_specs=[pl.BlockSp...]
    ppermute x4 -> x2, starting transfers between devices: 6.08 us -> 2.94 us  [across(): return lax.ppermute(array, ('tm', 'half'), pairs)]
    pallas_call x2 -> x1, Pallas kernels: 14.5 us -> 11.4 us  [lags(): pl.pallas_call(lags_kernel, grid=(pairs // block,), in_specs=[in_smem, in...]
    unnamed x53 -> x28, local copies, waits for them, and re-layouts: 6.28 us -> 3.47 us
    concatenate x6 -> x0, other arithmetic: 1.86 us -> none  [the longest x1 0.99 us: on_device(): jnp.concatenate(low_across, axis=0)]
  transfers between devices with their start and end apart: 13 -> 10, of which waited for: 7 -> 4; matrix products, arithmetic and copies ran while one was open for 3% -> 2% of each run, Pallas kernels for 30% -> 26%
where the time goes in v3:
time: 150 us; the launch traced here: 149 us
  Pallas kernels  58 us (39%)
  waiting for transfers between devices  54.4 us (36%)
  starting transfers between devices  29.2 us (19%)
  local copies, waits for them, and re-layouts  4.18 us (3%)
  other arithmetic  2.98 us (2%)
    ppermute x2, waiting for transfers between devices, across(): return lax.ppermute(array, ('tm', 'half'), pairs)  34.3 us
    all_to_all x2, waiting for transfers between devices, exchange(): return lax.all_to_all(array, ('tm', 'sub'), 0, 0, tiled=True)  20 us
    pallas_call x2, Pallas kernels, whiten(): pl.pallas_call(whiten_kernel, grid=(held // chunk,), in_specs=[pl.BlockSp...  11.6 us
    pallas_call x1, Pallas kernels, lags(): pl.pallas_call(lags_kernel, grid=(pairs // block,), in_specs=[in_smem, in...  11.4 us
    pallas_call x1, Pallas kernels, cross_own(): pl.pallas_call(own_kernel, grid=(pairs // block,), in_specs=[pl.BlockSpec...  9.41 us
    all_to_all x2, starting transfers between devices, exchange(): return lax.all_to_all(array, ('tm', 'sub'), 0, 0, tiled=True)  9.37 us
    pallas_call x1, Pallas kernels, receive(): pl.pallas_call(receive_kernel, grid=(pairs // block,), in_specs=[ids_spec...  7.93 us
    pallas_call x1, Pallas kernels, decimate(): pl.pallas_call(decimate_kernel, in_specs=[pl.BlockSpec(memory_space=pltpu...  7.85 us
  transfers between devices with their start and end apart: 10, of which 4 were waited for; matrix products, arithmetic and copies ran while one was open for 2% of the time, Pallas kernels for 26%

profile of v3, /device:TPU:0, one launch (start us, length us, event | category | flops | bytes accessed | tf_op | source)
XLA Modules:
  0.0 149.5 jit_solution(3456902290645259334)
XLA Ops:
  0.0 0.7 copy-done.5
  0.7 2.5 %shard_map.145 = (bf16[128,1280]{1,0:T(8,128)(2,1)S(1)}, bf16[128,1280]{1,0:T(8,128)(2,1)S(1)}, bf16[32,128]{1,0:T(8,128)(2,1)S(1)}) custom-call(f32[40]{0:T(128)S(1)} %copy-done.5, bf16[5120,1280]{1,0:T(8,128)(2,1)} %x_ref.3), custom_call_target="tpu_custom_call" | custom-call | tf_op jit(solution)/shard_map/pallas_call | solution.py:115
  3.2 0.6 copy-done.4
  3.8 1.3 collective-permute-start.1
  5.1 5.5 %collective-permute-start = (bf16[128,1280]{1,0:T(8,128)(2,1)S(1)}, bf16[128,1280]{1,0:T(8,128)(2,1)S(1)}, u32[]{:S(2)}, u32[]{:S(2)}) collective-permute-start(bf16[128,1280]{1,0:T(8,128)(2,1)S(1)} %get-tuple-element.31.last_ref), channel_id=1, source_target_pairs={{0,8},{8,16},{16,24},{1,9},{9,17},{17,25},{2,10},{10,18},{18,26},{... | collective-permute-start | bytes 983048 | tf_op jit(solution)/shard_map/ppermute | solution.py:429
  10.7 0.6 broadcast_in_dim.15
  11.3 6.2 %all-to-all-start = ((s32[8,4,128]{2,1,0:T(4,128)}), s32[8,4,128]{2,1,0:T(4,128)S(1)}, u32[]{:S(2)}, u32[]{:S(2)}) async-start(s32[8,4,128]{2,1,0:T(4,128)} %bitcast.2), calls=%async_computation | async-start | bytes 32768 | tf_op jit(solution)/shard_map/all_to_all | solution.py:432
  17.5 0.6 pad_add_fusion.place_ref
  18.1 7.9 %shard_map.146.dec_ref = bf16[1024,1280]{1,0:T(8,128)(2,1)} custom-call(f32[40]{0:T(128)S(1)} %copy-done.6, bf16[5120,1280]{1,0:T(8,128)(2,1)} %x_ref.3), custom_call_target="tpu_custom_call" | custom-call | tf_op jit(solution)/shard_map/pallas_call | solution.py:162
  26.1 0.7 copy-done.8
  26.9 5.8 %shard_map.148.rows_ref = bf16[640,512]{1,0:T(8,128)(2,1)} custom-call(s32[2]{0:T(128)} %pad_add_fusion.place_ref, bf16[1024,1280]{1,0:T(8,128)(2,1)} %shard_map.146.dec_ref, bf16[128,1280]{1,0:T(8,128)(2,1)} %copy-done.2, bf16[128,1280]{1,0:T(8,128)(2,1)} %copy-done.3, bf16[128,1280]{1,0:T(8,128)(2,1)} %copy-done.9, bf16[128,1280]{1,0:T(8,128)(2,1)} %copy-done.8, ...), custom_call_target="tpu_custom_call" | custom-call | tf_op jit(solution)/shard_map/pallas_call | solution.py:233
  32.7 2.9 %collective-permute-start.3 = (bf16[640,512]{1,0:T(8,128)(2,1)}, bf16[640,512]{1,0:T(8,128)(2,1)S(1)}, u32[]{:S(2)}, u32[]{:S(2)}) collective-permute-start(bf16[640,512]{1,0:T(8,128)(2,1)} %shard_map.148.rows_ref), channel_id=1, source_target_pairs={{0,4},{4,0},{8,12},{12,8},{16,20},{20,16},{24,28},{28,24},{1,5},{5... | collective-permute-start | bytes 1966088 | tf_op jit(solution)/shard_map/ppermute | solution.py:418
  35.6 5.8 %shard_map.147.rows_ref = bf16[640,512]{1,0:T(8,128)(2,1)} custom-call(s32[2]{0:T(128)} %pad_add_fusion.place_ref, bf16[1024,1280]{1,0:T(8,128)(2,1)} %shard_map.146.dec_ref, bf16[128,1280]{1,0:T(8,128)(2,1)} %copy-done.2, bf16[128,1280]{1,0:T(8,128)(2,1)} %copy-done.3, bf16[128,1280]{1,0:T(8,128)(2,1)} %copy-done.9, bf16[128,1280]{1,0:T(8,128)(2,1)} %copy-done.8, ...), custom_call_target="tpu_custom_call" | custom-call | tf_op jit(solution)/shard_map/pallas_call | solution.py:233
  41.5 1.8 %shard_map.151.refs_0_ = bf16[16,128,512]{2,1,0:T(8,128)(2,1)} custom-call(s32[2,4,128]{2,1,0:T(4,128)S(1)} %get-tuple-element.49.ids_ref, bf16[640,512]{1,0:T(8,128)(2,1)S(1)} %copy-done), custom_call_target="tpu_custom_call" | custom-call | tf_op jit(solution)/shard_map/pallas_call | solution.py:287
  43.3 1.8 %shard_map.152 = bf16[16,128,512]{2,1,0:T(8,128)(2,1)} custom-call(s32[2,4,128]{2,1,0:T(4,128)S(1)} %get-tuple-element.50.ids_ref, bf16[640,512]{1,0:T(8,128)(2,1)S(1)} %copy-done.1, bf16[16,128,512]{2,1,0:T(8,128)(2,1)} %shard_map.151.refs_0_), custom_call_target="tpu_custom_call", output_to_operand_aliasing={{}: (2, {})} | custom-call | tf_op jit(solution)/shard_map/pallas_call | solution.py:287
  45.1 5.3 %all-to-all-start.1 = ((bf16[16,128,512]{2,1,0:T(8,128)(2,1)}), bf16[16,128,512]{2,1,0:T(8,128)(2,1)}, u32[]{:S(2)}, u32[]{:S(2)}) async-start(bf16[16,128,512]{2,1,0:T(8,128)(2,1)} %shard_map.152), calls=%async_computation.1 | async-start | bytes 4194304 | tf_op jit(solution)/shard_map/all_to_all | solution.py:421
  50.5 1.2 dynamic-slice_select_fusion
  51.6 2.8 %collective-permute-start.6 = (bf16[320,512]{1,0:T(8,128)(2,1)S(1)}, bf16[320,512]{1,0:T(8,128)(2,1)S(1)}, u32[]{:S(2)}, u32[]{:S(2)}) collective-permute-start(bf16[320,512]{1,0:T(8,128)(2,1)S(1)} %get-tuple-element.45), channel_id=1, source_target_pairs={{0,24},{8,0},{16,8},{24,16},{1,25},{9,1},{17,9},{25,17},{2,26},{10... | collective-permute-start | bytes 983048 | tf_op jit(solution)/shard_map/ppermute | solution.py:414
  54.4 0.6 collective-permute-start.5
  55.0 0.6 collective-permute-start.4
  55.5 23.3 %collective-permute-done.3.rows_ref = bf16[640,512]{1,0:T(8,128)(2,1)S(1)} collective-permute-done((bf16[640,512]{1,0:T(8,128)(2,1)}, bf16[640,512]{1,0:T(8,128)(2,1)S(1)}, u32[]{:S(2)}, u32[]{:S(2)}) %collective-permute-start.3) | collective-permute-done | bytes 655392 | tf_op jit(solution)/shard_map/ppermute | solution.py:418
  78.8 1.8 %shard_map.149.refs_0_ = bf16[16,128,512]{2,1,0:T(8,128)(2,1)} custom-call(s32[2,4,128]{2,1,0:T(4,128)S(1)} %get-tuple-element.52.ids_ref, bf16[640,512]{1,0:T(8,128)(2,1)S(1)} %collective-permute-done.3.rows_ref), custom_call_target="tpu_custom_call" | custom-call | flops 69000003584 | bytes 230000000 | tf_op jit(solution)/shard_map/pallas_call | solution.py:287
  80.6 11.1 %collective-permute-done.2.rows_ref = bf16[640,512]{1,0:T(8,128)(2,1)S(1)} collective-permute-done((bf16[640,512]{1,0:T(8,128)(2,1)}, bf16[640,512]{1,0:T(8,128)(2,1)S(1)}, u32[]{:S(2)}, u32[]{:S(2)}) %collective-permute-start.2) | collective-permute-done | bytes 655392 | tf_op jit(solution)/shard_map/ppermute | solution.py:418
  91.7 1.8 %shard_map.150 = bf16[16,128,512]{2,1,0:T(8,128)(2,1)} custom-call(s32[2,4,128]{2,1,0:T(4,128)S(1)} %get-tuple-element.51.ids_ref, bf16[640,512]{1,0:T(8,128)(2,1)S(1)} %collective-permute-done.2.rows_ref, bf16[16,128,512]{2,1,0:T(8,128)(2,1)} %shard_map.149.refs_0_), custom_call_target="tpu_custom_call", output_to_operand_aliasing={{}: (2, {})} | custom-call | flops 69000003584 | bytes 230000000 | tf_op jit(solution)/shard_map/pallas_call | solution.py:287
  93.5 11.5 %all-to-all-done.1 = bf16[16,128,512]{2,1,0:T(8,128)(2,1)} async-done(((bf16[16,128,512]{2,1,0:T(8,128)(2,1)}), bf16[16,128,512]{2,1,0:T(8,128)(2,1)}, u32[]{:S(2)}, u32[]{:S(2)}) %all-to-all-start.1) | async-done | bytes 2097184 | tf_op jit(solution)/shard_map/all_to_all | solution.py:421
  105.0 4.0 %all-to-all-start.2 = ((bf16[16,128,512]{2,1,0:T(8,128)(2,1)}), bf16[16,128,512]{2,1,0:T(8,128)(2,1)S(1)}, u32[]{:S(2)}, u32[]{:S(2)}) async-start(bf16[16,128,512]{2,1,0:T(8,128)(2,1)} %shard_map.150), calls=%async_computation.2 | async-start | bytes 4194304 | tf_op jit(solution)/shard_map/all_to_all | solution.py:421
  110.2 0.7 fusion.4.ids_ref
  110.9 7.9 %shard_map.153 = (bf16[4,2048,256]{2,1,0:T(8,128)(2,1)}, bf16[4,2048,256]{2,1,0:T(8,128)(2,1)}) custom-call(s32[4,4,128]{2,1,0:T(4,128)} %bitcast.22, bf16[320,512]{1,0:T(8,128)(2,1)} %get-tuple-element.36.refs_0_, bf16[320,512]{1,0:T(8,128)(2,1)} %collective-permute-done.4.refs_1_, bf16[320,512]{1,0:T(8,128)(2,1)} %copy-done.11, bf16[320,512]{1,0:T(8,128)(2,1)} %copy-done.10), custom_call_target="tpu_custom_call" | custom-call | tf_op jit(solution)/shard_map/pallas_call | solution.py:327
  118.8 9.4 %shard_map.154 = (bf16[2048,256]{1,0:T(8,128)(2,1)}, bf16[2048,256]{1,0:T(8,128)(2,1)}) custom-call(s32[4]{0:T(128)} %and_select_fusion.segment_ref, s32[4,4,128]{2,1,0:T(4,128)} %fusion.4.ids_ref, bf16[4,512,512]{2,1,0:T(8,128)(2,1)} %bitcast.11.own_ref, bf16[4,2048,256]{2,1,0:T(8,128)(2,1)} %get-tuple-element.40.low_ref, ...), custom_call_target="tpu_custom_call" | custom-call | tf_op jit(solution)/shard_map/pallas_call | solution.py:361
  128.2 8.5 %all-to-all-done.2 = bf16[16,128,512]{2,1,0:T(8,128)(2,1)S(1)} async-done(((bf16[16,128,512]{2,1,0:T(8,128)(2,1)}), bf16[16,128,512]{2,1,0:T(8,128)(2,1)S(1)}, u32[]{:S(2)}, u32[]{:S(2)}) %all-to-all-start.2) | async-done | bytes 2097184 | tf_op jit(solution)/shard_map/all_to_all | solution.py:421
  136.7 1.4 copy-done.7
  138.1 11.4 %shard_map.155 = f32[2048,256]{1,0:T(8,128)} custom-call(s32[4]{0:T(128)} %and_select_fusion.segment_ref, s32[1]{0:T(128)S(6)} %copy.27.count_ref, s32[4,4,128]{2,1,0:T(4,128)} %fusion.4.ids_ref, bf16[4,512,512]{2,1,0:T(8,128)(2,1)} %bitcast.19, bf16[4,2048,256]{2,1,0:T(8,128)(2,1)} %get-tuple-element.40.low_ref, ...), custom_call_target="tpu_custom_call" | custom-call | tf_op jit(solution)/shard_map/pallas_call | solution.py:393
  (37 shorter events, 0.8 us)
Async XLA Ops:
  0.0 0.7 copy-start.5
  0.7 9.9 %copy-start.12 = (s32[1,4,8,32]{3,2,1,0:T(8,128)S(1)}, s32[1,4,8,32]{3,2,1,0:T(8,128)}, u32[]{:S(2)}) copy-start(s32[1,4,8,32]{3,2,1,0:T(8,128)} %param.17) | copy-start | bytes 12292
  0.7 17.5 %copy-start.6 = (f32[40]{0:T(128)S(1)}, f32[40]{0:T(128)}, u32[]{:S(2)}) copy-start(f32[40]{0:T(128)} %taps_ref.3) | copy-start | bytes 484
  3.2 0.6 copy-start.4
  3.8 22.2 %copy-start.2 = (bf16[128,1280]{1,0:T(8,128)(2,1)}, bf16[128,1280]{1,0:T(8,128)(2,1)S(1)}, u32[]{:S(2)}) copy-start(bf16[128,1280]{1,0:T(8,128)(2,1)S(1)} %get-tuple-element.30.first_ref) | copy-start | bytes 983044
  3.8 22.2 %copy-start.3 = (bf16[128,1280]{1,0:T(8,128)(2,1)}, bf16[128,1280]{1,0:T(8,128)(2,1)S(1)}, u32[]{:S(2)}) copy-start(bf16[128,1280]{1,0:T(8,128)(2,1)S(1)} %get-tuple-element.31.last_ref) | copy-start | bytes 983044
  3.8 22.3 %collective-permute-start.1 = (bf16[128,1280]{1,0:T(8,128)(2,1)S(1)}, bf16[128,1280]{1,0:T(8,128)(2,1)S(1)}, u32[]{:S(2)}, u32[]{:S(2)}) collective-permute-start(bf16[128,1280]{1,0:T(8,128)(2,1)S(1)} %get-tuple-element.30.first_ref), channel_id=1, source_target_pairs={{8,0},{16,8},{24,16},{9,1},{17,9},{25,17},{10,2},{18,10},{26,18},{... | collective-permute-start | bytes 983048 | tf_op jit(solution)/shard_map/ppermute | solution.py:430
  5.1 21.0 %collective-permute-start = (bf16[128,1280]{1,0:T(8,128)(2,1)S(1)}, bf16[128,1280]{1,0:T(8,128)(2,1)S(1)}, u32[]{:S(2)}, u32[]{:S(2)}) collective-permute-start(bf16[128,1280]{1,0:T(8,128)(2,1)S(1)} %get-tuple-element.31.last_ref), channel_id=1, source_target_pairs={{0,8},{8,16},{16,24},{1,9},{9,17},{17,25},{2,10},{10,18},{18,26},{... | collective-permute-start | bytes 983048 | tf_op jit(solution)/shard_map/ppermute | solution.py:429
  11.3 14.7 %all-to-all-start = ((s32[8,4,128]{2,1,0:T(4,128)}), s32[8,4,128]{2,1,0:T(4,128)S(1)}, u32[]{:S(2)}, u32[]{:S(2)}) async-start(s32[8,4,128]{2,1,0:T(4,128)} %bitcast.2), calls=%async_computation | async-start | bytes 32768 | tf_op jit(solution)/shard_map/all_to_all | solution.py:432
  26.0 0.7 copy-start.8
  26.1 0.8 copy-start.9
  32.7 46.1 %collective-permute-start.3 = (bf16[640,512]{1,0:T(8,128)(2,1)}, bf16[640,512]{1,0:T(8,128)(2,1)S(1)}, u32[]{:S(2)}, u32[]{:S(2)}) collective-permute-start(bf16[640,512]{1,0:T(8,128)(2,1)} %shard_map.148.rows_ref), channel_id=1, source_target_pairs={{0,4},{4,0},{8,12},{12,8},{16,20},{20,16},{24,28},{28,24},{1,5},{5... | collective-permute-start | bytes 1966088 | tf_op jit(solution)/shard_map/ppermute | solution.py:418
  35.6 5.9 %copy-start = (bf16[640,512]{1,0:T(8,128)(2,1)S(1)}, bf16[640,512]{1,0:T(8,128)(2,1)}, u32[]{:S(2)}) copy-start(bf16[640,512]{1,0:T(8,128)(2,1)} %shard_map.148.rows_ref) | copy-start | bytes 1966084
  41.5 1.8 %copy-start.1 = (bf16[640,512]{1,0:T(8,128)(2,1)S(1)}, bf16[640,512]{1,0:T(8,128)(2,1)}, u32[]{:S(2)}) copy-start(bf16[640,512]{1,0:T(8,128)(2,1)} %shard_map.147.rows_ref) | copy-start | bytes 1966084
  41.5 50.2 %collective-permute-start.2 = (bf16[640,512]{1,0:T(8,128)(2,1)}, bf16[640,512]{1,0:T(8,128)(2,1)S(1)}, u32[]{:S(2)}, u32[]{:S(2)}) collective-permute-start(bf16[640,512]{1,0:T(8,128)(2,1)} %shard_map.147.rows_ref), channel_id=1, source_target_pairs={{0,4},{4,0},{8,12},{12,8},{16,20},{20,16},{24,28},{28,24},{1,5},{5... | collective-permute-start | bytes 1966088 | tf_op jit(solution)/shard_map/ppermute | solution.py:418
  45.1 59.8 %all-to-all-start.1 = ((bf16[16,128,512]{2,1,0:T(8,128)(2,1)}), bf16[16,128,512]{2,1,0:T(8,128)(2,1)}, u32[]{:S(2)}, u32[]{:S(2)}) async-start(bf16[16,128,512]{2,1,0:T(8,128)(2,1)} %shard_map.152), calls=%async_computation.1 | async-start | bytes 4194304 | tf_op jit(solution)/shard_map/all_to_all | solution.py:421
  51.6 41.8 %collective-permute-start.6 = (bf16[320,512]{1,0:T(8,128)(2,1)S(1)}, bf16[320,512]{1,0:T(8,128)(2,1)S(1)}, u32[]{:S(2)}, u32[]{:S(2)}) collective-permute-start(bf16[320,512]{1,0:T(8,128)(2,1)S(1)} %get-tuple-element.45), channel_id=1, source_target_pairs={{0,24},{8,0},{16,8},{24,16},{1,25},{9,1},{17,9},{25,17},{2,26},{10... | collective-permute-start | bytes 983048 | tf_op jit(solution)/shard_map/ppermute | solution.py:414
  54.4 39.1 %collective-permute-start.5 = (bf16[320,512]{1,0:T(8,128)(2,1)S(1)}, bf16[320,512]{1,0:T(8,128)(2,1)S(1)}, u32[]{:S(2)}, u32[]{:S(2)}) collective-permute-start(bf16[320,512]{1,0:T(8,128)(2,1)S(1)} %get-tuple-element.46), channel_id=1, source_target_pairs={{0,16},{8,24},{16,0},{24,8},{1,17},{9,25},{17,1},{25,9},{2,18},{10... | collective-permute-start | bytes 983048 | tf_op jit(solution)/shard_map/ppermute | solution.py:414
  55.0 38.5 %collective-permute-start.4 = (bf16[320,512]{1,0:T(8,128)(2,1)S(1)}, bf16[320,512]{1,0:T(8,128)(2,1)}, u32[]{:S(2)}, u32[]{:S(2)}) collective-permute-start(bf16[320,512]{1,0:T(8,128)(2,1)S(1)} %get-tuple-element.47), channel_id=1, source_target_pairs={{0,8},{8,16},{16,24},{24,0},{1,9},{9,17},{17,25},{25,1},{2,10},{10... | collective-permute-start | bytes 983048 | tf_op jit(solution)/shard_map/ppermute | solution.py:414
  93.4 11.5 %copy-start.10 = (bf16[320,512]{1,0:T(8,128)(2,1)}, bf16[320,512]{1,0:T(8,128)(2,1)S(1)}, u32[]{:S(2)}) copy-start(bf16[320,512]{1,0:T(8,128)(2,1)S(1)} %collective-permute-done.6.refs_3_) | copy-start | bytes 983044
  93.5 11.5 %copy-start.11 = (bf16[320,512]{1,0:T(8,128)(2,1)}, bf16[320,512]{1,0:T(8,128)(2,1)S(1)}, u32[]{:S(2)}) copy-start(bf16[320,512]{1,0:T(8,128)(2,1)S(1)} %collective-permute-done.5.refs_2_) | copy-start | bytes 983044
  105.0 5.2 %copy-start.13 = (s32[1,2048]{1,0:T(1,128)S(1)}, s32[1,2048]{1,0:T(1,128)}, u32[]{:S(2)}) copy-start(s32[1,2048]{1,0:T(1,128)} %param.18) | copy-start | bytes 24580
  105.0 31.7 %all-to-all-start.2 = ((bf16[16,128,512]{2,1,0:T(8,128)(2,1)}), bf16[16,128,512]{2,1,0:T(8,128)(2,1)S(1)}, u32[]{:S(2)}, u32[]{:S(2)}) async-start(bf16[16,128,512]{2,1,0:T(8,128)(2,1)} %shard_map.150), calls=%async_computation.2 | async-start | bytes 4194304 | tf_op jit(solution)/shard_map/all_to_all | solution.py:421
  136.7 1.4 copy-start.7

commit v4 on v3

--- a/solution.py
+++ b/solution.py
@@ -441,8 +441,11 @@
     spectra, mirrored, outgoing = [], [], []
     for p in range(parts):
         spectra.append(whiten(place, dec, first, last, before, after, fix, p * held, held))
-        mirrored.append(across(spectra[p]))
         outgoing = [pick(asked_own, spectra[p], capacity, p, parts, outgoing)]
+        crossing = spectra[p]
+        if p:
+            crossing, outgoing[0] = lax.optimization_barrier((crossing, outgoing[0]))
+        mirrored.append(across(crossing))
     own = exchange(outgoing[0])
 
     *spectra, outgoing[0] = lax.optimization_barrier((*spectra, outgoing[0]))

time: 150 us -> 147 us (0.980)
  waiting for transfers between devices: 54.4 us -> 49.2 us
  local copies, waits for them, and re-layouts: 4.18 us -> 6.4 us
    all_to_all x2, waiting for transfers between devices: 20 us -> 16.2 us  [exchange(): return lax.all_to_all(array, ('tm', 'sub'), 0, 0, tiled=True)]
    unnamed x28 -> x34, local copies, waits for them, and re-layouts: 3.47 us -> 5.69 us
  transfers between devices with their start and end apart: 10 -> 10, of which waited for: 4 -> 4; matrix products, arithmetic and copies ran while one was open for 2% -> 3% of each run, Pallas kernels for 26% -> 26%
where the time goes in v4:
time: 147 us
  Pallas kernels  58 us (39%)
  waiting for transfers between devices  49.2 us (33%)
  starting transfers between devices  29.2 us (20%)
  local copies, waits for them, and re-layouts  6.4 us (4%)
  other arithmetic  3.06 us (2%)
    ppermute x2, waiting for transfers between devices, across(): return lax.ppermute(array, ('tm', 'half'), pairs)  33 us
    all_to_all x2, waiting for transfers between devices, exchange(): return lax.all_to_all(array, ('tm', 'sub'), 0, 0, tiled=True)  16.2 us
    pallas_call x2, Pallas kernels, whiten(): pl.pallas_call(whiten_kernel, grid=(held // chunk,), in_specs=[pl.BlockSp...  11.6 us
    pallas_call x1, Pallas kernels, lags(): pl.pallas_call(lags_kernel, grid=(pairs // block,), in_specs=[in_smem, in...  11.4 us
    pallas_call x1, Pallas kernels, cross_own(): pl.pallas_call(own_kernel, grid=(pairs // block,), in_specs=[pl.BlockSpec...  9.41 us
    all_to_all x2, starting transfers between devices, exchange(): return lax.all_to_all(array, ('tm', 'sub'), 0, 0, tiled=True)  8.85 us
    pallas_call x1, Pallas kernels, receive(): pl.pallas_call(receive_kernel, grid=(pairs // block,), in_specs=[ids_spec...  7.92 us
    pallas_call x1, Pallas kernels, decimate(): pl.pallas_call(decimate_kernel, in_specs=[pl.BlockSpec(memory_space=pltpu...  7.84 us
  transfers between devices with their start and end apart: 10, of which 4 were waited for; matrix products, arithmetic and copies ran while one was open for 3% of the time, Pallas kernels for 26%

profile of v4, /device:TPU:0, one launch (start us, length us, event | category | flops | bytes accessed | tf_op | source)
XLA Modules:
  0.0 146.7 jit_solution(9593590388688466625)
XLA Ops:
  0.0 0.7 copy-done.7
  0.7 2.5 %shard_map.145 = (bf16[128,1280]{1,0:T(8,128)(2,1)S(1)}, bf16[128,1280]{1,0:T(8,128)(2,1)S(1)}, bf16[32,128]{1,0:T(8,128)(2,1)S(1)}) custom-call(f32[40]{0:T(128)S(1)} %copy-done.7, bf16[5120,1280]{1,0:T(8,128)(2,1)} %x_ref.3), custom_call_target="tpu_custom_call" | custom-call | tf_op jit(solution)/shard_map/pallas_call | solution.py:115
  3.8 1.3 collective-permute-start.1
  5.1 5.5 %collective-permute-start = (bf16[128,1280]{1,0:T(8,128)(2,1)S(1)}, bf16[128,1280]{1,0:T(8,128)(2,1)S(1)}, u32[]{:S(2)}, u32[]{:S(2)}) collective-permute-start(bf16[128,1280]{1,0:T(8,128)(2,1)S(1)} %get-tuple-element.33.last_ref), channel_id=1, source_target_pairs={{0,8},{8,16},{16,24},{1,9},{9,17},{17,25},{2,10},{10,18},{18,26},{... | collective-permute-start | bytes 983048 | tf_op jit(solution)/shard_map/ppermute | solution.py:429
  10.7 0.6 broadcast_in_dim.15
  11.3 6.2 %all-to-all-start = ((s32[8,4,128]{2,1,0:T(4,128)}), s32[8,4,128]{2,1,0:T(4,128)S(1)}, u32[]{:S(2)}, u32[]{:S(2)}) async-start(s32[8,4,128]{2,1,0:T(4,128)} %bitcast.2), calls=%async_computation | async-start | bytes 32768 | tf_op jit(solution)/shard_map/all_to_all | solution.py:432
  17.5 0.7 pad_add_fusion.place_ref
  18.1 7.8 %shard_map.146.dec_ref = bf16[1024,1280]{1,0:T(8,128)(2,1)} custom-call(f32[40]{0:T(128)S(1)} %copy-done.8, bf16[5120,1280]{1,0:T(8,128)(2,1)} %x_ref.3), custom_call_target="tpu_custom_call" | custom-call | tf_op jit(solution)/shard_map/pallas_call | solution.py:162
  26.1 0.7 copy-done.10
  26.9 5.8 %shard_map.148.rows_ref = bf16[640,512]{1,0:T(8,128)(2,1)} custom-call(s32[2]{0:T(128)} %pad_add_fusion.place_ref, bf16[1024,1280]{1,0:T(8,128)(2,1)} %shard_map.146.dec_ref, bf16[128,1280]{1,0:T(8,128)(2,1)} %copy-done.4, bf16[128,1280]{1,0:T(8,128)(2,1)} %copy-done.5, bf16[128,1280]{1,0:T(8,128)(2,1)} %copy-done.11, bf16[128,1280]{1,0:T(8,128)(2,1)} %copy-done.10, ...), custom_call_target="tpu_custom_call" | custom-call | tf_op jit(solution)/shard_map/pallas_call | solution.py:233
  32.8 2.9 %collective-permute-start.3 = (bf16[640,512]{1,0:T(8,128)(2,1)}, bf16[640,512]{1,0:T(8,128)(2,1)S(1)}, u32[]{:S(2)}, u32[]{:S(2)}) collective-permute-start(bf16[640,512]{1,0:T(8,128)(2,1)} %shard_map.148.rows_ref), channel_id=1, source_target_pairs={{0,4},{4,0},{8,12},{12,8},{16,20},{20,16},{24,28},{28,24},{1,5},{5... | collective-permute-start | bytes 1966088 | tf_op jit(solution)/shard_map/ppermute | solution.py:418
  35.7 1.1 copy-done
  36.8 1.8 %shard_map.149.refs_0_ = bf16[16,128,512]{2,1,0:T(8,128)(2,1)} custom-call(s32[2,4,128]{2,1,0:T(4,128)S(1)} %get-tuple-element.56.ids_ref, bf16[640,512]{1,0:T(8,128)(2,1)S(1)} %copy-done), custom_call_target="tpu_custom_call" | custom-call | tf_op jit(solution)/shard_map/pallas_call | solution.py:287
  38.6 5.8 %shard_map.147.rows_ref = bf16[640,512]{1,0:T(8,128)(2,1)} custom-call(s32[2]{0:T(128)} %pad_add_fusion.place_ref, bf16[1024,1280]{1,0:T(8,128)(2,1)} %shard_map.146.dec_ref, bf16[128,1280]{1,0:T(8,128)(2,1)} %copy-done.4, bf16[128,1280]{1,0:T(8,128)(2,1)} %copy-done.5, bf16[128,1280]{1,0:T(8,128)(2,1)} %copy-done.11, bf16[128,1280]{1,0:T(8,128)(2,1)} %copy-done.10, ...), custom_call_target="tpu_custom_call" | custom-call | tf_op jit(solution)/shard_map/pallas_call | solution.py:233
  44.4 1.1 copy-done.2
  45.5 1.8 %shard_map.150 = bf16[16,128,512]{2,1,0:T(8,128)(2,1)} custom-call(s32[2,4,128]{2,1,0:T(4,128)S(1)} %get-tuple-element.54.ids_ref, bf16[640,512]{1,0:T(8,128)(2,1)S(1)} %copy-done.2, bf16[16,128,512]{2,1,0:T(8,128)(2,1)} %shard_map.149.refs_0_), custom_call_target="tpu_custom_call", output_to_operand_aliasing={{}: (2, {})} | custom-call | tf_op jit(solution)/shard_map/pallas_call | solution.py:287
  47.4 4.9 %all-to-all-start.1 = ((bf16[16,128,512]{2,1,0:T(8,128)(2,1)}), bf16[16,128,512]{2,1,0:T(8,128)(2,1)}, u32[]{:S(2)}, u32[]{:S(2)}) async-start(bf16[16,128,512]{2,1,0:T(8,128)(2,1)} %shard_map.150), calls=%async_computation.1 | async-start | bytes 4194304 | tf_op jit(solution)/shard_map/all_to_all | solution.py:421
  52.3 1.2 dynamic-slice_select_fusion
  53.5 2.8 %collective-permute-start.6 = (bf16[320,512]{1,0:T(8,128)(2,1)S(1)}, bf16[320,512]{1,0:T(8,128)(2,1)S(1)}, u32[]{:S(2)}, u32[]{:S(2)}) collective-permute-start(bf16[320,512]{1,0:T(8,128)(2,1)S(1)} %get-tuple-element.49), channel_id=1, source_target_pairs={{0,24},{8,0},{16,8},{24,16},{1,25},{9,1},{17,9},{25,17},{2,26},{10... | collective-permute-start | bytes 983048 | tf_op jit(solution)/shard_map/ppermute | solution.py:414
  57.9 6.9 %collective-permute-done.3.rows_ref = bf16[640,512]{1,0:T(8,128)(2,1)S(1)} collective-permute-done((bf16[640,512]{1,0:T(8,128)(2,1)}, bf16[640,512]{1,0:T(8,128)(2,1)S(1)}, u32[]{:S(2)}, u32[]{:S(2)}) %collective-permute-start.3) | collective-permute-done | bytes 655392 | tf_op jit(solution)/shard_map/ppermute | solution.py:418
  64.8 1.8 %shard_map.151.refs_0_ = bf16[16,128,512]{2,1,0:T(8,128)(2,1)} custom-call(s32[2,4,128]{2,1,0:T(4,128)S(1)} %get-tuple-element.53.ids_ref, bf16[640,512]{1,0:T(8,128)(2,1)S(1)} %collective-permute-done.3.rows_ref), custom_call_target="tpu_custom_call" | custom-call | flops 69000003584 | bytes 230000000 | tf_op jit(solution)/shard_map/pallas_call | solution.py:287
  66.6 26.1 %collective-permute-done.2.rows_ref = bf16[640,512]{1,0:T(8,128)(2,1)S(1)} collective-permute-done((bf16[640,512]{1,0:T(8,128)(2,1)S(1)}, bf16[640,512]{1,0:T(8,128)(2,1)S(1)}, u32[]{:S(2)}, u32[]{:S(2)}) %collective-permute-start.2) | collective-permute-done | bytes 655392 | tf_op jit(solution)/shard_map/ppermute | solution.py:418
  92.7 1.8 %shard_map.152 = bf16[16,128,512]{2,1,0:T(8,128)(2,1)} custom-call(s32[2,4,128]{2,1,0:T(4,128)S(1)} %get-tuple-element.55.ids_ref, bf16[640,512]{1,0:T(8,128)(2,1)S(1)} %collective-permute-done.2.rows_ref, bf16[16,128,512]{2,1,0:T(8,128)(2,1)} %shard_map.151.refs_0_), custom_call_target="tpu_custom_call", output_to_operand_aliasing={{}: (2, {})} | custom-call | flops 69000003584 | bytes 230000000 | tf_op jit(solution)/shard_map/pallas_call | solution.py:287
  94.5 7.8 %all-to-all-done.1 = bf16[16,128,512]{2,1,0:T(8,128)(2,1)} async-done(((bf16[16,128,512]{2,1,0:T(8,128)(2,1)}), bf16[16,128,512]{2,1,0:T(8,128)(2,1)}, u32[]{:S(2)}, u32[]{:S(2)}) %all-to-all-start.1) | async-done | bytes 2097184 | tf_op jit(solution)/shard_map/all_to_all | solution.py:421
  102.3 3.9 %all-to-all-start.2 = ((bf16[16,128,512]{2,1,0:T(8,128)(2,1)}), bf16[16,128,512]{2,1,0:T(8,128)(2,1)S(1)}, u32[]{:S(2)}, u32[]{:S(2)}) async-start(bf16[16,128,512]{2,1,0:T(8,128)(2,1)} %shard_map.152), calls=%async_computation.2 | async-start | bytes 4194304 | tf_op jit(solution)/shard_map/all_to_all | solution.py:421
  106.9 0.6 and_select_fusion.segment_ref
  107.5 0.7 fusion.4.ids_ref
  108.2 7.9 %shard_map.153 = (bf16[4,2048,256]{2,1,0:T(8,128)(2,1)}, bf16[4,2048,256]{2,1,0:T(8,128)(2,1)}) custom-call(s32[4,4,128]{2,1,0:T(4,128)} %bitcast.22, bf16[320,512]{1,0:T(8,128)(2,1)} %get-tuple-element.40.refs_0_, bf16[320,512]{1,0:T(8,128)(2,1)} %copy-done.14, bf16[320,512]{1,0:T(8,128)(2,1)} %copy-done.13, bf16[320,512]{1,0:T(8,128)(2,1)} %copy-done.12), custom_call_target="tpu_custom_call" | custom-call | tf_op jit(solution)/shard_map/pallas_call | solution.py:327
  116.1 9.4 %shard_map.154 = (bf16[2048,256]{1,0:T(8,128)(2,1)}, bf16[2048,256]{1,0:T(8,128)(2,1)}) custom-call(s32[4]{0:T(128)} %and_select_fusion.segment_ref, s32[4,4,128]{2,1,0:T(4,128)} %fusion.4.ids_ref, bf16[4,512,512]{2,1,0:T(8,128)(2,1)} %bitcast.11.own_ref, bf16[4,2048,256]{2,1,0:T(8,128)(2,1)} %get-tuple-element.44.low_ref, ...), custom_call_target="tpu_custom_call" | custom-call | tf_op jit(solution)/shard_map/pallas_call | solution.py:361
  125.5 8.4 %all-to-all-done.2 = bf16[16,128,512]{2,1,0:T(8,128)(2,1)S(1)} async-done(((bf16[16,128,512]{2,1,0:T(8,128)(2,1)}), bf16[16,128,512]{2,1,0:T(8,128)(2,1)S(1)}, u32[]{:S(2)}, u32[]{:S(2)}) %all-to-all-start.2) | async-done | bytes 2097184 | tf_op jit(solution)/shard_map/all_to_all | solution.py:421
  133.9 1.4 copy-done.9
  135.3 11.4 %shard_map.155 = f32[2048,256]{1,0:T(8,128)} custom-call(s32[4]{0:T(128)} %and_select_fusion.segment_ref, s32[1]{0:T(128)S(6)} %copy.27.count_ref, s32[4,4,128]{2,1,0:T(4,128)} %fusion.4.ids_ref, bf16[4,512,512]{2,1,0:T(8,128)(2,1)} %bitcast.19, bf16[4,2048,256]{2,1,0:T(8,128)(2,1)} %get-tuple-element.44.low_ref, ...), custom_call_target="tpu_custom_call" | custom-call | tf_op jit(solution)/shard_map/pallas_call | solution.py:393
  (43 shorter events, 2.6 us)
Async XLA Ops:
  0.0 0.7 copy-start.7
  0.7 9.9 %copy-start.15 = (s32[1,4,8,32]{3,2,1,0:T(8,128)S(1)}, s32[1,4,8,32]{3,2,1,0:T(8,128)}, u32[]{:S(2)}) copy-start(s32[1,4,8,32]{3,2,1,0:T(8,128)} %param.17) | copy-start | bytes 12292
  0.7 17.5 %copy-start.8 = (f32[40]{0:T(128)S(1)}, f32[40]{0:T(128)}, u32[]{:S(2)}) copy-start(f32[40]{0:T(128)} %taps_ref.3) | copy-start | bytes 484
  3.2 0.6 copy-start.6
  3.8 22.2 %copy-start.4 = (bf16[128,1280]{1,0:T(8,128)(2,1)}, bf16[128,1280]{1,0:T(8,128)(2,1)S(1)}, u32[]{:S(2)}) copy-start(bf16[128,1280]{1,0:T(8,128)(2,1)S(1)} %get-tuple-element.32.first_ref) | copy-start | bytes 983044
  3.8 22.2 %copy-start.5 = (bf16[128,1280]{1,0:T(8,128)(2,1)}, bf16[128,1280]{1,0:T(8,128)(2,1)S(1)}, u32[]{:S(2)}) copy-start(bf16[128,1280]{1,0:T(8,128)(2,1)S(1)} %get-tuple-element.33.last_ref) | copy-start | bytes 983044
  3.8 22.2 %collective-permute-start.1 = (bf16[128,1280]{1,0:T(8,128)(2,1)S(1)}, bf16[128,1280]{1,0:T(8,128)(2,1)S(1)}, u32[]{:S(2)}, u32[]{:S(2)}) collective-permute-start(bf16[128,1280]{1,0:T(8,128)(2,1)S(1)} %get-tuple-element.32.first_ref), channel_id=1, source_target_pairs={{8,0},{16,8},{24,16},{9,1},{17,9},{25,17},{10,2},{18,10},{26,18},{... | collective-permute-start | bytes 983048 | tf_op jit(solution)/shard_map/ppermute | solution.py:430
  5.1 21.0 %collective-permute-start = (bf16[128,1280]{1,0:T(8,128)(2,1)S(1)}, bf16[128,1280]{1,0:T(8,128)(2,1)S(1)}, u32[]{:S(2)}, u32[]{:S(2)}) collective-permute-start(bf16[128,1280]{1,0:T(8,128)(2,1)S(1)} %get-tuple-element.33.last_ref), channel_id=1, source_target_pairs={{0,8},{8,16},{16,24},{1,9},{9,17},{17,25},{2,10},{10,18},{18,26},{... | collective-permute-start | bytes 983048 | tf_op jit(solution)/shard_map/ppermute | solution.py:429
  11.3 14.7 %all-to-all-start = ((s32[8,4,128]{2,1,0:T(4,128)}), s32[8,4,128]{2,1,0:T(4,128)S(1)}, u32[]{:S(2)}, u32[]{:S(2)}) async-start(s32[8,4,128]{2,1,0:T(4,128)} %bitcast.2), calls=%async_computation | async-start | bytes 32768 | tf_op jit(solution)/shard_map/all_to_all | solution.py:432
  26.0 0.7 copy-start.10
  26.1 0.9 copy-start.11
  32.8 32.1 %collective-permute-start.3 = (bf16[640,512]{1,0:T(8,128)(2,1)}, bf16[640,512]{1,0:T(8,128)(2,1)S(1)}, u32[]{:S(2)}, u32[]{:S(2)}) collective-permute-start(bf16[640,512]{1,0:T(8,128)(2,1)} %shard_map.148.rows_ref), channel_id=1, source_target_pairs={{0,4},{4,0},{8,12},{12,8},{16,20},{20,16},{24,28},{28,24},{1,5},{5... | collective-permute-start | bytes 1966088 | tf_op jit(solution)/shard_map/ppermute | solution.py:418
  35.7 1.1 copy-start
  44.4 1.1 copy-start.2
  47.3 5.0 %copy-start.1 = (bf16[640,512]{1,0:T(8,128)(2,1)S(1)}, bf16[640,512]{1,0:T(8,128)(2,1)}, u32[]{:S(2)}) copy-start(bf16[640,512]{1,0:T(8,128)(2,1)} %shard_map.148.rows_ref) | copy-start | bytes 1966084
  47.3 5.0 %copy-start.3 = (bf16[640,512]{1,0:T(8,128)(2,1)S(1)}, bf16[640,512]{1,0:T(8,128)(2,1)}, u32[]{:S(2)}) copy-start(bf16[640,512]{1,0:T(8,128)(2,1)} %shard_map.147.rows_ref) | copy-start | bytes 1966084
  47.4 55.0 %all-to-all-start.1 = ((bf16[16,128,512]{2,1,0:T(8,128)(2,1)}), bf16[16,128,512]{2,1,0:T(8,128)(2,1)}, u32[]{:S(2)}, u32[]{:S(2)}) async-start(bf16[16,128,512]{2,1,0:T(8,128)(2,1)} %shard_map.150), calls=%async_computation.1 | async-start | bytes 4194304 | tf_op jit(solution)/shard_map/all_to_all | solution.py:421
  53.5 41.0 %collective-permute-start.6 = (bf16[320,512]{1,0:T(8,128)(2,1)S(1)}, bf16[320,512]{1,0:T(8,128)(2,1)S(1)}, u32[]{:S(2)}, u32[]{:S(2)}) collective-permute-start(bf16[320,512]{1,0:T(8,128)(2,1)S(1)} %get-tuple-element.49), channel_id=1, source_target_pairs={{0,24},{8,0},{16,8},{24,16},{1,25},{9,1},{17,9},{25,17},{2,26},{10... | collective-permute-start | bytes 983048 | tf_op jit(solution)/shard_map/ppermute | solution.py:414
  56.3 38.2 %collective-permute-start.5 = (bf16[320,512]{1,0:T(8,128)(2,1)S(1)}, bf16[320,512]{1,0:T(8,128)(2,1)S(1)}, u32[]{:S(2)}, u32[]{:S(2)}) collective-permute-start(bf16[320,512]{1,0:T(8,128)(2,1)S(1)} %get-tuple-element.50), channel_id=1, source_target_pairs={{0,16},{8,24},{16,0},{24,8},{1,17},{9,25},{17,1},{25,9},{2,18},{10... | collective-permute-start | bytes 983048 | tf_op jit(solution)/shard_map/ppermute | solution.py:414
  56.8 37.7 %collective-permute-start.4 = (bf16[320,512]{1,0:T(8,128)(2,1)S(1)}, bf16[320,512]{1,0:T(8,128)(2,1)S(1)}, u32[]{:S(2)}, u32[]{:S(2)}) collective-permute-start(bf16[320,512]{1,0:T(8,128)(2,1)S(1)} %get-tuple-element.51), channel_id=1, source_target_pairs={{0,8},{8,16},{16,24},{24,0},{1,9},{9,17},{17,25},{25,1},{2,10},{10... | collective-permute-start | bytes 983048 | tf_op jit(solution)/shard_map/ppermute | solution.py:414
  57.4 35.3 %collective-permute-start.2 = (bf16[640,512]{1,0:T(8,128)(2,1)S(1)}, bf16[640,512]{1,0:T(8,128)(2,1)S(1)}, u32[]{:S(2)}, u32[]{:S(2)}) collective-permute-start(bf16[640,512]{1,0:T(8,128)(2,1)S(1)} %copy-done.3), channel_id=1, source_target_pairs={{0,4},{4,0},{8,12},{12,8},{16,20},{20,16},{24,28},{28,24},{1,5},{5... | collective-permute-start | bytes 1966088 | tf_op jit(solution)/shard_map/ppermute | solution.py:418
  94.5 7.9 %copy-start.12 = (bf16[320,512]{1,0:T(8,128)(2,1)}, bf16[320,512]{1,0:T(8,128)(2,1)S(1)}, u32[]{:S(2)}) copy-start(bf16[320,512]{1,0:T(8,128)(2,1)S(1)} %collective-permute-done.6.refs_3_) | copy-start | bytes 983044
  94.5 7.8 %copy-start.13 = (bf16[320,512]{1,0:T(8,128)(2,1)}, bf16[320,512]{1,0:T(8,128)(2,1)S(1)}, u32[]{:S(2)}) copy-start(bf16[320,512]{1,0:T(8,128)(2,1)S(1)} %collective-permute-done.5.refs_2_) | copy-start | bytes 983044
  94.5 7.8 %copy-start.14 = (bf16[320,512]{1,0:T(8,128)(2,1)}, bf16[320,512]{1,0:T(8,128)(2,1)S(1)}, u32[]{:S(2)}) copy-start(bf16[320,512]{1,0:T(8,128)(2,1)S(1)} %collective-permute-done.4.refs_1_) | copy-start | bytes 983044
  102.3 5.2 %copy-start.16 = (s32[1,2048]{1,0:T(1,128)S(1)}, s32[1,2048]{1,0:T(1,128)}, u32[]{:S(2)}) copy-start(s32[1,2048]{1,0:T(1,128)} %param.18) | copy-start | bytes 24580
  102.3 31.6 %all-to-all-start.2 = ((bf16[16,128,512]{2,1,0:T(8,128)(2,1)}), bf16[16,128,512]{2,1,0:T(8,128)(2,1)S(1)}, u32[]{:S(2)}, u32[]{:S(2)}) async-start(bf16[16,128,512]{2,1,0:T(8,128)(2,1)} %shard_map.152), calls=%async_computation.2 | async-start | bytes 4194304 | tf_op jit(solution)/shard_map/all_to_all | solution.py:421
  133.9 1.4 copy-start.9

commit v5 on v4

--- a/solution.py
+++ b/solution.py
@@ -369,11 +369,19 @@
 
 
 def lags_kernel(
-    segment_ref, count_ref, ids_ref, rows_ref, low_ref, high_ref, low_own_ref, high_own_ref, table_ref, out_ref
+    segment_ref, count_ref, ids_ref, given_ref, low_ref, high_ref, low_own_ref, high_own_ref, table_ref, out_ref,
+    rows_ref, arrived
 ):
     pairs = out_ref.shape[0]
     held = rows_ref.shape[1]
     hot = one_hot(ids_ref[0] - held, held)
+
+    @pl.when(pl.program_id(0) == 0)
+    def _():
+        fetch = pltpu.make_async_copy(given_ref, rows_ref, arrived)
+        fetch.start()
+        fetch.wait()
+
     low = low_own_ref[...] + cross(hot, segment_ref, rows_ref, slice(0, 2 * NH), low_ref)
     values = jnp.dot(low, table_ref[: 2 * NH], preferred_element_type=F32)
     high = high_own_ref[...] + cross(hot, segment_ref, rows_ref, slice(2 * NH, 4 * NH), high_ref)
@@ -393,10 +401,11 @@
     return pl.pallas_call(
         lags_kernel,
         grid=(pairs // block,),
-        in_specs=[in_smem, in_smem, ids_spec(block), once(rows.shape), receivers, receivers, bins, bins]
+        in_specs=[in_smem, in_smem, ids_spec(block), pl.BlockSpec(memory_space=pl.ANY), receivers, receivers, bins, bins]
         + [whole(table.shape)],
         out_specs=pl.BlockSpec((block, LAGS), lambda p: (p, 0)),
         out_shape=jax.ShapeDtypeStruct((pairs, LAGS), F32),
+        scratch_shapes=[pltpu.VMEM(rows.shape, BF), pltpu.SemaphoreType.DMA],
         compiler_params=params(TAIL),
     )(segment, count, ids.reshape(-1, block // 128, 128), rows, low, high, low_own, high_own, table)
 

time: 147 us -> 148 us (level)
  no operation moved by 1% of the time
where the time goes in v5:
time: 148 us
  Pallas kernels  58.9 us (40%)
  waiting for transfers between devices  49.2 us (33%)
  starting transfers between devices  29.2 us (20%)
  local copies, waits for them, and re-layouts  6.4 us (4%)
  other arithmetic  3.06 us (2%)
    ppermute x2, waiting for transfers between devices, across(): return lax.ppermute(array, ('tm', 'half'), pairs)  33 us
    all_to_all x2, waiting for transfers between devices, exchange(): return lax.all_to_all(array, ('tm', 'sub'), 0, 0, tiled=True)  16.2 us
    pallas_call x1, Pallas kernels, lags(): pl.pallas_call(lags_kernel, grid=(pairs // block,), in_specs=[in_smem, in...  12.4 us
    pallas_call x2, Pallas kernels, whiten(): pl.pallas_call(whiten_kernel, grid=(held // chunk,), in_specs=[pl.BlockSp...  11.6 us
    pallas_call x1, Pallas kernels, cross_own(): pl.pallas_call(own_kernel, grid=(pairs // block,), in_specs=[pl.BlockSpec...  9.41 us
    all_to_all x2, starting transfers between devices, exchange(): return lax.all_to_all(array, ('tm', 'sub'), 0, 0, tiled=True)  8.85 us
    pallas_call x1, Pallas kernels, receive(): pl.pallas_call(receive_kernel, grid=(pairs // block,), in_specs=[ids_spec...  7.92 us
    pallas_call x1, Pallas kernels, decimate(): pl.pallas_call(decimate_kernel, in_specs=[pl.BlockSpec(memory_space=pltpu...  7.84 us
  transfers between devices with their start and end apart: 10, of which 4 were waited for; matrix products, arithmetic and copies ran while one was open for 3% of the time, Pallas kernels for 26%

profile of v5, /device:TPU:0, one launch (start us, length us, event | category | flops | bytes accessed | tf_op | source)
XLA Modules:
  0.0 147.8 jit_solution(15561271853328025008)
XLA Ops:
  0.0 0.7 copy-done.7
  0.7 2.5 %shard_map.145 = (bf16[128,1280]{1,0:T(8,128)(2,1)S(1)}, bf16[128,1280]{1,0:T(8,128)(2,1)S(1)}, bf16[32,128]{1,0:T(8,128)(2,1)S(1)}) custom-call(f32[40]{0:T(128)S(1)} %copy-done.7, bf16[5120,1280]{1,0:T(8,128)(2,1)} %x_ref.3), custom_call_target="tpu_custom_call" | custom-call | tf_op jit(solution)/shard_map/pallas_call | solution.py:115
  3.8 1.3 collective-permute-start.1
  5.1 5.5 %collective-permute-start = (bf16[128,1280]{1,0:T(8,128)(2,1)S(1)}, bf16[128,1280]{1,0:T(8,128)(2,1)S(1)}, u32[]{:S(2)}, u32[]{:S(2)}) collective-permute-start(bf16[128,1280]{1,0:T(8,128)(2,1)S(1)} %get-tuple-element.33.last_ref), channel_id=1, source_target_pairs={{0,8},{8,16},{16,24},{1,9},{9,17},{17,25},{2,10},{10,18},{18,26},{... | collective-permute-start | bytes 983048 | tf_op jit(solution)/shard_map/ppermute | solution.py:438
  10.7 0.6 broadcast_in_dim.15
  11.3 6.2 %all-to-all-start = ((s32[8,4,128]{2,1,0:T(4,128)}), s32[8,4,128]{2,1,0:T(4,128)S(1)}, u32[]{:S(2)}, u32[]{:S(2)}) async-start(s32[8,4,128]{2,1,0:T(4,128)} %bitcast.2), calls=%async_computation | async-start | bytes 32768 | tf_op jit(solution)/shard_map/all_to_all | solution.py:441
  17.5 0.7 pad_add_fusion.place_ref
  18.1 7.8 %shard_map.146.dec_ref = bf16[1024,1280]{1,0:T(8,128)(2,1)} custom-call(f32[40]{0:T(128)S(1)} %copy-done.8, bf16[5120,1280]{1,0:T(8,128)(2,1)} %x_ref.3), custom_call_target="tpu_custom_call" | custom-call | tf_op jit(solution)/shard_map/pallas_call | solution.py:162
  26.1 0.7 copy-done.10
  26.9 5.8 %shard_map.148.rows_ref = bf16[640,512]{1,0:T(8,128)(2,1)} custom-call(s32[2]{0:T(128)} %pad_add_fusion.place_ref, bf16[1024,1280]{1,0:T(8,128)(2,1)} %shard_map.146.dec_ref, bf16[128,1280]{1,0:T(8,128)(2,1)} %copy-done.4, bf16[128,1280]{1,0:T(8,128)(2,1)} %copy-done.5, bf16[128,1280]{1,0:T(8,128)(2,1)} %copy-done.11, bf16[128,1280]{1,0:T(8,128)(2,1)} %copy-done.10, ...), custom_call_target="tpu_custom_call" | custom-call | tf_op jit(solution)/shard_map/pallas_call | solution.py:233
  32.8 2.9 %collective-permute-start.3 = (bf16[640,512]{1,0:T(8,128)(2,1)}, bf16[640,512]{1,0:T(8,128)(2,1)S(1)}, u32[]{:S(2)}, u32[]{:S(2)}) collective-permute-start(bf16[640,512]{1,0:T(8,128)(2,1)} %shard_map.148.rows_ref), channel_id=1, source_target_pairs={{0,4},{4,0},{8,12},{12,8},{16,20},{20,16},{24,28},{28,24},{1,5},{5... | collective-permute-start | bytes 1966088 | tf_op jit(solution)/shard_map/ppermute | solution.py:427
  35.7 1.1 copy-done
  36.8 1.8 %shard_map.149.refs_0_ = bf16[16,128,512]{2,1,0:T(8,128)(2,1)} custom-call(s32[2,4,128]{2,1,0:T(4,128)S(1)} %get-tuple-element.56.ids_ref, bf16[640,512]{1,0:T(8,128)(2,1)S(1)} %copy-done), custom_call_target="tpu_custom_call" | custom-call | tf_op jit(solution)/shard_map/pallas_call | solution.py:287
  38.6 5.8 %shard_map.147.rows_ref = bf16[640,512]{1,0:T(8,128)(2,1)} custom-call(s32[2]{0:T(128)} %pad_add_fusion.place_ref, bf16[1024,1280]{1,0:T(8,128)(2,1)} %shard_map.146.dec_ref, bf16[128,1280]{1,0:T(8,128)(2,1)} %copy-done.4, bf16[128,1280]{1,0:T(8,128)(2,1)} %copy-done.5, bf16[128,1280]{1,0:T(8,128)(2,1)} %copy-done.11, bf16[128,1280]{1,0:T(8,128)(2,1)} %copy-done.10, ...), custom_call_target="tpu_custom_call" | custom-call | tf_op jit(solution)/shard_map/pallas_call | solution.py:233
  44.4 1.1 copy-done.2
  45.5 1.8 %shard_map.150 = bf16[16,128,512]{2,1,0:T(8,128)(2,1)} custom-call(s32[2,4,128]{2,1,0:T(4,128)S(1)} %get-tuple-element.54.ids_ref, bf16[640,512]{1,0:T(8,128)(2,1)S(1)} %copy-done.2, bf16[16,128,512]{2,1,0:T(8,128)(2,1)} %shard_map.149.refs_0_), custom_call_target="tpu_custom_call", output_to_operand_aliasing={{}: (2, {})} | custom-call | tf_op jit(solution)/shard_map/pallas_call | solution.py:287
  47.4 4.9 %all-to-all-start.1 = ((bf16[16,128,512]{2,1,0:T(8,128)(2,1)}), bf16[16,128,512]{2,1,0:T(8,128)(2,1)}, u32[]{:S(2)}, u32[]{:S(2)}) async-start(bf16[16,128,512]{2,1,0:T(8,128)(2,1)} %shard_map.150), calls=%async_computation.1 | async-start | bytes 4194304 | tf_op jit(solution)/shard_map/all_to_all | solution.py:430
  52.3 1.2 dynamic-slice_select_fusion
  53.5 2.8 %collective-permute-start.6 = (bf16[320,512]{1,0:T(8,128)(2,1)S(1)}, bf16[320,512]{1,0:T(8,128)(2,1)S(1)}, u32[]{:S(2)}, u32[]{:S(2)}) collective-permute-start(bf16[320,512]{1,0:T(8,128)(2,1)S(1)} %get-tuple-element.49), channel_id=1, source_target_pairs={{0,24},{8,0},{16,8},{24,16},{1,25},{9,1},{17,9},{25,17},{2,26},{10... | collective-permute-start | bytes 983048 | tf_op jit(solution)/shard_map/ppermute | solution.py:423
  57.9 6.9 %collective-permute-done.3.rows_ref = bf16[640,512]{1,0:T(8,128)(2,1)S(1)} collective-permute-done((bf16[640,512]{1,0:T(8,128)(2,1)}, bf16[640,512]{1,0:T(8,128)(2,1)S(1)}, u32[]{:S(2)}, u32[]{:S(2)}) %collective-permute-start.3) | collective-permute-done | bytes 655392 | tf_op jit(solution)/shard_map/ppermute | solution.py:427
  64.8 1.8 %shard_map.151.refs_0_ = bf16[16,128,512]{2,1,0:T(8,128)(2,1)} custom-call(s32[2,4,128]{2,1,0:T(4,128)S(1)} %get-tuple-element.53.ids_ref, bf16[640,512]{1,0:T(8,128)(2,1)S(1)} %collective-permute-done.3.rows_ref), custom_call_target="tpu_custom_call" | custom-call | flops 69000003584 | bytes 230000000 | tf_op jit(solution)/shard_map/pallas_call | solution.py:287
  66.6 26.1 %collective-permute-done.2.rows_ref = bf16[640,512]{1,0:T(8,128)(2,1)S(1)} collective-permute-done((bf16[640,512]{1,0:T(8,128)(2,1)S(1)}, bf16[640,512]{1,0:T(8,128)(2,1)S(1)}, u32[]{:S(2)}, u32[]{:S(2)}) %collective-permute-start.2) | collective-permute-done | bytes 655392 | tf_op jit(solution)/shard_map/ppermute | solution.py:427
  92.7 1.8 %shard_map.152 = bf16[16,128,512]{2,1,0:T(8,128)(2,1)} custom-call(s32[2,4,128]{2,1,0:T(4,128)S(1)} %get-tuple-element.55.ids_ref, bf16[640,512]{1,0:T(8,128)(2,1)S(1)} %collective-permute-done.2.rows_ref, bf16[16,128,512]{2,1,0:T(8,128)(2,1)} %shard_map.151.refs_0_), custom_call_target="tpu_custom_call", output_to_operand_aliasing={{}: (2, {})} | custom-call | flops 69000003584 | bytes 230000000 | tf_op jit(solution)/shard_map/pallas_call | solution.py:287
  94.5 7.8 %all-to-all-done.1 = bf16[16,128,512]{2,1,0:T(8,128)(2,1)} async-done(((bf16[16,128,512]{2,1,0:T(8,128)(2,1)}), bf16[16,128,512]{2,1,0:T(8,128)(2,1)}, u32[]{:S(2)}, u32[]{:S(2)}) %all-to-all-start.1) | async-done | bytes 2097184 | tf_op jit(solution)/shard_map/all_to_all | solution.py:430
  102.3 3.9 %all-to-all-start.2 = ((bf16[16,128,512]{2,1,0:T(8,128)(2,1)}), bf16[16,128,512]{2,1,0:T(8,128)(2,1)S(1)}, u32[]{:S(2)}, u32[]{:S(2)}) async-start(bf16[16,128,512]{2,1,0:T(8,128)(2,1)} %shard_map.152), calls=%async_computation.2 | async-start | bytes 4194304 | tf_op jit(solution)/shard_map/all_to_all | solution.py:430
  106.9 0.6 and_select_fusion.segment_ref
  107.5 0.7 fusion.4.ids_ref
  108.2 7.9 %shard_map.153 = (bf16[4,2048,256]{2,1,0:T(8,128)(2,1)}, bf16[4,2048,256]{2,1,0:T(8,128)(2,1)}) custom-call(s32[4,4,128]{2,1,0:T(4,128)} %bitcast.22, bf16[320,512]{1,0:T(8,128)(2,1)} %get-tuple-element.40.refs_0_, bf16[320,512]{1,0:T(8,128)(2,1)} %copy-done.14, bf16[320,512]{1,0:T(8,128)(2,1)} %copy-done.13, bf16[320,512]{1,0:T(8,128)(2,1)} %copy-done.12), custom_call_target="tpu_custom_call" | custom-call | tf_op jit(solution)/shard_map/pallas_call | solution.py:327
  116.1 9.4 %shard_map.154 = (bf16[2048,256]{1,0:T(8,128)(2,1)}, bf16[2048,256]{1,0:T(8,128)(2,1)}) custom-call(s32[4]{0:T(128)} %and_select_fusion.segment_ref, s32[4,4,128]{2,1,0:T(4,128)} %fusion.4.ids_ref, bf16[4,512,512]{2,1,0:T(8,128)(2,1)} %bitcast.11.own_ref, bf16[4,2048,256]{2,1,0:T(8,128)(2,1)} %get-tuple-element.44.low_ref, ...), custom_call_target="tpu_custom_call" | custom-call | tf_op jit(solution)/shard_map/pallas_call | solution.py:361
  125.5 8.4 %all-to-all-done.2 = bf16[16,128,512]{2,1,0:T(8,128)(2,1)S(1)} async-done(((bf16[16,128,512]{2,1,0:T(8,128)(2,1)}), bf16[16,128,512]{2,1,0:T(8,128)(2,1)S(1)}, u32[]{:S(2)}, u32[]{:S(2)}) %all-to-all-start.2) | async-done | bytes 2097184 | tf_op jit(solution)/shard_map/all_to_all | solution.py:430
  133.9 1.4 copy-done.9
  135.3 12.4 %shard_map.155 = f32[2048,256]{1,0:T(8,128)} custom-call(s32[4]{0:T(128)} %and_select_fusion.segment_ref, s32[1]{0:T(128)S(6)} %copy.27.count_ref, s32[4,4,128]{2,1,0:T(4,128)} %fusion.4.ids_ref, bf16[4,512,512]{2,1,0:T(8,128)(2,1)} %bitcast.19, bf16[4,2048,256]{2,1,0:T(8,128)(2,1)} %get-tuple-element.44.low_ref, ...), custom_call_target="tpu_custom_call" | custom-call | tf_op jit(solution)/shard_map/pallas_call | solution.py:401
  (43 shorter events, 2.6 us)
Async XLA Ops:
  0.0 0.7 copy-start.7
  0.7 9.9 %copy-start.15 = (s32[1,4,8,32]{3,2,1,0:T(8,128)S(1)}, s32[1,4,8,32]{3,2,1,0:T(8,128)}, u32[]{:S(2)}) copy-start(s32[1,4,8,32]{3,2,1,0:T(8,128)} %param.17) | copy-start | bytes 12292
  0.7 17.5 %copy-start.8 = (f32[40]{0:T(128)S(1)}, f32[40]{0:T(128)}, u32[]{:S(2)}) copy-start(f32[40]{0:T(128)} %taps_ref.3) | copy-start | bytes 484
  3.2 0.6 copy-start.6
  3.8 22.2 %copy-start.4 = (bf16[128,1280]{1,0:T(8,128)(2,1)}, bf16[128,1280]{1,0:T(8,128)(2,1)S(1)}, u32[]{:S(2)}) copy-start(bf16[128,1280]{1,0:T(8,128)(2,1)S(1)} %get-tuple-element.32.first_ref) | copy-start | bytes 983044
  3.8 22.2 %copy-start.5 = (bf16[128,1280]{1,0:T(8,128)(2,1)}, bf16[128,1280]{1,0:T(8,128)(2,1)S(1)}, u32[]{:S(2)}) copy-start(bf16[128,1280]{1,0:T(8,128)(2,1)S(1)} %get-tuple-element.33.last_ref) | copy-start | bytes 983044
  3.8 22.2 %collective-permute-start.1 = (bf16[128,1280]{1,0:T(8,128)(2,1)S(1)}, bf16[128,1280]{1,0:T(8,128)(2,1)S(1)}, u32[]{:S(2)}, u32[]{:S(2)}) collective-permute-start(bf16[128,1280]{1,0:T(8,128)(2,1)S(1)} %get-tuple-element.32.first_ref), channel_id=1, source_target_pairs={{8,0},{16,8},{24,16},{9,1},{17,9},{25,17},{10,2},{18,10},{26,18},{... | collective-permute-start | bytes 983048 | tf_op jit(solution)/shard_map/ppermute | solution.py:439
  5.1 21.0 %collective-permute-start = (bf16[128,1280]{1,0:T(8,128)(2,1)S(1)}, bf16[128,1280]{1,0:T(8,128)(2,1)S(1)}, u32[]{:S(2)}, u32[]{:S(2)}) collective-permute-start(bf16[128,1280]{1,0:T(8,128)(2,1)S(1)} %get-tuple-element.33.last_ref), channel_id=1, source_target_pairs={{0,8},{8,16},{16,24},{1,9},{9,17},{17,25},{2,10},{10,18},{18,26},{... | collective-permute-start | bytes 983048 | tf_op jit(solution)/shard_map/ppermute | solution.py:438
  11.3 14.7 %all-to-all-start = ((s32[8,4,128]{2,1,0:T(4,128)}), s32[8,4,128]{2,1,0:T(4,128)S(1)}, u32[]{:S(2)}, u32[]{:S(2)}) async-start(s32[8,4,128]{2,1,0:T(4,128)} %bitcast.2), calls=%async_computation | async-start | bytes 32768 | tf_op jit(solution)/shard_map/all_to_all | solution.py:441
  26.0 0.7 copy-start.10
  26.1 0.9 copy-start.11
  32.8 32.1 %collective-permute-start.3 = (bf16[640,512]{1,0:T(8,128)(2,1)}, bf16[640,512]{1,0:T(8,128)(2,1)S(1)}, u32[]{:S(2)}, u32[]{:S(2)}) collective-permute-start(bf16[640,512]{1,0:T(8,128)(2,1)} %shard_map.148.rows_ref), channel_id=1, source_target_pairs={{0,4},{4,0},{8,12},{12,8},{16,20},{20,16},{24,28},{28,24},{1,5},{5... | collective-permute-start | bytes 1966088 | tf_op jit(solution)/shard_map/ppermute | solution.py:427
  35.7 1.1 copy-start
  44.4 1.1 copy-start.2
  47.3 5.0 %copy-start.1 = (bf16[640,512]{1,0:T(8,128)(2,1)S(1)}, bf16[640,512]{1,0:T(8,128)(2,1)}, u32[]{:S(2)}) copy-start(bf16[640,512]{1,0:T(8,128)(2,1)} %shard_map.148.rows_ref) | copy-start | bytes 1966084
  47.3 5.0 %copy-start.3 = (bf16[640,512]{1,0:T(8,128)(2,1)S(1)}, bf16[640,512]{1,0:T(8,128)(2,1)}, u32[]{:S(2)}) copy-start(bf16[640,512]{1,0:T(8,128)(2,1)} %shard_map.147.rows_ref) | copy-start | bytes 1966084
  47.4 55.0 %all-to-all-start.1 = ((bf16[16,128,512]{2,1,0:T(8,128)(2,1)}), bf16[16,128,512]{2,1,0:T(8,128)(2,1)}, u32[]{:S(2)}, u32[]{:S(2)}) async-start(bf16[16,128,512]{2,1,0:T(8,128)(2,1)} %shard_map.150), calls=%async_computation.1 | async-start | bytes 4194304 | tf_op jit(solution)/shard_map/all_to_all | solution.py:430
  53.5 41.0 %collective-permute-start.6 = (bf16[320,512]{1,0:T(8,128)(2,1)S(1)}, bf16[320,512]{1,0:T(8,128)(2,1)S(1)}, u32[]{:S(2)}, u32[]{:S(2)}) collective-permute-start(bf16[320,512]{1,0:T(8,128)(2,1)S(1)} %get-tuple-element.49), channel_id=1, source_target_pairs={{0,24},{8,0},{16,8},{24,16},{1,25},{9,1},{17,9},{25,17},{2,26},{10... | collective-permute-start | bytes 983048 | tf_op jit(solution)/shard_map/ppermute | solution.py:423
  56.3 38.2 %collective-permute-start.5 = (bf16[320,512]{1,0:T(8,128)(2,1)S(1)}, bf16[320,512]{1,0:T(8,128)(2,1)S(1)}, u32[]{:S(2)}, u32[]{:S(2)}) collective-permute-start(bf16[320,512]{1,0:T(8,128)(2,1)S(1)} %get-tuple-element.50), channel_id=1, source_target_pairs={{0,16},{8,24},{16,0},{24,8},{1,17},{9,25},{17,1},{25,9},{2,18},{10... | collective-permute-start | bytes 983048 | tf_op jit(solution)/shard_map/ppermute | solution.py:423
  56.8 37.7 %collective-permute-start.4 = (bf16[320,512]{1,0:T(8,128)(2,1)S(1)}, bf16[320,512]{1,0:T(8,128)(2,1)S(1)}, u32[]{:S(2)}, u32[]{:S(2)}) collective-permute-start(bf16[320,512]{1,0:T(8,128)(2,1)S(1)} %get-tuple-element.51), channel_id=1, source_target_pairs={{0,8},{8,16},{16,24},{24,0},{1,9},{9,17},{17,25},{25,1},{2,10},{10... | collective-permute-start | bytes 983048 | tf_op jit(solution)/shard_map/ppermute | solution.py:423
  57.4 35.3 %collective-permute-start.2 = (bf16[640,512]{1,0:T(8,128)(2,1)S(1)}, bf16[640,512]{1,0:T(8,128)(2,1)S(1)}, u32[]{:S(2)}, u32[]{:S(2)}) collective-permute-start(bf16[640,512]{1,0:T(8,128)(2,1)S(1)} %copy-done.3), channel_id=1, source_target_pairs={{0,4},{4,0},{8,12},{12,8},{16,20},{20,16},{24,28},{28,24},{1,5},{5... | collective-permute-start | bytes 1966088 | tf_op jit(solution)/shard_map/ppermute | solution.py:427
  94.5 7.9 %copy-start.12 = (bf16[320,512]{1,0:T(8,128)(2,1)}, bf16[320,512]{1,0:T(8,128)(2,1)S(1)}, u32[]{:S(2)}) copy-start(bf16[320,512]{1,0:T(8,128)(2,1)S(1)} %collective-permute-done.6.refs_3_) | copy-start | bytes 983044
  94.5 7.8 %copy-start.13 = (bf16[320,512]{1,0:T(8,128)(2,1)}, bf16[320,512]{1,0:T(8,128)(2,1)S(1)}, u32[]{:S(2)}) copy-start(bf16[320,512]{1,0:T(8,128)(2,1)S(1)} %collective-permute-done.5.refs_2_) | copy-start | bytes 983044
  94.5 7.8 %copy-start.14 = (bf16[320,512]{1,0:T(8,128)(2,1)}, bf16[320,512]{1,0:T(8,128)(2,1)S(1)}, u32[]{:S(2)}) copy-start(bf16[320,512]{1,0:T(8,128)(2,1)S(1)} %collective-permute-done.4.refs_1_) | copy-start | bytes 983044
  102.3 5.2 %copy-start.16 = (s32[1,2048]{1,0:T(1,128)S(1)}, s32[1,2048]{1,0:T(1,128)}, u32[]{:S(2)}) copy-start(s32[1,2048]{1,0:T(1,128)} %param.18) | copy-start | bytes 24580
  102.3 31.6 %all-to-all-start.2 = ((bf16[16,128,512]{2,1,0:T(8,128)(2,1)}), bf16[16,128,512]{2,1,0:T(8,128)(2,1)S(1)}, u32[]{:S(2)}, u32[]{:S(2)}) async-start(bf16[16,128,512]{2,1,0:T(8,128)(2,1)} %shard_map.152), calls=%async_computation.2 | async-start | bytes 4194304 | tf_op jit(solution)/shard_map/all_to_all | solution.py:430
  133.9 1.4 copy-start.9
